TPU v7x, 32 devices: a whole 2x2x4 slice. The times are simulated.
32 devices in a mesh: gx: 8 (over y, x, core), gy: 4 (over z).
Axes of the slice: x: 2, y: 2, z: 4, core: 2. Of those that a mesh axis runs over, the one named last changes fastest.
Arguments:
- load: float32 [8, 4, 96, 896], P('gx', 'gy'), may hold values from -80 to 80
- dual_operator: bfloat16 [8, 4, 896, 896], P('gx', 'gy'), may hold values from -1 to 2
- dirichlet: bfloat16 [8, 4, 896, 896], P('gx', 'gy'), may hold values from -1 to 2
- modes: bfloat16 [8, 4, 12, 896], P('gx', 'gy'), may hold values from -1 to 1
- coarse_inverse: float32 [8, 48, 4, 96], P('gx', None, 'gy'), may hold values from -1 to 2, as said below
- face_counts: int32 [8, 4, 4], P('gx', 'gy'), may hold values from 0 to 224, as said below
- partners: int32 [8, 4, 4, 224], P('gx', 'gy'), may hold values from 0 to 223, as said below
Outputs:
- multipliers: float32 [8, 4, 96, 896], P('gx', 'gy')
- residual: float32 [8, 4, 96, 896], P('gx', 'gy')
Inputs may be any that keep to these rules, and one draw needn't show every extreme that they name: `face_counts`: the two faces of one interface have equal counts; faces on the grid's outer boundary have 0; every other face has at least half of 224; some face has exactly 224. `partners`: each face's list is a permutation of the slots that maps the live slots onto the live slots of the neighbour's facing face; the facing face's list is its inverse. `coarse_inverse`: the coarse inverse is symmetric: the entry of coefficients u, v equals that of v, u.
All inputs are finite; a program needn't handle non-finite values.
Results may differ from a plain program's by a relative error of at most 0.00365.
The roundings to bfloat16 on the way count: a program that leaves them out, or rounds other values in their place, can miss the bound.
Values may be sent and summed in bfloat16 or wider, within the bound.
No kernel may reach another device: no remote copies, remote signals or barrier semaphores. Data moves between devices by JAX's collectives and lax.ppermute only.
A program may use at most 64 MiB of HBM per device.

v0:
```python
import jax
import jax.numpy as jnp
from jax import lax
from jax.sharding import PartitionSpec as P

precise = lax.Precision.HIGHEST
spectrum_low = 0.5
spectrum_high = 4.0


def extended(shard, sides, width):
    for axis, dim in sides:
        size, length = (lax.axis_size(axis), shard.shape[dim])
        up = [(i, (i + 1) % size) for i in range(size - 1)]
        down = [(j, i) for i, j in up]
        last = lax.slice_in_dim(shard, length - width, length, axis=dim)
        first = lax.slice_in_dim(shard, 0, width, axis=dim)
        before = lax.ppermute(last, axis, up)
        after = lax.ppermute(first, axis, down)
        shard = jnp.concatenate([before, shard, after], axis=dim)
    return shard


def chebyshev_coefficients():
    center = (spectrum_high + spectrum_low) / 2.0
    radius = (spectrum_high - spectrum_low) / 2.0
    center_ratio = center / radius
    factor_prev = 1.0 / center_ratio
    result = [(1.0 / center, 0.0)]
    factor = 1.0 / (2.0 * center_ratio - factor_prev)
    result.append((2.0 * factor / radius, factor * factor_prev))
    return result


def assemble_west_east(values, partner_slots):
    face_width = partner_slots.shape[1]
    shaped = values.reshape(values.shape[0], 2, face_width)
    padded = extended(shaped, (("gx", 1),), 1)
    west_sum = values[:, :face_width] + jnp.take(padded[:, 0], partner_slots[0], axis=1)
    east_sum = values[:, face_width:] + jnp.take(padded[:, 3], partner_slots[1], axis=1)
    return (west_sum, east_sum)


def assemble_south_north(values, partner_slots):
    face_width = partner_slots.shape[1]
    shaped = values.reshape(values.shape[0], 2, face_width)
    padded = extended(shaped, (("gy", 1),), 1)
    south_sum = values[:, :face_width] + jnp.take(padded[:, 0], partner_slots[2], axis=1)
    north_sum = values[:, face_width:] + jnp.take(padded[:, 3], partner_slots[3], axis=1)
    return (south_sum, north_sum)


def assemble(values, partner_slots, live_slots):
    split_at = values.shape[1] // 2
    west_sum, east_sum = assemble_west_east(values[:, :split_at], partner_slots)
    south_sum, north_sum = assemble_south_north(values[:, split_at:], partner_slots)
    return jnp.concatenate([west_sum, east_sum, south_sum, north_sum], axis=1) * live_slots


def apply_block(vector, matrix, partner_slots, live_slots):
    rounded = vector.astype(jnp.bfloat16)
    split_at = matrix.shape[1] // 2
    product = jnp.dot(rounded, matrix, preferred_element_type=jnp.float32)
    west_sum, east_sum = assemble_west_east(product[:, :split_at], partner_slots)
    south_sum, north_sum = assemble_south_north(product[:, split_at:], partner_slots)
    return jnp.concatenate([west_sum, east_sum, south_sum, north_sum], axis=1) * live_slots


def mode_faces(mode_half, partner_slots):
    face_width = partner_slots.shape[1]
    count_modes = mode_half.shape[0]
    split_at = 2 * face_width
    padded_x = extended(
        mode_half[:, :split_at].reshape(count_modes, 2, face_width), (("gx", 1),), 1
    )
    padded_y = extended(
        mode_half[:, split_at:].reshape(count_modes, 2, face_width), (("gy", 1),), 1
    )
    received = [padded_x[:, 0], padded_x[:, 3], padded_y[:, 0], padded_y[:, 3]]
    result = []
    for face_index in range(4):
        result.append(
            jnp.take(received[face_index], partner_slots[face_index], axis=1).astype(jnp.float32)
        )
    return result


def coarse_values(coeffs, inverse_block):
    partial_terms = lax.dot_general(
        lax.all_gather(coeffs, "gx", axis=1, tiled=True),
        inverse_block,
        (((1,), (1,)), ((), ())),
        precision=precise,
        preferred_element_type=jnp.float32,
    )
    return lax.psum_scatter(partial_terms, "gy", scatter_dimension=1, tiled=True)


def project(vector, mode_rows, inverse_block, partner_slots, live_slots, neighbour_modes):
    coeffs = jnp.dot(vector, mode_rows.T, precision=precise, preferred_element_type=jnp.float32)
    solved = coarse_values(coeffs, inverse_block)
    own_part = jnp.dot(solved, mode_rows, precision=precise, preferred_element_type=jnp.float32)
    padded = extended(solved[None, None], (("gx", 0), ("gy", 1)), 1)
    sources = [padded[0, 1], padded[2, 1], padded[1, 0], padded[1, 2]]
    face_width = partner_slots.shape[1]
    pieces = []
    for face_index in range(4):
        local_face = own_part[:, face_index * face_width : (face_index + 1) * face_width]
        remote_face = jnp.dot(
            sources[face_index],
            neighbour_modes[face_index],
            precision=precise,
            preferred_element_type=jnp.float32,
        )
        pieces.append(local_face + remote_face)
    correction = jnp.concatenate(pieces, axis=1) * live_slots
    return vector - correction


def local(load, dual_operator, dirichlet, modes, coarse_inverse, face_counts, partners):
    partner_slots = partners[0, 0]
    face_width = partner_slots.shape[1]
    positions = lax.broadcasted_iota(jnp.int32, (4, face_width), 1)
    live_slots = (
        (positions < face_counts[0, 0][:, None]).astype(jnp.float32).reshape(1, 4 * face_width)
    )
    mode_half = modes[0, 0]
    mode_rows = mode_half.astype(jnp.float32)
    inverse_block = coarse_inverse[0, :, 0, :]
    dual_local = dual_operator[0, 0]
    dirichlet_local = dirichlet[0, 0]
    chebyshev = chebyshev_coefficients()
    neighbour_modes = mode_faces(mode_half, partner_slots)
    gap_values = assemble(load[0, 0], partner_slots, live_slots)
    residual = project(
        gap_values, mode_rows, inverse_block, partner_slots, live_slots, neighbour_modes
    )
    multipliers = jnp.zeros_like(residual)
    direction = jnp.zeros_like(residual)
    for alpha_step, beta_step in chebyshev:
        smoothed = apply_block(residual, dirichlet_local, partner_slots, live_slots)
        preconditioned = project(
            smoothed, mode_rows, inverse_block, partner_slots, live_slots, neighbour_modes
        )
        direction = alpha_step * preconditioned + beta_step * direction
        multipliers = multipliers + direction
        applied = apply_block(direction, dual_local, partner_slots, live_slots)
        residual = residual - project(
            applied, mode_rows, inverse_block, partner_slots, live_slots, neighbour_modes
        )
    return (multipliers[None, None], residual[None, None])


def solution(mesh):
    return jax.shard_map(
        local,
        mesh=mesh,
        in_specs=(
            P("gx", "gy", None, None),
            P("gx", "gy", None, None),
            P("gx", "gy", None, None),
            P("gx", "gy", None, None),
            P("gx", None, "gy", None),
            P("gx", "gy", None),
            P("gx", "gy", None, None),
        ),
        out_specs=(P("gx", "gy", None, None), P("gx", "gy", None, None)),
        check_vma=False,
    )
```

profile of v0, /device:TPU:0, one launch (start us, length us, event | category | flops | bytes accessed | tf_op | source)
XLA Modules:
  0.0 333.8 jit_solution(15866892305757446724)
XLA Ops:
  5.4 4.5 %collective-permute-start = (f32[96,1,224]{0,2,1:T(8,128)S(1)}, f32[96,1,224]{0,2,1:T(8,128)S(1)}, u32[]{:S(2)}, u32[]{:S(2)}) collective-permute-start(f32[96,1,224]{0,2,1:T(8,128)S(1)} %get-tuple-element.50), channel_id=1, source_target_pairs={{0,4},{4,8},{8,12},{12,16},{16,20},{20,24},{24,28},{1,5},{5,9},{9,... | collective-permute-start | bytes 258056 | tf_op jit(solution)/shard_map/ppermute | solution.py:18
  11.4 3.5 %collective-permute-start.2 = (f32[96,1,224]{0,2,1:T(8,128)S(1)}, f32[96,1,224]{0,2,1:T(8,128)S(1)}, u32[]{:S(2)}, u32[]{:S(2)}) collective-permute-start(f32[96,1,224]{0,2,1:T(8,128)S(1)} %get-tuple-element.52), channel_id=1, source_target_pairs={{0,1},{1,2},{2,3},{4,5},{5,6},{6,7},{8,9},{9,10},{10,11},{12,13},{... | collective-permute-start | bytes 258056 | tf_op jit(solution)/shard_map/ppermute | solution.py:18
  18.9 4.5 %collective-permute-start.9 = (bf16[12,1,224]{0,2,1:T(8,128)(2,1)S(1)}, bf16[12,1,224]{0,2,1:T(8,128)(2,1)S(1)}, u32[]{:S(2)}, u32[]{:S(2)}) collective-permute-start(bf16[12,1,224]{0,2,1:T(8,128)(2,1)S(1)} %get-tuple-element.56), channel_id=1, source_target_pairs={{0,1},{1,2},{2,3},{4,5},{5,6},{6,7},{8,9},{9,10},{10,11},{12,13},{... | collective-permute-start | bytes 16136 | tf_op jit(solution)/shard_map/ppermute | solution.py:18
  27.8 11.6 %all-gather = f32[8,12,96]{2,1,0:T(8,128)S(1)} all-gather(f32[1,12,96]{2,1,0:T(8,128)S(1)} %convolution_bitcast_fusion.4), channel_id=1, replica_groups=mesh['gx'=8,'gy'=4] {'gx'}, dimensions={0}, use_global_device_ids=true | all-gather | bytes 41472 | tf_op jit(solution)/shard_map/all_gather | solution.py:90
  39.5 13.7 %fusion = f32[96,16]{0,1:T(8,128)S(1)} fusion(f32[96,48]{0,1:T(8,128)S(1)} %fusion.195), kind=kCustom, calls=%all-reduce-scatter | all-reduce-scatter fusion | flops 6145 | bytes 25088
  53.2 2.9 collective-permute-start.44
  62.2 3.0 collective-permute-start.4
  67.3 4.5 %collective-permute-start.8 = (f32[3,1,96,12]{2,3,1,0:T(8,128)S(1)}, f32[3,1,96,12]{2,3,1,0:T(8,128)S(1)}, u32[]{:S(2)}, u32[]{:S(2)}) collective-permute-start(f32[3,1,96,12]{2,3,1,0:T(8,128)S(1)} %pad_maximum_fusion), channel_id=1, source_target_pairs={{0,1},{1,2},{2,3},{4,5},{5,6},{6,7},{8,9},{9,10},{10,11},{12,13},{... | collective-permute-start | bytes 41480 | tf_op jit(solution)/shard_map/ppermute | solution.py:18
  80.3 4.2 %collective-permute-start.14 = (f32[96,1,224]{0,2,1:T(8,128)}, f32[96,1,224]{0,2,1:T(8,128)S(1)}, u32[]{:S(2)}, u32[]{:S(2)}) collective-permute-start(f32[96,1,224]{0,2,1:T(8,128)} %get-tuple-element.48), channel_id=1, source_target_pairs={{0,1},{1,2},{2,3},{4,5},{5,6},{6,7},{8,9},{9,10},{10,11},{12,13},{... | collective-permute-start | bytes 258056 | tf_op jit(solution)/shard_map/ppermute | solution.py:18
  88.5 2.9 collective-permute-done.15
  93.4 15.0 %all-gather.1 = f32[8,12,96]{2,1,0:T(8,128)S(1)} all-gather(f32[1,12,96]{2,1,0:T(8,128)S(1)} %convolution_bitcast_fusion.3), channel_id=1, replica_groups=mesh['gx'=8,'gy'=4] {'gx'}, dimensions={0}, use_global_device_ids=true | all-gather | bytes 41472 | tf_op jit(solution)/shard_map/all_gather | solution.py:90
  108.5 11.5 %fusion.1 = f32[96,16]{0,1:T(8,128)S(1)} fusion(f32[96,48]{0,1:T(8,128)S(1)} %fusion.196), kind=kCustom, calls=%all-reduce-scatter.1 | all-reduce-scatter fusion | flops 6145 | bytes 25088
  124.1 3.0 collective-permute-start.16
  129.2 4.8 %collective-permute-start.18 = (f32[3,1,96,12]{2,3,1,0:T(8,128)S(1)}, f32[3,1,96,12]{2,3,1,0:T(8,128)S(1)}, u32[]{:S(2)}, u32[]{:S(2)}) collective-permute-start(f32[3,1,96,12]{2,3,1,0:T(8,128)S(1)} %pad_maximum_fusion.1), channel_id=1, source_target_pairs={{0,1},{1,2},{2,3},{4,5},{5,6},{6,7},{8,9},{9,10},{10,11},{12,13},{... | collective-permute-start | bytes 41480 | tf_op jit(solution)/shard_map/ppermute | solution.py:18
  144.2 3.9 %collective-permute-start.22 = (f32[96,1,224]{0,2,1:T(8,128)}, f32[96,1,224]{0,2,1:T(8,128)S(1)}, u32[]{:S(2)}, u32[]{:S(2)}) collective-permute-start(f32[96,1,224]{0,2,1:T(8,128)} %get-tuple-element.44), channel_id=1, source_target_pairs={{0,1},{1,2},{2,3},{4,5},{5,6},{6,7},{8,9},{9,10},{10,11},{12,13},{... | collective-permute-start | bytes 258056 | tf_op jit(solution)/shard_map/ppermute | solution.py:18
  157.1 14.4 %all-gather.2 = f32[8,12,96]{2,1,0:T(8,128)S(1)} all-gather(f32[1,12,96]{2,1,0:T(8,128)S(1)} %convolution_bitcast_fusion.2), channel_id=1, replica_groups=mesh['gx'=8,'gy'=4] {'gx'}, dimensions={0}, use_global_device_ids=true | all-gather | bytes 41472 | tf_op jit(solution)/shard_map/all_gather | solution.py:90
  171.7 12.4 %fusion.2 = f32[96,16]{0,1:T(8,128)S(1)} fusion(f32[96,48]{0,1:T(8,128)S(1)} %fusion.197), kind=kCustom, calls=%all-reduce-scatter.2 | all-reduce-scatter fusion | flops 6145 | bytes 25088
  188.9 3.0 collective-permute-start.24
  194.0 4.8 %collective-permute-start.26 = (f32[3,1,96,12]{2,3,1,0:T(8,128)S(1)}, f32[3,1,96,12]{2,3,1,0:T(8,128)S(1)}, u32[]{:S(2)}, u32[]{:S(2)}) collective-permute-start(f32[3,1,96,12]{2,3,1,0:T(8,128)S(1)} %pad_maximum_fusion.2), channel_id=1, source_target_pairs={{0,1},{1,2},{2,3},{4,5},{5,6},{6,7},{8,9},{9,10},{10,11},{12,13},{... | collective-permute-start | bytes 41480 | tf_op jit(solution)/shard_map/ppermute | solution.py:18
  207.9 3.9 %collective-permute-start.30 = (f32[96,1,224]{0,2,1:T(8,128)}, f32[96,1,224]{0,2,1:T(8,128)S(1)}, u32[]{:S(2)}, u32[]{:S(2)}) collective-permute-start(f32[96,1,224]{0,2,1:T(8,128)} %get-tuple-element.40), channel_id=1, source_target_pairs={{0,1},{1,2},{2,3},{4,5},{5,6},{6,7},{8,9},{9,10},{10,11},{12,13},{... | collective-permute-start | bytes 258056 | tf_op jit(solution)/shard_map/ppermute | solution.py:18
  215.8 2.9 collective-permute-done.31
  220.7 14.5 %all-gather.3 = f32[8,12,96]{2,1,0:T(8,128)S(1)} all-gather(f32[1,12,96]{2,1,0:T(8,128)S(1)} %convolution_bitcast_fusion.1), channel_id=1, replica_groups=mesh['gx'=8,'gy'=4] {'gx'}, dimensions={0}, use_global_device_ids=true | all-gather | bytes 41472 | tf_op jit(solution)/shard_map/all_gather | solution.py:90
  235.4 12.4 %fusion.3 = f32[96,16]{0,1:T(8,128)S(1)} fusion(f32[96,48]{0,1:T(8,128)S(1)} %fusion.198), kind=kCustom, calls=%all-reduce-scatter.3 | all-reduce-scatter fusion | flops 6145 | bytes 25088
  252.6 3.0 collective-permute-start.32
  257.8 4.8 %collective-permute-start.34 = (f32[3,1,96,12]{2,3,1,0:T(8,128)S(1)}, f32[3,1,96,12]{2,3,1,0:T(8,128)S(1)}, u32[]{:S(2)}, u32[]{:S(2)}) collective-permute-start(f32[3,1,96,12]{2,3,1,0:T(8,128)S(1)} %pad_maximum_fusion.3), channel_id=1, source_target_pairs={{0,1},{1,2},{2,3},{4,5},{5,6},{6,7},{8,9},{9,10},{10,11},{12,13},{... | collective-permute-start | bytes 41480 | tf_op jit(solution)/shard_map/ppermute | solution.py:18
  273.4 3.9 %collective-permute-start.38 = (f32[96,1,224]{0,2,1:T(8,128)}, f32[96,1,224]{0,2,1:T(8,128)S(1)}, u32[]{:S(2)}, u32[]{:S(2)}) collective-permute-start(f32[96,1,224]{0,2,1:T(8,128)} %get-tuple-element.36), channel_id=1, source_target_pairs={{0,1},{1,2},{2,3},{4,5},{5,6},{6,7},{8,9},{9,10},{10,11},{12,13},{... | collective-permute-start | bytes 258056 | tf_op jit(solution)/shard_map/ppermute | solution.py:18
  281.3 2.9 collective-permute-done.39
  286.2 14.3 %all-gather.4 = f32[8,12,96]{2,1,0:T(8,128)S(1)} all-gather(f32[1,12,96]{2,1,0:T(8,128)S(1)} %convolution_bitcast_fusion), channel_id=1, replica_groups=mesh['gx'=8,'gy'=4] {'gx'}, dimensions={0}, use_global_device_ids=true | all-gather | bytes 41472 | tf_op jit(solution)/shard_map/all_gather | solution.py:90
  300.7 12.4 %fusion.4 = f32[96,16]{0,1:T(8,128)S(1)} fusion(f32[96,48]{0,1:T(8,128)S(1)} %fusion.199), kind=kCustom, calls=%all-reduce-scatter.4 | all-reduce-scatter fusion | flops 6145 | bytes 25088
  315.5 2.8 fusion.22
  319.7 3.0 collective-permute-start.40
  324.8 4.5 %collective-permute-start.42 = (f32[3,1,96,12]{2,3,1,0:T(8,128)S(1)}, f32[3,1,96,12]{2,3,1,0:T(8,128)S(1)}, u32[]{:S(2)}, u32[]{:S(2)}) collective-permute-start(f32[3,1,96,12]{2,3,1,0:T(8,128)S(1)} %pad_maximum_fusion.4), channel_id=1, source_target_pairs={{0,1},{1,2},{2,3},{4,5},{5,6},{6,7},{8,9},{9,10},{10,11},{12,13},{... | collective-permute-start | bytes 41480 | tf_op jit(solution)/shard_map/ppermute | solution.py:18
  (363 shorter events, 116.6 us)
Async XLA Ops:
  1.8 55.6 %collective-permute-start.5 = (bf16[12,1,224]{0,2,1:T(8,128)(2,1)S(1)}, bf16[12,1,224]{0,2,1:T(8,128)(2,1)S(1)}, u32[]{:S(2)}, u32[]{:S(2)}) collective-permute-start(bf16[12,1,224]{0,2,1:T(8,128)(2,1)S(1)} %get-tuple-element.54), channel_id=1, source_target_pairs={{0,4},{4,8},{8,12},{12,16},{16,20},{20,24},{24,28},{1,5},{5,9},{9,... | collective-permute-start | bytes 16136 | tf_op jit(solution)/shard_map/ppermute | solution.py:18
  5.4 11.3 %collective-permute-start = (f32[96,1,224]{0,2,1:T(8,128)S(1)}, f32[96,1,224]{0,2,1:T(8,128)S(1)}, u32[]{:S(2)}, u32[]{:S(2)}) collective-permute-start(f32[96,1,224]{0,2,1:T(8,128)S(1)} %get-tuple-element.50), channel_id=1, source_target_pairs={{0,4},{4,8},{8,12},{12,16},{16,20},{20,24},{24,28},{1,5},{5,9},{9,... | collective-permute-start | bytes 258056 | tf_op jit(solution)/shard_map/ppermute | solution.py:18
  10.0 8.9 %collective-permute-start.1 = (f32[96,1,224]{0,2,1:T(8,128)S(1)}, f32[96,1,224]{0,2,1:T(8,128)S(1)}, u32[]{:S(2)}, u32[]{:S(2)}) collective-permute-start(f32[96,1,224]{0,2,1:T(8,128)S(1)} %get-tuple-element.51), channel_id=1, source_target_pairs={{4,0},{8,4},{12,8},{16,12},{20,16},{24,20},{28,24},{5,1},{9,5},{13... | collective-permute-start | bytes 258056 | tf_op jit(solution)/shard_map/ppermute | solution.py:19
  11.4 12.8 %collective-permute-start.2 = (f32[96,1,224]{0,2,1:T(8,128)S(1)}, f32[96,1,224]{0,2,1:T(8,128)S(1)}, u32[]{:S(2)}, u32[]{:S(2)}) collective-permute-start(f32[96,1,224]{0,2,1:T(8,128)S(1)} %get-tuple-element.52), channel_id=1, source_target_pairs={{0,1},{1,2},{2,3},{4,5},{5,6},{6,7},{8,9},{9,10},{10,11},{12,13},{... | collective-permute-start | bytes 258056 | tf_op jit(solution)/shard_map/ppermute | solution.py:18
  14.9 11.5 %collective-permute-start.3 = (f32[96,1,224]{0,2,1:T(8,128)S(1)}, f32[96,1,224]{0,2,1:T(8,128)S(1)}, u32[]{:S(2)}, u32[]{:S(2)}) collective-permute-start(f32[96,1,224]{0,2,1:T(8,128)S(1)} %get-tuple-element.53), channel_id=1, source_target_pairs={{1,0},{2,1},{3,2},{5,4},{6,5},{7,6},{9,8},{10,9},{11,10},{13,12},{... | collective-permute-start | bytes 258056 | tf_op jit(solution)/shard_map/ppermute | solution.py:19
  16.7 41.5 %collective-permute-start.7 = (bf16[12,1,224]{0,2,1:T(8,128)(2,1)S(1)}, bf16[12,1,224]{0,2,1:T(8,128)(2,1)S(1)}, u32[]{:S(2)}, u32[]{:S(2)}) collective-permute-start(bf16[12,1,224]{0,2,1:T(8,128)(2,1)S(1)} %get-tuple-element.55), channel_id=1, source_target_pairs={{4,0},{8,4},{12,8},{16,12},{20,16},{24,20},{28,24},{5,1},{9,5},{13... | collective-permute-start | bytes 16136 | tf_op jit(solution)/shard_map/ppermute | solution.py:19
  18.9 40.2 %collective-permute-start.9 = (bf16[12,1,224]{0,2,1:T(8,128)(2,1)S(1)}, bf16[12,1,224]{0,2,1:T(8,128)(2,1)S(1)}, u32[]{:S(2)}, u32[]{:S(2)}) collective-permute-start(bf16[12,1,224]{0,2,1:T(8,128)(2,1)S(1)} %get-tuple-element.56), channel_id=1, source_target_pairs={{0,1},{1,2},{2,3},{4,5},{5,6},{6,7},{8,9},{9,10},{10,11},{12,13},{... | collective-permute-start | bytes 16136 | tf_op jit(solution)/shard_map/ppermute | solution.py:18
  24.3 35.6 %collective-permute-start.11 = (bf16[12,1,224]{0,2,1:T(8,128)(2,1)S(1)}, bf16[12,1,224]{0,2,1:T(8,128)(2,1)S(1)}, u32[]{:S(2)}, u32[]{:S(2)}) collective-permute-start(bf16[12,1,224]{0,2,1:T(8,128)(2,1)S(1)} %get-tuple-element.57), channel_id=1, source_target_pairs={{1,0},{2,1},{3,2},{5,4},{6,5},{7,6},{9,8},{10,9},{11,10},{13,12},{... | collective-permute-start | bytes 16136 | tf_op jit(solution)/shard_map/ppermute | solution.py:19
  53.2 7.5 %collective-permute-start.44 = (f32[96,12]{0,1:T(8,128)S(1)}, f32[96,12]{0,1:T(8,128)S(1)}, u32[]{:S(2)}, u32[]{:S(2)}) collective-permute-start(f32[96,12]{0,1:T(8,128)S(1)} %slice.538), channel_id=1, source_target_pairs={{0,1},{1,2},{2,3},{4,5},{5,6},{6,7},{8,9},{9,10},{10,11},{12,13},{... | collective-permute-start | bytes 13832
  66.0 6.5 %collective-permute-start.10 = (f32[3,1,96,12]{2,3,1,0:T(8,128)S(1)}, f32[3,1,96,12]{2,3,1,0:T(8,128)S(1)}, u32[]{:S(2)}, u32[]{:S(2)}) collective-permute-start(f32[3,1,96,12]{2,3,1,0:T(8,128)S(1)} %pad_maximum_fusion), channel_id=1, source_target_pairs={{1,0},{2,1},{3,2},{5,4},{6,5},{7,6},{9,8},{10,9},{11,10},{13,12},{... | collective-permute-start | bytes 41480 | tf_op jit(solution)/shard_map/ppermute | solution.py:19
  75.9 9.9 %collective-permute-start.12 = (f32[96,1,224]{0,2,1:T(8,128)S(1)}, f32[96,1,224]{0,2,1:T(8,128)S(1)}, u32[]{:S(2)}, u32[]{:S(2)}) collective-permute-start(f32[96,1,224]{0,2,1:T(8,128)S(1)} %get-tuple-element.46), channel_id=1, source_target_pairs={{0,4},{4,8},{8,12},{12,16},{16,20},{20,24},{24,28},{1,5},{5,9},{9,... | collective-permute-start | bytes 258056 | tf_op jit(solution)/shard_map/ppermute | solution.py:18
  77.2 9.5 %collective-permute-start.13 = (f32[96,1,224]{0,2,1:T(8,128)}, f32[96,1,224]{0,2,1:T(8,128)S(1)}, u32[]{:S(2)}, u32[]{:S(2)}) collective-permute-start(f32[96,1,224]{0,2,1:T(8,128)} %get-tuple-element.47), channel_id=1, source_target_pairs={{4,0},{8,4},{12,8},{16,12},{20,16},{24,20},{28,24},{5,1},{9,5},{13... | collective-permute-start | bytes 258056 | tf_op jit(solution)/shard_map/ppermute | solution.py:19
  80.3 7.4 %collective-permute-start.14 = (f32[96,1,224]{0,2,1:T(8,128)}, f32[96,1,224]{0,2,1:T(8,128)S(1)}, u32[]{:S(2)}, u32[]{:S(2)}) collective-permute-start(f32[96,1,224]{0,2,1:T(8,128)} %get-tuple-element.48), channel_id=1, source_target_pairs={{0,1},{1,2},{2,3},{4,5},{5,6},{6,7},{8,9},{9,10},{10,11},{12,13},{... | collective-permute-start | bytes 258056 | tf_op jit(solution)/shard_map/ppermute | solution.py:18
  84.5 6.9 %collective-permute-start.15 = (f32[96,1,224]{0,2,1:T(8,128)}, f32[96,1,224]{0,2,1:T(8,128)S(1)}, u32[]{:S(2)}, u32[]{:S(2)}) collective-permute-start(f32[96,1,224]{0,2,1:T(8,128)} %get-tuple-element.49), channel_id=1, source_target_pairs={{1,0},{2,1},{3,2},{5,4},{6,5},{7,6},{9,8},{10,9},{11,10},{13,12},{... | collective-permute-start | bytes 258056 | tf_op jit(solution)/shard_map/ppermute | solution.py:19
  127.9 6.8 %collective-permute-start.19 = (f32[3,1,96,12]{2,3,1,0:T(8,128)S(1)}, f32[3,1,96,12]{2,3,1,0:T(8,128)S(1)}, u32[]{:S(2)}, u32[]{:S(2)}) collective-permute-start(f32[3,1,96,12]{2,3,1,0:T(8,128)S(1)} %pad_maximum_fusion.1), channel_id=1, source_target_pairs={{1,0},{2,1},{3,2},{5,4},{6,5},{7,6},{9,8},{10,9},{11,10},{13,12},{... | collective-permute-start | bytes 41480 | tf_op jit(solution)/shard_map/ppermute | solution.py:19
  129.2 6.3 %collective-permute-start.18 = (f32[3,1,96,12]{2,3,1,0:T(8,128)S(1)}, f32[3,1,96,12]{2,3,1,0:T(8,128)S(1)}, u32[]{:S(2)}, u32[]{:S(2)}) collective-permute-start(f32[3,1,96,12]{2,3,1,0:T(8,128)S(1)} %pad_maximum_fusion.1), channel_id=1, source_target_pairs={{0,1},{1,2},{2,3},{4,5},{5,6},{6,7},{8,9},{9,10},{10,11},{12,13},{... | collective-permute-start | bytes 41480 | tf_op jit(solution)/shard_map/ppermute | solution.py:18
  139.6 10.0 %collective-permute-start.20 = (f32[96,1,224]{0,2,1:T(8,128)S(1)}, f32[96,1,224]{0,2,1:T(8,128)S(1)}, u32[]{:S(2)}, u32[]{:S(2)}) collective-permute-start(f32[96,1,224]{0,2,1:T(8,128)S(1)} %get-tuple-element.42), channel_id=1, source_target_pairs={{0,4},{4,8},{8,12},{12,16},{16,20},{20,24},{24,28},{1,5},{5,9},{9,... | collective-permute-start | bytes 258056 | tf_op jit(solution)/shard_map/ppermute | solution.py:18
  141.2 9.4 %collective-permute-start.21 = (f32[96,1,224]{0,2,1:T(8,128)}, f32[96,1,224]{0,2,1:T(8,128)S(1)}, u32[]{:S(2)}, u32[]{:S(2)}) collective-permute-start(f32[96,1,224]{0,2,1:T(8,128)} %get-tuple-element.43), channel_id=1, source_target_pairs={{4,0},{8,4},{12,8},{16,12},{20,16},{24,20},{28,24},{5,1},{9,5},{13... | collective-permute-start | bytes 258056 | tf_op jit(solution)/shard_map/ppermute | solution.py:19
  144.2 7.3 %collective-permute-start.22 = (f32[96,1,224]{0,2,1:T(8,128)}, f32[96,1,224]{0,2,1:T(8,128)S(1)}, u32[]{:S(2)}, u32[]{:S(2)}) collective-permute-start(f32[96,1,224]{0,2,1:T(8,128)} %get-tuple-element.44), channel_id=1, source_target_pairs={{0,1},{1,2},{2,3},{4,5},{5,6},{6,7},{8,9},{9,10},{10,11},{12,13},{... | collective-permute-start | bytes 258056 | tf_op jit(solution)/shard_map/ppermute | solution.py:18
  148.1 6.9 %collective-permute-start.23 = (f32[96,1,224]{0,2,1:T(8,128)}, f32[96,1,224]{0,2,1:T(8,128)S(1)}, u32[]{:S(2)}, u32[]{:S(2)}) collective-permute-start(f32[96,1,224]{0,2,1:T(8,128)} %get-tuple-element.45), channel_id=1, source_target_pairs={{1,0},{2,1},{3,2},{5,4},{6,5},{7,6},{9,8},{10,9},{11,10},{13,12},{... | collective-permute-start | bytes 258056 | tf_op jit(solution)/shard_map/ppermute | solution.py:19
  192.8 6.8 %collective-permute-start.27 = (f32[3,1,96,12]{2,3,1,0:T(8,128)S(1)}, f32[3,1,96,12]{2,3,1,0:T(8,128)S(1)}, u32[]{:S(2)}, u32[]{:S(2)}) collective-permute-start(f32[3,1,96,12]{2,3,1,0:T(8,128)S(1)} %pad_maximum_fusion.2), channel_id=1, source_target_pairs={{1,0},{2,1},{3,2},{5,4},{6,5},{7,6},{9,8},{10,9},{11,10},{13,12},{... | collective-permute-start | bytes 41480 | tf_op jit(solution)/shard_map/ppermute | solution.py:19
  203.2 9.9 %collective-permute-start.28 = (f32[96,1,224]{0,2,1:T(8,128)S(1)}, f32[96,1,224]{0,2,1:T(8,128)S(1)}, u32[]{:S(2)}, u32[]{:S(2)}) collective-permute-start(f32[96,1,224]{0,2,1:T(8,128)S(1)} %get-tuple-element.38), channel_id=1, source_target_pairs={{0,4},{4,8},{8,12},{12,16},{16,20},{20,24},{24,28},{1,5},{5,9},{9,... | collective-permute-start | bytes 258056 | tf_op jit(solution)/shard_map/ppermute | solution.py:18
  204.8 9.2 %collective-permute-start.29 = (f32[96,1,224]{0,2,1:T(8,128)}, f32[96,1,224]{0,2,1:T(8,128)S(1)}, u32[]{:S(2)}, u32[]{:S(2)}) collective-permute-start(f32[96,1,224]{0,2,1:T(8,128)} %get-tuple-element.39), channel_id=1, source_target_pairs={{4,0},{8,4},{12,8},{16,12},{20,16},{24,20},{28,24},{5,1},{9,5},{13... | collective-permute-start | bytes 258056 | tf_op jit(solution)/shard_map/ppermute | solution.py:19
  207.9 7.1 %collective-permute-start.30 = (f32[96,1,224]{0,2,1:T(8,128)}, f32[96,1,224]{0,2,1:T(8,128)S(1)}, u32[]{:S(2)}, u32[]{:S(2)}) collective-permute-start(f32[96,1,224]{0,2,1:T(8,128)} %get-tuple-element.40), channel_id=1, source_target_pairs={{0,1},{1,2},{2,3},{4,5},{5,6},{6,7},{8,9},{9,10},{10,11},{12,13},{... | collective-permute-start | bytes 258056 | tf_op jit(solution)/shard_map/ppermute | solution.py:18
  211.8 6.9 %collective-permute-start.31 = (f32[96,1,224]{0,2,1:T(8,128)}, f32[96,1,224]{0,2,1:T(8,128)S(1)}, u32[]{:S(2)}, u32[]{:S(2)}) collective-permute-start(f32[96,1,224]{0,2,1:T(8,128)} %get-tuple-element.41), channel_id=1, source_target_pairs={{1,0},{2,1},{3,2},{5,4},{6,5},{7,6},{9,8},{10,9},{11,10},{13,12},{... | collective-permute-start | bytes 258056 | tf_op jit(solution)/shard_map/ppermute | solution.py:19
  256.5 6.8 %collective-permute-start.35 = (f32[3,1,96,12]{2,3,1,0:T(8,128)S(1)}, f32[3,1,96,12]{2,3,1,0:T(8,128)S(1)}, u32[]{:S(2)}, u32[]{:S(2)}) collective-permute-start(f32[3,1,96,12]{2,3,1,0:T(8,128)S(1)} %pad_maximum_fusion.3), channel_id=1, source_target_pairs={{1,0},{2,1},{3,2},{5,4},{6,5},{7,6},{9,8},{10,9},{11,10},{13,12},{... | collective-permute-start | bytes 41480 | tf_op jit(solution)/shard_map/ppermute | solution.py:19
  257.8 6.3 %collective-permute-start.34 = (f32[3,1,96,12]{2,3,1,0:T(8,128)S(1)}, f32[3,1,96,12]{2,3,1,0:T(8,128)S(1)}, u32[]{:S(2)}, u32[]{:S(2)}) collective-permute-start(f32[3,1,96,12]{2,3,1,0:T(8,128)S(1)} %pad_maximum_fusion.3), channel_id=1, source_target_pairs={{0,1},{1,2},{2,3},{4,5},{5,6},{6,7},{8,9},{9,10},{10,11},{12,13},{... | collective-permute-start | bytes 41480 | tf_op jit(solution)/shard_map/ppermute | solution.py:18
  268.7 9.9 %collective-permute-start.36 = (f32[96,1,224]{0,2,1:T(8,128)}, f32[96,1,224]{0,2,1:T(8,128)S(1)}, u32[]{:S(2)}, u32[]{:S(2)}) collective-permute-start(f32[96,1,224]{0,2,1:T(8,128)} %get-tuple-element.34), channel_id=1, source_target_pairs={{0,4},{4,8},{8,12},{12,16},{16,20},{20,24},{24,28},{1,5},{5,9},{9,... | collective-permute-start | bytes 258056 | tf_op jit(solution)/shard_map/ppermute | solution.py:18
  270.3 9.2 %collective-permute-start.37 = (f32[96,1,224]{0,2,1:T(8,128)}, f32[96,1,224]{0,2,1:T(8,128)S(1)}, u32[]{:S(2)}, u32[]{:S(2)}) collective-permute-start(f32[96,1,224]{0,2,1:T(8,128)} %get-tuple-element.35), channel_id=1, source_target_pairs={{4,0},{8,4},{12,8},{16,12},{20,16},{24,20},{28,24},{5,1},{9,5},{13... | collective-permute-start | bytes 258056 | tf_op jit(solution)/shard_map/ppermute | solution.py:19
  273.4 7.1 %collective-permute-start.38 = (f32[96,1,224]{0,2,1:T(8,128)}, f32[96,1,224]{0,2,1:T(8,128)S(1)}, u32[]{:S(2)}, u32[]{:S(2)}) collective-permute-start(f32[96,1,224]{0,2,1:T(8,128)} %get-tuple-element.36), channel_id=1, source_target_pairs={{0,1},{1,2},{2,3},{4,5},{5,6},{6,7},{8,9},{9,10},{10,11},{12,13},{... | collective-permute-start | bytes 258056 | tf_op jit(solution)/shard_map/ppermute | solution.py:18
  277.3 6.9 %collective-permute-start.39 = (f32[96,1,224]{0,2,1:T(8,128)}, f32[96,1,224]{0,2,1:T(8,128)S(1)}, u32[]{:S(2)}, u32[]{:S(2)}) collective-permute-start(f32[96,1,224]{0,2,1:T(8,128)} %get-tuple-element.37), channel_id=1, source_target_pairs={{1,0},{2,1},{3,2},{5,4},{6,5},{7,6},{9,8},{10,9},{11,10},{13,12},{... | collective-permute-start | bytes 258056 | tf_op jit(solution)/shard_map/ppermute | solution.py:19
  323.6 6.5 %collective-permute-start.43 = (f32[3,1,96,12]{2,3,1,0:T(8,128)S(1)}, f32[3,1,96,12]{2,3,1,0:T(8,128)S(1)}, u32[]{:S(2)}, u32[]{:S(2)}) collective-permute-start(f32[3,1,96,12]{2,3,1,0:T(8,128)S(1)} %pad_maximum_fusion.4), channel_id=1, source_target_pairs={{1,0},{2,1},{3,2},{5,4},{6,5},{7,6},{9,8},{10,9},{11,10},{13,12},{... | collective-permute-start | bytes 41480 | tf_op jit(solution)/shard_map/ppermute | solution.py:19
  (81 other events, 1210.2 us)
where the time goes:
time: 337 us; the launch traced here: 334 us
  blocking collectives  132 us (39%)
  starting transfers between devices  115 us (34%)
  local copies, waits for them, and re-layouts  40.5 us (12%)
  waiting for transfers between devices  19.7 us (6%)
  matrix products  17.2 us (5%)
  other arithmetic  6.17 us (2%)
  between operations  3.52 us (1%)
    ppermute x22, starting transfers between devices, extended(): before = lax.ppermute(last, axis, up)  75.6 us
    all_gather x5, blocking collectives, coarse_values(): lax.all_gather(coeffs, 'gx', axis=1, tiled=True)  69.8 us
    unnamed x5, blocking collectives  62.4 us
    ppermute x22, starting transfers between devices, extended(): after = lax.ppermute(first, axis, down)  28.5 us
    ppermute x22, waiting for transfers between devices, extended(): after = lax.ppermute(first, axis, down)  11.3 us
    unnamed x5, starting transfers between devices  10.5 us
    dot_general x20, matrix products, project(): jnp.dot(sources[face_index], neighbour_modes[face_index], precision=preci...  6.88 us
  transfers between devices with their start and end apart: 49, of which 17 were waited for; matrix products, arithmetic and copies ran while one was open for 15% of the time, Pallas kernels for 0%

commit v1 on v0

v1 whole, which is shorter than its diff:
```python
import functools

import jax
import jax.numpy as jnp
from jax import lax
from jax.experimental import pallas as pl
from jax.experimental.pallas import tpu as pltpu
from jax.sharding import PartitionSpec as P

f32 = jnp.float32
bf16 = jnp.bfloat16
precise = lax.Precision.HIGHEST
spectrum_low = 0.5
spectrum_high = 4.0

EVEN_FACES = (1, 0, 3, 2)
ODD_FACES = (0, 1, 2, 3)
ARRIVES = (0, 1, 3, 2)
REORDERED = (0, 2)


def round_up(value, unit):
    return -(-value // unit) * unit


def exchanges(rows, cols):
    def pairs(target):
        return [
            (a * cols + b, target(a, b)[0] * cols + target(a, b)[1])
            for a in range(rows)
            for b in range(cols)
        ]

    def along(a, b, step):
        return (a, b + step) if 0 <= b + step < cols else (a ^ 1, b)

    return (
        pairs(lambda a, b: (a ^ 1, b)),
        pairs(lambda a, b: ((a + 1 if a % 2 else a - 1) % rows, b)),
        pairs(lambda a, b: along(a, b, -1 if a % 2 else 1)),
        pairs(lambda a, b: along(a, b, 1 if a % 2 else -1)),
    )


def exchange(values, lists):
    return [lax.ppermute(value, ("gx", "gy"), pairs) for value, pairs in zip(values, lists)]


def chebyshev_coefficients():
    center = (spectrum_high + spectrum_low) / 2.0
    radius = (spectrum_high - spectrum_low) / 2.0
    center_ratio = center / radius
    factor_prev = 1.0 / center_ratio
    result = [(1.0 / center, 0.0)]
    factor = 1.0 / (2.0 * center_ratio - factor_prev)
    result.append((2.0 * factor / radius, factor * factor_prev))
    return result


def split3(value):
    high = value.astype(bf16)
    rest = value - high.astype(f32)
    middle = rest.astype(bf16)
    low = (rest - middle.astype(f32)).astype(bf16)
    return high, middle, low


def contract(left, right, left_dim, right_dim, precision=None):
    return lax.dot_general(
        left,
        right,
        (((left_dim,), (right_dim,)), ((), ())),
        precision=precision,
        preferred_element_type=f32,
    )


def by_parity(parity, even, odd):
    return jnp.where(parity == 0, even, odd)


def face_columns(value, slot, parity, width):
    even, odd = EVEN_FACES[slot], ODD_FACES[slot]
    return by_parity(
        parity,
        value[:, even * width : (even + 1) * width],
        value[:, odd * width : (odd + 1) * width],
    )


def reorder_matrix(partners, slot, parity, width, padded):
    plain = lax.broadcasted_iota(jnp.int32, (1, width), 1)

    def places(face):
        return partners[face : face + 1, :] if face in REORDERED else plain

    place = by_parity(parity, places(EVEN_FACES[slot]), places(ODD_FACES[slot]))
    rows = lax.broadcasted_iota(jnp.int32, (padded, width), 0)
    return jnp.where(rows == place, 1.0, 0.0).astype(bf16)


def reorder_exact(value, matrix, dim):
    count = value.shape[0]
    parts = contract(jnp.concatenate(split3(value), axis=0), matrix, 1, dim)
    return parts[:count] + (parts[count : 2 * count] + parts[2 * count :])


def live_columns(counts_ref, slot, parity, padded):
    count = by_parity(parity, counts_ref[EVEN_FACES[slot]], counts_ref[ODD_FACES[slot]])
    return lax.broadcasted_iota(jnp.int32, (1, padded), 1) < count


def load_kernel(parity_ref, load_ref, modes_ref, partners_ref, *face_refs):
    parity = parity_ref[0]
    width = partners_ref.shape[1]
    columns, count = load_ref.shape[0], modes_ref.shape[0]
    padded = face_refs[0].shape[1]
    for slot, face_ref in enumerate(face_refs):
        matrix = reorder_matrix(partners_ref[...], slot, parity, width, padded)
        values = face_columns(load_ref[...], slot, parity, width)
        modes = face_columns(modes_ref[...], slot, parity, width)
        face_ref[columns:, :] = jnp.zeros((face_ref.shape[0] - columns, padded), f32)
        face_ref[:columns, :] = reorder_exact(values, matrix, 1)
        face_ref[columns : columns + count, :] = contract(modes, matrix, 1, 1)


def matrix_kernel(parity_ref, matrix_ref, partners_ref, out_ref):
    parity = parity_ref[0]
    width = partners_ref.shape[1]
    padded = out_ref.shape[1] // 4
    reorder = [reorder_matrix(partners_ref[...], s, parity, width, padded) for s in range(4)]
    for slot in range(4):
        block = face_columns(matrix_ref[...], slot, parity, width)
        block = contract(block, reorder[slot], 1, 1).astype(bf16)
        for row_slot in range(4):
            even, odd = EVEN_FACES[row_slot], ODD_FACES[row_slot]
            rows = by_parity(
                parity,
                block[even * width : (even + 1) * width],
                block[odd * width : (odd + 1) * width],
            )
            out_ref[
                row_slot * padded : (row_slot + 1) * padded, slot * padded : (slot + 1) * padded
            ] = contract(reorder[row_slot], rows, 1, 0).astype(bf16)


def inverse_kernel(group, own_ref, *refs):
    neighbour_refs, (out_ref, rows_ref) = refs[:4], refs[4:]
    cols, count, length = own_ref.shape
    rows = length // count
    long, short = pack_counts(count)
    ratio = long // short
    rows_ref[...] = jnp.zeros(rows_ref.shape, f32)
    wide = rows * long
    source = lax.broadcasted_iota(jnp.int32, (length, wide), 0)
    target = lax.broadcasted_iota(jnp.int32, (length, wide), 1)
    source_row, source_mode = lax.div(source, count), lax.rem(source, count)
    target_row, target_place = lax.div(target, long), lax.rem(target, long)
    same = source_row == target_row
    places = [jnp.where(same & (source_mode == target_place), 1.0, 0.0).astype(f32)]
    for part in range(ratio):
        wanted = target_place - part * short
        inside = (wanted >= 0) & (wanted < short)
        places.append(
            jnp.where(same & inside & (source_mode == long + wanted), 1.0, 0.0).astype(f32)
        )
    gathered = [[] for _ in places]
    for e in range(cols):
        for index, ref in enumerate((own_ref, *neighbour_refs)):
            rows_ref[index * group : index * group + count, :] = ref[e]
        for part, place in enumerate(places):
            gathered[part].append(contract(rows_ref[...], place, 1, 0, precise))
    height = rows_ref.shape[0]
    for part, pieces in enumerate(gathered):
        out_ref[part * height : (part + 1) * height, :] = jnp.concatenate(pieces, axis=1)


def pack_counts(count):
    long = count * 3 // 4
    return long, count - long


def pack_coefficients(coeffs, count):
    long, short = pack_counts(count)
    pieces = long // short
    piece = coeffs.shape[1] // pieces
    tail = coeffs[long:count]
    side = jnp.concatenate([tail[:, i * piece : (i + 1) * piece] for i in range(pieces)], axis=0)
    return jnp.concatenate([coeffs[:long], side], axis=1)


def write_copies(out_ref, value):
    height = value.shape[0]
    copies = out_ref.shape[0] // height
    together = 8 if copies % 8 == 0 else 1
    block = jnp.concatenate([value] * together, axis=0)
    for i in range(copies // together):
        out_ref[i * together * height : (i + 1) * together * height, :] = block


def join_kernel(count, columns, first, parity_ref, counts_ref, *refs):
    sent, arrived = refs[:4], refs[4:8]
    parity = parity_ref[0]
    padded = sent[0].shape[1]
    if first:
        vector_ref, coeff_ref, modes_ref, extended_ref = refs[8:]
        group = modes_ref.shape[0]
        third = extended_ref.shape[0] // 3
        extended_ref[...] = jnp.zeros(extended_ref.shape, bf16)
    else:
        modes_ref, vector_ref, coeff_ref = refs[8:]
    for slot in range(4):
        live = live_columns(counts_ref, slot, parity, padded)
        place = slice(slot * padded, (slot + 1) * padded)
        own, other = sent[slot], arrived[ARRIVES.index(slot)]
        total = own[:columns, :] + other[:columns, :]
        vector_ref[:, place] = jnp.where(live, total, 0.0)
        if first:
            own_modes = jnp.where(live, own[columns : columns + group, :], 0.0).astype(bf16)
            other_modes = jnp.where(live, other[columns : columns + group, :], 0.0).astype(bf16)
            modes_ref[:, place] = own_modes
            for copy in range(3):
                base = copy * third
                extended_ref[base : base + group, place] = own_modes
                base += (1 + slot) * group
                extended_ref[base : base + group, place] = other_modes
    parts = contract(modes_ref[...], jnp.concatenate(split3(vector_ref[...]), axis=0), 1, 1)
    coeffs = parts[:, :columns] + (
        parts[:, columns : 2 * columns] + parts[:, 2 * columns : 3 * columns]
    )
    write_copies(coeff_ref, pack_coefficients(coeffs, count))


def projected(coeff_ref, inverse_ref, extended_ref, vector_ref):
    columns = vector_ref.shape[0]
    terms = contract(inverse_ref[...], coeff_ref[...], 1, 0, precise)
    height = extended_ref.shape[0] // 3
    solved = terms[:height, :columns] + jnp.concatenate(
        [
            terms[i * height : (i + 1) * height, columns:]
            for i in range(1, terms.shape[0] // height)
        ],
        axis=1,
    )
    parts = jnp.concatenate(split3(solved), axis=0)
    return vector_ref[...] - contract(parts, extended_ref[...], 0, 0)


def apply_matrix(vector, matrix_ref, face_refs):
    rounded = vector.astype(bf16)
    padded = matrix_ref.shape[1] // 4
    for slot, face_ref in enumerate(face_refs):
        face_ref[...] = contract(
            rounded, matrix_ref[:, slot * padded : (slot + 1) * padded], 1, 0
        )


def start_kernel(coeff_ref, inverse_ref, extended_ref, vector_ref, matrix_ref, *refs):
    residual_ref, face_refs = refs[0], refs[1:]
    residual = projected(coeff_ref, inverse_ref, extended_ref, vector_ref)
    residual_ref[...] = residual
    apply_matrix(residual, matrix_ref, face_refs)


def residual_kernel(coeff_ref, inverse_ref, extended_ref, vector_ref, matrix_ref, old_ref, *refs):
    residual_ref, face_refs = refs[0], refs[1:]
    residual = old_ref[...] - projected(coeff_ref, inverse_ref, extended_ref, vector_ref)
    residual_ref[...] = residual
    apply_matrix(residual, matrix_ref, face_refs)


def first_direction_kernel(alpha, coeff_ref, inverse_ref, extended_ref, vector_ref, matrix_ref, *refs):
    direction_ref, face_refs = refs[0], refs[1:]
    direction = alpha * projected(coeff_ref, inverse_ref, extended_ref, vector_ref)
    direction_ref[...] = direction
    apply_matrix(direction, matrix_ref, face_refs)


def direction_kernel(
    alpha, beta, coeff_ref, inverse_ref, extended_ref, vector_ref, matrix_ref, old_ref, *refs
):
    multipliers_ref, face_refs = refs[0], refs[1:]
    old = old_ref[...]
    preconditioned = projected(coeff_ref, inverse_ref, extended_ref, vector_ref)
    direction = alpha * preconditioned + beta * old
    multipliers_ref[...] = old + direction
    apply_matrix(direction, matrix_ref, face_refs)


def face_order(value, parity, partners, width):
    padded = value.shape[1] // 4
    slots = []
    for slot in range(4):
        matrix = reorder_matrix(partners, slot, parity, width, padded)
        slots.append(reorder_exact(value[:, slot * padded : (slot + 1) * padded], matrix, 0))
    return jnp.concatenate(
        [
            by_parity(parity, slots[EVEN_FACES.index(face)], slots[ODD_FACES.index(face)])
            for face in range(4)
        ],
        axis=1,
    )


def last_kernel(
    parity_ref, coeff_ref, inverse_ref, extended_ref, vector_ref, old_ref, partners_ref, out_ref
):
    residual = old_ref[...] - projected(coeff_ref, inverse_ref, extended_ref, vector_ref)
    out_ref[...] = face_order(residual, parity_ref[0], partners_ref[...], partners_ref.shape[1])


def multipliers_kernel(parity_ref, vector_ref, partners_ref, out_ref):
    out_ref[...] = face_order(
        vector_ref[...], parity_ref[0], partners_ref[...], partners_ref.shape[1]
    )


def call(kernel, outs, args, scalars=0, scratch=()):
    smem = pl.BlockSpec(memory_space=pltpu.SMEM)
    vmem = pl.BlockSpec(memory_space=pltpu.VMEM)
    size = sum(o.size * o.dtype.itemsize for o in (*outs, *args))
    return pl.pallas_call(
        kernel,
        out_shape=tuple(outs),
        in_specs=[smem] * scalars + [vmem] * (len(args) - scalars),
        out_specs=tuple([vmem] * len(outs)),
        scratch_shapes=list(scratch),
        compiler_params=pltpu.CompilerParams(
            vmem_limit_bytes=min(2 * size + (16 << 20), 56 << 20)
        ),
    )(*args)


def local(rows, cols, load, dual_operator, dirichlet, modes, coarse_inverse, face_counts, partners):
    devices = rows * cols
    columns, slots = load.shape[2:]
    width = partners.shape[3]
    padded = round_up(width, 128)
    count = modes.shape[2]
    group = round_up(count, 16)
    long, short = pack_counts(count)
    packed = columns + columns // (long // short)
    lists = exchanges(rows, cols)
    shape = jax.ShapeDtypeStruct
    vector = shape((columns, 4 * padded), f32)
    faces = [shape((columns, padded), f32)] * 4
    tall_faces = [shape((columns + group, padded), f32)] * 4
    matrix = shape((4 * padded, 4 * padded), bf16)
    coeff = shape((devices * long, packed), f32)
    height = 5 * group

    parity = (lax.axis_index("gx") % 2).astype(jnp.int32).reshape(1)
    counts = face_counts[0, 0]
    partners = partners[0, 0]
    chebyshev = chebyshev_coefficients()

    def everywhere(values):
        chunks = values.reshape(devices, long, 1, packed)
        return lax.all_to_all(chunks, ("gy", "gx"), 0, 0).reshape(devices * long, packed)

    sent = call(load_kernel, tall_faces, (parity, load[0, 0], modes[0, 0], partners), 1)
    arrived = exchange(sent, lists)
    own_rows = lax.all_to_all(
        coarse_inverse[0, :, 0, :].reshape(cols, count, rows * count), "gy", 0, 0
    )
    other_rows = exchange([own_rows] * 4, lists)
    (inverse,) = call(
        functools.partial(inverse_kernel, group),
        [shape(((1 + long // short) * height, devices * long), f32)],
        (own_rows, *[other_rows[ARRIVES.index(slot)] for slot in range(4)]),
        scratch=[pltpu.VMEM((height, rows * count), f32)],
    )
    (smoother,) = call(matrix_kernel, [matrix], (parity, dirichlet[0, 0], partners), 1)
    (operator,) = call(matrix_kernel, [matrix], (parity, dual_operator[0, 0], partners), 1)

    current, coeffs, mode_rows, extended = call(
        functools.partial(join_kernel, count, columns, True),
        [vector, coeff, shape((group, 4 * padded), bf16), shape((3 * height, 4 * padded), bf16)],
        (parity, counts, *sent, *arrived),
        2,
    )

    def join(sent):
        arrived = exchange(sent, lists)
        current, coeffs = call(
            functools.partial(join_kernel, count, columns, False),
            [vector, coeff],
            (parity, counts, *sent, *arrived, mode_rows),
            2,
        )
        return everywhere(coeffs), inverse, extended, current

    (alpha_0, _), (alpha_1, beta_1) = chebyshev
    residual, *sent = call(
        start_kernel,
        [vector, *faces],
        (everywhere(coeffs), inverse, extended, current, smoother),
    )
    direction, *sent = call(
        functools.partial(first_direction_kernel, alpha_0),
        [vector, *faces],
        (*join(sent), operator),
    )
    residual, *sent = call(
        residual_kernel, [vector, *faces], (*join(sent), smoother, residual)
    )
    multipliers, *sent = call(
        functools.partial(direction_kernel, alpha_1, beta_1),
        [vector, *faces],
        (*join(sent), operator, direction),
    )
    result = shape((columns, slots), f32)
    (residual,) = call(last_kernel, [result], (parity, *join(sent), residual, partners), 1)
    (multipliers,) = call(multipliers_kernel, [result], (parity, multipliers, partners), 1)
    return (multipliers[None, None], residual[None, None])


def solution(mesh):
    return jax.shard_map(
        functools.partial(local, mesh.shape["gx"], mesh.shape["gy"]),
        mesh=mesh,
        in_specs=(
            P("gx", "gy", None, None),
            P("gx", "gy", None, None),
            P("gx", "gy", None, None),
            P("gx", "gy", None, None),
            P("gx", None, "gy", None),
            P("gx", "gy", None),
            P("gx", "gy", None, None),
        ),
        out_specs=(P("gx", "gy", None, None), P("gx", "gy", None, None)),
        check_vma=False,
    )
```

time: 337 us -> 125 us (0.37)
  blocking collectives: 132 us -> 21.3 us
  starting transfers between devices: 115 us -> 32.6 us
  local copies, waits for them, and re-layouts: 40.5 us -> 14.2 us
  Pallas kernels: 0 us -> 22.1 us
  matrix products: 17.2 us -> 0 us
  waiting for transfers between devices: 19.7 us -> 31.8 us
  other arithmetic: 6.17 us -> 1.45 us
    ppermute x44 -> x24, starting transfers between devices: 104 us -> 18.1 us  [exchange(): lax.ppermute(value, ('gx', 'gy'), pairs)]
    all_gather x5 -> x0, blocking collectives: 69.8 us -> none  [coarse_values(): lax.all_gather(coeffs, 'gx', axis=1, tiled=True)]
    unnamed x5 -> x0, blocking collectives: 62.4 us -> none
    pallas_call x0 -> x15, Pallas kernels: none -> 22.1 us  [call(): pl.pallas_call(kernel, out_shape=tuple(outs), in_specs=[smem] * scalars +...]
    all_to_all x0 -> x2, blocking collectives: none -> 21.3 us  [everywhere(): lax.all_to_all(chunks, ('gy', 'gx'), 0, 0).reshape(devices * long, packed)]
    gather x44 -> x0, local copies, waits for them, and re-layouts: 20.4 us -> none  [the longest x10 4.56 us: assemble_west_east(): jnp.take(padded[:, 3], partner_slots[1], axis=1)]
    dot_general x39 -> x0, matrix products: 17.2 us -> none  [the longest x20 6.88 us: project(): jnp.dot(sources[face_index], neighbour_modes[face_index], precision=preci...]
    all_to_all x0 -> x4, starting transfers between devices: none -> 14.5 us  [the longest x3 9.19 us: everywhere(): lax.all_to_all(chunks, ('gy', 'gx'), 0, 0).reshape(devices * long, packed)]
  transfers between devices with their start and end apart: 49 -> 28, of which waited for: 17 -> 11; matrix products, arithmetic and copies ran while one was open for 15% -> 2% of each run, Pallas kernels for 0% -> 6%
where the time goes in v1:
time: 125 us; the launch traced here: 124 us
  starting transfers between devices  32.6 us (26%)
  waiting for transfers between devices  31.8 us (25%)
  Pallas kernels  22.1 us (18%)
  blocking collectives  21.3 us (17%)
  local copies, waits for them, and re-layouts  14.2 us (11%)
  other arithmetic  1.45 us (1%)
    pallas_call x15, Pallas kernels, call(): pl.pallas_call(kernel, out_shape=tuple(outs), in_specs=[smem] * scalars +...  22.1 us
    all_to_all x2, blocking collectives, everywhere(): lax.all_to_all(chunks, ('gy', 'gx'), 0, 0).reshape(devices * long, packed)  21.3 us
    ppermute x24, waiting for transfers between devices, exchange(): lax.ppermute(value, ('gx', 'gy'), pairs)  18.5 us
    ppermute x24, starting transfers between devices, exchange(): lax.ppermute(value, ('gx', 'gy'), pairs)  18.1 us
    unnamed x41, local copies, waits for them, and re-layouts  13.6 us
    all_to_all x3, waiting for transfers between devices, everywhere(): lax.all_to_all(chunks, ('gy', 'gx'), 0, 0).reshape(devices * long, packed)  11 us
    all_to_all x3, starting transfers between devices, everywhere(): lax.all_to_all(chunks, ('gy', 'gx'), 0, 0).reshape(devices * long, packed)  9.19 us
    all_to_all x1, starting transfers between devices, local(): lax.all_to_all(coarse_inverse[0, :, 0, :].reshape(cols, count, rows * cou...  5.32 us
  transfers between devices with their start and end apart: 28, of which 11 were waited for; matrix products, arithmetic and copies ran while one was open for 2% of the time, Pallas kernels for 6%

profile of v1, /device:TPU:0, one launch (start us, length us, event | category | flops | bytes accessed | tf_op | source)
XLA Modules:
  0.0 124.4 jit_solution(8435760739417066239)
XLA Ops:
  4.2 3.6 %collective-permute-start.1 = (f32[112,256]{1,0:T(8,128)S(1)}, f32[112,256]{1,0:T(8,128)S(1)}, u32[]{:S(2)}, u32[]{:S(2)}) collective-permute-start(f32[112,256]{1,0:T(8,128)S(1)} %get-tuple-element.39.refs_1_), channel_id=1, source_target_pairs={{0,28},{1,29},{2,30},{3,31},{4,8},{5,9},{6,10},{7,11},{8,4},{9,5},... | collective-permute-start | bytes 344072 | tf_op jit(solution)/shard_map/ppermute | solution.py:46
  7.7 1.6 %collective-permute-start.2 = (f32[112,256]{1,0:T(8,128)S(1)}, f32[112,256]{1,0:T(8,128)S(1)}, u32[]{:S(2)}, u32[]{:S(2)}) collective-permute-start(f32[112,256]{1,0:T(8,128)S(1)} %get-tuple-element.40.refs_2_), channel_id=1, source_target_pairs={{0,1},{1,2},{2,3},{3,7},{4,0},{5,4},{6,5},{7,6},{8,9},{9,10},{10,1... | collective-permute-start | bytes 344072 | tf_op jit(solution)/shard_map/ppermute | solution.py:46
  9.8 1.4 %reduce.3 = f32[48,96]{1,0:T(8,128)S(1)} reduce(f32[1,48,1,96]{3,2,1,0:T(1,128)} %param.11, f32[]{:T(128)} %broadcast.4), dimensions={0,2}, to_apply=%param.11.reduce_sub_computation.3 | reduce | bytes 36868 | tf_op args[4]
  11.9 5.3 %all-to-all-start.1 = ((f32[4,12,96]{2,1,0:T(8,128)}), f32[4,12,96]{2,1,0:T(8,128)S(1)}, u32[]{:S(2)}, u32[]{:S(2)}) async-start(f32[4,12,96]{2,1,0:T(8,128)} %reshape_squeeze.3), calls=%async_computation.1 | async-start | bytes 65536 | tf_op jit(solution)/shard_map/all_to_all | solution.py:363
  17.9 1.8 %shard_map.87 = (f32[96,1024]{1,0:T(8,128)S(1)}, f32[288,128]{1,0:T(8,128)}, bf16[16,1024]{1,0:T(8,128)(2,1)S(1)}, bf16[240,1024]{1,0:T(8,128)(2,1)S(1)}) custom-call(s32[1]{0:T(128)} %bitcast.parity_ref, s32[4]{0:T(128)S(1)} %bitcast.36, f32[112,256]{1,0:T(8,128)S(1)} %get-tuple-element.38.refs_0_, f32[112,256]{1,0:T(8,128)S(1)} %get-tuple-element.39.refs_1_, ...), custom_call_target="tpu_custom_call" | custom-call | tf_op jit(solution)/shard_map/pallas_call | solution.py:322
  20.5 2.4 %all-to-all-done.1.own_ref = f32[4,12,96]{2,1,0:T(8,128)S(1)} async-done(((f32[4,12,96]{2,1,0:T(8,128)}), f32[4,12,96]{2,1,0:T(8,128)S(1)}, u32[]{:S(2)}, u32[]{:S(2)}) %all-to-all-start.1) | async-done | bytes 18464 | tf_op jit(solution)/shard_map/all_to_all | solution.py:363
  22.9 2.6 %all-to-all-start = ((f32[32,9,1,128]{3,2,1,0:T(1,128)}), f32[32,9,1,128]{3,2,1,0:T(1,128)S(1)}, u32[]{:S(2)}, u32[]{:S(2)}) async-start(f32[32,9,1,128]{3,2,1,0:T(1,128)} %bitcast.5), calls=%async_computation | async-start | bytes 294912 | tf_op jit(solution)/shard_map/all_to_all | solution.py:359
  25.4 1.7 %collective-permute-start.7 = (f32[4,12,96]{2,1,0:T(8,128)S(1)}, f32[4,12,96]{2,1,0:T(8,128)S(1)}, u32[]{:S(2)}, u32[]{:S(2)}) collective-permute-start(f32[4,12,96]{2,1,0:T(8,128)S(1)} %all-to-all-done.1.own_ref), channel_id=1, source_target_pairs={{0,1},{1,2},{2,3},{3,7},{4,0},{5,4},{6,5},{7,6},{8,9},{9,10},{10,1... | collective-permute-start | bytes 55304 | tf_op jit(solution)/shard_map/ppermute | solution.py:46
  27.2 2.1 %collective-permute-start.5 = (f32[4,12,96]{2,1,0:T(8,128)S(1)}, f32[4,12,96]{2,1,0:T(8,128)S(1)}, u32[]{:S(2)}, u32[]{:S(2)}) collective-permute-start(f32[4,12,96]{2,1,0:T(8,128)S(1)} %all-to-all-done.1.own_ref), channel_id=1, source_target_pairs={{0,28},{1,29},{2,30},{3,31},{4,8},{5,9},{6,10},{7,11},{8,4},{9,5},... | collective-permute-start | bytes 55304 | tf_op jit(solution)/shard_map/ppermute | solution.py:46
  29.3 1.4 %copy-done.3 = bf16[1,1,896,896]{3,2,1,0:T(8,128)(2,1)S(1)} copy-done((bf16[1,1,896,896]{3,2,1,0:T(8,128)(2,1)S(1)}, bf16[1,1,896,896]{3,2,1,0:T(8,128)(2,1)}, u32[]{:S(2)}) %copy-start.3) | copy-done | bytes 1605656
  31.4 1.9 %shard_map.89.matrix_ref = bf16[1024,1024]{1,0:T(8,128)(2,1)S(1)} custom-call(s32[1]{0:T(128)} %bitcast.parity_ref, bf16[896,896]{1,0:T(8,128)(2,1)S(1)} %bitcast.20, s32[4,224]{1,0:T(4,128)S(1)} %bitcast.31), custom_call_target="tpu_custom_call" | custom-call | tf_op jit(solution)/shard_map/pallas_call | solution.py:322
  35.2 1.5 %shard_map.90 = (f32[96,1024]{1,0:T(8,128)S(1)}, f32[96,256]{1,0:T(8,128)S(1)}, f32[96,256]{1,0:T(8,128)S(1)}, f32[96,256]{1,0:T(8,128)S(1)}, f32[96,256]{1,0:T(8,128)S(1)}) custom-call(f32[288,128]{1,0:T(8,128)S(1)} %bitcast.22, f32[320,288]{1,0:T(8,128)S(1)} %shard_map.88.inverse_ref, bf16[240,1024]{1,0:T(8,128)(2,1)S(1)} %get-tuple-element.43.extended_ref, ...), custom_call_target="tpu_custom_call" | custom-call | tf_op jit(solution)/shard_map/pallas_call | solution.py:322
  37.8 2.0 %collective-permute-start.10 = (f32[96,256]{1,0:T(8,128)S(1)}, f32[96,256]{1,0:T(8,128)S(1)}, u32[]{:S(2)}, u32[]{:S(2)}) collective-permute-start(f32[96,256]{1,0:T(8,128)S(1)} %get-tuple-element.47.refs_2_), channel_id=1, source_target_pairs={{0,1},{1,2},{2,3},{3,7},{4,0},{5,4},{6,5},{7,6},{8,9},{9,10},{10,1... | collective-permute-start | bytes 294920 | tf_op jit(solution)/shard_map/ppermute | solution.py:46
  39.8 3.1 %collective-permute-done.9.refs_5_ = f32[96,256]{1,0:T(8,128)S(1)} collective-permute-done((f32[96,256]{1,0:T(8,128)S(1)}, f32[96,256]{1,0:T(8,128)S(1)}, u32[]{:S(2)}, u32[]{:S(2)}) %collective-permute-start.9) | collective-permute-done | bytes 98336 | tf_op jit(solution)/shard_map/ppermute | solution.py:46
  43.0 1.5 %collective-permute-done.11.refs_7_ = f32[96,256]{1,0:T(8,128)S(1)} collective-permute-done((f32[96,256]{1,0:T(8,128)S(1)}, f32[96,256]{1,0:T(8,128)S(1)}, u32[]{:S(2)}, u32[]{:S(2)}) %collective-permute-start.11) | collective-permute-done | bytes 98336 | tf_op jit(solution)/shard_map/ppermute | solution.py:46
  44.4 1.8 %shard_map.91 = (f32[96,1024]{1,0:T(8,128)S(1)}, f32[288,128]{1,0:T(8,128)}) custom-call(s32[1]{0:T(128)} %bitcast.parity_ref, s32[4]{0:T(128)S(1)} %bitcast.37, f32[96,256]{1,0:T(8,128)S(1)} %get-tuple-element.45.refs_0_, f32[96,256]{1,0:T(8,128)S(1)} %get-tuple-element.46.refs_1_, f32[96,256]{1,0:T(8,128)S(1)} %get-tuple-element.47.refs_2_, ...), custom_call_target="tpu_custom_call" | custom-call | tf_op jit(solution)/shard_map/pallas_call | solution.py:322
  47.0 4.0 %all-to-all-start.2 = ((f32[32,9,1,128]{3,2,1,0:T(1,128)}), f32[32,9,1,128]{3,2,1,0:T(1,128)S(1)}, u32[]{:S(2)}, u32[]{:S(2)}) async-start(f32[32,9,1,128]{3,2,1,0:T(1,128)} %bitcast.8), calls=%async_computation.2 | async-start | bytes 294912 | tf_op jit(solution)/shard_map/all_to_all | solution.py:359
  52.5 1.9 %shard_map.92.matrix_ref = bf16[1024,1024]{1,0:T(8,128)(2,1)S(1)} custom-call(s32[1]{0:T(128)} %bitcast.parity_ref, bf16[896,896]{1,0:T(8,128)(2,1)S(1)} %bitcast.21, s32[4,224]{1,0:T(4,128)S(1)} %bitcast.32), custom_call_target="tpu_custom_call" | custom-call | tf_op jit(solution)/shard_map/pallas_call | solution.py:322
  55.7 3.7 %all-to-all-done.2 = f32[32,9,1,128]{3,2,1,0:T(1,128)S(1)} async-done(((f32[32,9,1,128]{3,2,1,0:T(1,128)}), f32[32,9,1,128]{3,2,1,0:T(1,128)S(1)}, u32[]{:S(2)}, u32[]{:S(2)}) %all-to-all-start.2) | async-done | bytes 147488 | tf_op jit(solution)/shard_map/all_to_all | solution.py:359
  59.5 1.6 %copy-done.1 = bf16[1024,1024]{1,0:T(8,128)(2,1)S(1)} copy-done((bf16[1024,1024]{1,0:T(8,128)(2,1)S(1)}, bf16[1024,1024]{1,0:T(8,128)(2,1)}, u32[]{:S(2)}) %copy-start.1) | copy-done | bytes 2097176
  62.1 1.5 %shard_map.93 = (f32[96,1024]{1,0:T(8,128)S(1)}, f32[96,256]{1,0:T(8,128)S(1)}, f32[96,256]{1,0:T(8,128)S(1)}, f32[96,256]{1,0:T(8,128)S(1)}, f32[96,256]{1,0:T(8,128)S(1)}) custom-call(f32[288,128]{1,0:T(8,128)S(1)} %bitcast.24, f32[320,288]{1,0:T(8,128)S(1)} %shard_map.88.inverse_ref, bf16[240,1024]{1,0:T(8,128)(2,1)S(1)} %get-tuple-element.43.extended_ref, ...), custom_call_target="tpu_custom_call" | custom-call | tf_op jit(solution)/shard_map/pallas_call | solution.py:322
  65.4 4.2 %collective-permute-done.13.refs_5_ = f32[96,256]{1,0:T(8,128)S(1)} collective-permute-done((f32[96,256]{1,0:T(8,128)S(1)}, f32[96,256]{1,0:T(8,128)S(1)}, u32[]{:S(2)}, u32[]{:S(2)}) %collective-permute-start.13) | collective-permute-done | bytes 98336 | tf_op jit(solution)/shard_map/ppermute | solution.py:46
  71.1 10.7 %all_to_all.30 = f32[32,9,1,128]{3,2,1,0:T(1,128)S(1)} all-to-all(f32[32,9,1,128]{3,2,1,0:T(1,128)S(1)} %bitcast.28), channel_id=1, replica_groups=mesh['gx'=8,'gy'=4] {'gy','gx'}, dimensions={0} | all-to-all | bytes 294912 | tf_op jit(solution)/shard_map/all_to_all | solution.py:359
  81.8 1.5 %shard_map.95 = (f32[96,1024]{1,0:T(8,128)S(1)}, f32[96,256]{1,0:T(8,128)S(1)}, f32[96,256]{1,0:T(8,128)S(1)}, f32[96,256]{1,0:T(8,128)S(1)}, f32[96,256]{1,0:T(8,128)S(1)}) custom-call(f32[288,128]{1,0:T(8,128)S(1)} %bitcast.25, f32[320,288]{1,0:T(8,128)S(1)} %shard_map.88.inverse_ref, bf16[240,1024]{1,0:T(8,128)(2,1)S(1)} %get-tuple-element.43.extended_ref, ...), custom_call_target="tpu_custom_call" | custom-call | tf_op jit(solution)/shard_map/pallas_call | solution.py:322
  85.1 4.2 %collective-permute-done.17.refs_5_ = f32[96,256]{1,0:T(8,128)S(1)} collective-permute-done((f32[96,256]{1,0:T(8,128)S(1)}, f32[96,256]{1,0:T(8,128)S(1)}, u32[]{:S(2)}, u32[]{:S(2)}) %collective-permute-start.17) | collective-permute-done | bytes 98336 | tf_op jit(solution)/shard_map/ppermute | solution.py:46
  90.9 10.7 %all_to_all.31 = f32[32,9,1,128]{3,2,1,0:T(1,128)S(1)} all-to-all(f32[32,9,1,128]{3,2,1,0:T(1,128)S(1)} %bitcast.29), channel_id=1, replica_groups=mesh['gx'=8,'gy'=4] {'gy','gx'}, dimensions={0} | all-to-all | bytes 294912 | tf_op jit(solution)/shard_map/all_to_all | solution.py:359
  101.5 1.5 %shard_map.97 = (f32[96,1024]{1,0:T(8,128)S(1)}, f32[96,256]{1,0:T(8,128)S(1)}, f32[96,256]{1,0:T(8,128)S(1)}, f32[96,256]{1,0:T(8,128)S(1)}, f32[96,256]{1,0:T(8,128)S(1)}) custom-call(f32[288,128]{1,0:T(8,128)S(1)} %bitcast.26, f32[320,288]{1,0:T(8,128)S(1)} %shard_map.88.inverse_ref, bf16[240,1024]{1,0:T(8,128)(2,1)S(1)} %get-tuple-element.43.extended_ref, ...), custom_call_target="tpu_custom_call" | custom-call | tf_op jit(solution)/shard_map/pallas_call | solution.py:322
  104.8 4.2 %collective-permute-done.21.refs_5_ = f32[96,256]{1,0:T(8,128)S(1)} collective-permute-done((f32[96,256]{1,0:T(8,128)S(1)}, f32[96,256]{1,0:T(8,128)S(1)}, u32[]{:S(2)}, u32[]{:S(2)}) %collective-permute-start.21) | collective-permute-done | bytes 98336 | tf_op jit(solution)/shard_map/ppermute | solution.py:46
  109.5 1.8 %shard_map.99 = (f32[96,1024]{1,0:T(8,128)S(1)}, f32[288,128]{1,0:T(8,128)}) custom-call(s32[1]{0:T(128)} %bitcast.parity_ref, s32[4]{0:T(128)S(1)} %bitcast.40, f32[96,256]{1,0:T(8,128)S(1)} %get-tuple-element.67.refs_0_, f32[96,256]{1,0:T(8,128)S(1)} %get-tuple-element.68.refs_1_, f32[96,256]{1,0:T(8,128)S(1)} %get-tuple-element.69.refs_2_, ...), custom_call_target="tpu_custom_call" | custom-call | tf_op jit(solution)/shard_map/pallas_call | solution.py:322
  111.3 2.6 %all-to-all-start.5 = ((f32[32,9,1,128]{3,2,1,0:T(1,128)}), f32[32,9,1,128]{3,2,1,0:T(1,128)S(1)}, u32[]{:S(2)}, u32[]{:S(2)}) async-start(f32[32,9,1,128]{3,2,1,0:T(1,128)} %bitcast.16), calls=%async_computation.5 | async-start | bytes 294912 | tf_op jit(solution)/shard_map/all_to_all | solution.py:359
  115.0 7.2 %all-to-all-done.5 = f32[32,9,1,128]{3,2,1,0:T(1,128)S(1)} async-done(((f32[32,9,1,128]{3,2,1,0:T(1,128)}), f32[32,9,1,128]{3,2,1,0:T(1,128)S(1)}, u32[]{:S(2)}, u32[]{:S(2)}) %all-to-all-start.5) | async-done | bytes 147488 | tf_op jit(solution)/shard_map/all_to_all | solution.py:359
  122.3 2.1 %shard_map.100 = f32[96,896]{1,0:T(8,128)} custom-call(s32[1]{0:T(128)} %bitcast.parity_ref, f32[288,128]{1,0:T(8,128)S(1)} %bitcast.23, f32[320,288]{1,0:T(8,128)S(1)} %shard_map.88.inverse_ref, bf16[240,1024]{1,0:T(8,128)(2,1)S(1)} %get-tuple-element.43.extended_ref, f32[96,1024]{1,0:T(8,128)S(1)} %get-tuple-element.72.vector_ref, ...), custom_call_target="tpu_custom_call" | custom-call | tf_op jit(solution)/shard_map/pallas_call | solution.py:322
  (84 shorter events, 24.6 us)
Async XLA Ops:
  3.7 13.5 %collective-permute-start = (f32[112,256]{1,0:T(8,128)S(1)}, f32[112,256]{1,0:T(8,128)S(1)}, u32[]{:S(2)}, u32[]{:S(2)}) collective-permute-start(f32[112,256]{1,0:T(8,128)S(1)} %get-tuple-element.38.refs_0_), channel_id=1, source_target_pairs={{0,4},{1,5},{2,6},{3,7},{4,0},{5,1},{6,2},{7,3},{8,12},{9,13},{10,... | collective-permute-start | bytes 344072 | tf_op jit(solution)/shard_map/ppermute | solution.py:46
  4.2 13.0 %collective-permute-start.1 = (f32[112,256]{1,0:T(8,128)S(1)}, f32[112,256]{1,0:T(8,128)S(1)}, u32[]{:S(2)}, u32[]{:S(2)}) collective-permute-start(f32[112,256]{1,0:T(8,128)S(1)} %get-tuple-element.39.refs_1_), channel_id=1, source_target_pairs={{0,28},{1,29},{2,30},{3,31},{4,8},{5,9},{6,10},{7,11},{8,4},{9,5},... | collective-permute-start | bytes 344072 | tf_op jit(solution)/shard_map/ppermute | solution.py:46
  7.7 9.5 %collective-permute-start.2 = (f32[112,256]{1,0:T(8,128)S(1)}, f32[112,256]{1,0:T(8,128)S(1)}, u32[]{:S(2)}, u32[]{:S(2)}) collective-permute-start(f32[112,256]{1,0:T(8,128)S(1)} %get-tuple-element.40.refs_2_), channel_id=1, source_target_pairs={{0,1},{1,2},{2,3},{3,7},{4,0},{5,4},{6,5},{7,6},{8,9},{9,10},{10,1... | collective-permute-start | bytes 344072 | tf_op jit(solution)/shard_map/ppermute | solution.py:46
  9.3 7.9 %collective-permute-start.3 = (f32[112,256]{1,0:T(8,128)S(1)}, f32[112,256]{1,0:T(8,128)S(1)}, u32[]{:S(2)}, u32[]{:S(2)}) collective-permute-start(f32[112,256]{1,0:T(8,128)S(1)} %get-tuple-element.41.refs_3_), channel_id=1, source_target_pairs={{0,4},{1,0},{2,1},{3,2},{4,5},{5,6},{6,7},{7,3},{8,12},{9,8},{10,9... | collective-permute-start | bytes 344072 | tf_op jit(solution)/shard_map/ppermute | solution.py:46
  11.9 11.0 %all-to-all-start.1 = ((f32[4,12,96]{2,1,0:T(8,128)}), f32[4,12,96]{2,1,0:T(8,128)S(1)}, u32[]{:S(2)}, u32[]{:S(2)}) async-start(f32[4,12,96]{2,1,0:T(8,128)} %reshape_squeeze.3), calls=%async_computation.1 | async-start | bytes 65536 | tf_op jit(solution)/shard_map/all_to_all | solution.py:363
  22.9 11.3 %all-to-all-start = ((f32[32,9,1,128]{3,2,1,0:T(1,128)}), f32[32,9,1,128]{3,2,1,0:T(1,128)S(1)}, u32[]{:S(2)}, u32[]{:S(2)}) async-start(f32[32,9,1,128]{3,2,1,0:T(1,128)} %bitcast.5), calls=%async_computation | async-start | bytes 294912 | tf_op jit(solution)/shard_map/all_to_all | solution.py:359
  25.4 7.8 %collective-permute-start.7 = (f32[4,12,96]{2,1,0:T(8,128)S(1)}, f32[4,12,96]{2,1,0:T(8,128)S(1)}, u32[]{:S(2)}, u32[]{:S(2)}) collective-permute-start(f32[4,12,96]{2,1,0:T(8,128)S(1)} %all-to-all-done.1.own_ref), channel_id=1, source_target_pairs={{0,1},{1,2},{2,3},{3,7},{4,0},{5,4},{6,5},{7,6},{8,9},{9,10},{10,1... | collective-permute-start | bytes 55304 | tf_op jit(solution)/shard_map/ppermute | solution.py:46
  27.1 6.1 %collective-permute-start.6 = (f32[4,12,96]{2,1,0:T(8,128)S(1)}, f32[4,12,96]{2,1,0:T(8,128)S(1)}, u32[]{:S(2)}, u32[]{:S(2)}) collective-permute-start(f32[4,12,96]{2,1,0:T(8,128)S(1)} %all-to-all-done.1.own_ref), channel_id=1, source_target_pairs={{0,4},{1,0},{2,1},{3,2},{4,5},{5,6},{6,7},{7,3},{8,12},{9,8},{10,9... | collective-permute-start | bytes 55304 | tf_op jit(solution)/shard_map/ppermute | solution.py:46
  27.2 6.1 %collective-permute-start.5 = (f32[4,12,96]{2,1,0:T(8,128)S(1)}, f32[4,12,96]{2,1,0:T(8,128)S(1)}, u32[]{:S(2)}, u32[]{:S(2)}) collective-permute-start(f32[4,12,96]{2,1,0:T(8,128)S(1)} %all-to-all-done.1.own_ref), channel_id=1, source_target_pairs={{0,28},{1,29},{2,30},{3,31},{4,8},{5,9},{6,10},{7,11},{8,4},{9,5},... | collective-permute-start | bytes 55304 | tf_op jit(solution)/shard_map/ppermute | solution.py:46
  29.2 4.0 %collective-permute-start.4 = (f32[4,12,96]{2,1,0:T(8,128)S(1)}, f32[4,12,96]{2,1,0:T(8,128)S(1)}, u32[]{:S(2)}, u32[]{:S(2)}) collective-permute-start(f32[4,12,96]{2,1,0:T(8,128)S(1)} %all-to-all-done.1.own_ref), channel_id=1, source_target_pairs={{0,4},{1,5},{2,6},{3,7},{4,0},{5,1},{6,2},{7,3},{8,12},{9,13},{10,... | collective-permute-start | bytes 55304 | tf_op jit(solution)/shard_map/ppermute | solution.py:46
  35.2 15.9 %copy-start.16 = (s32[1,1,4,224]{3,2,1,0:T(4,128)S(1)}, s32[1,1,4,224]{3,2,1,0:T(4,128)}, u32[]{:S(2)}) copy-start(s32[1,1,4,224]{3,2,1,0:T(4,128)} %param.13) | copy-start | bytes 10756
  36.7 3.1 %collective-permute-start.8 = (f32[96,256]{1,0:T(8,128)S(1)}, f32[96,256]{1,0:T(8,128)S(1)}, u32[]{:S(2)}, u32[]{:S(2)}) collective-permute-start(f32[96,256]{1,0:T(8,128)S(1)} %get-tuple-element.45.refs_0_), channel_id=1, source_target_pairs={{0,4},{1,5},{2,6},{3,7},{4,0},{5,1},{6,2},{7,3},{8,12},{9,13},{10,... | collective-permute-start | bytes 294920 | tf_op jit(solution)/shard_map/ppermute | solution.py:46
  37.2 5.7 %collective-permute-start.9 = (f32[96,256]{1,0:T(8,128)S(1)}, f32[96,256]{1,0:T(8,128)S(1)}, u32[]{:S(2)}, u32[]{:S(2)}) collective-permute-start(f32[96,256]{1,0:T(8,128)S(1)} %get-tuple-element.46.refs_1_), channel_id=1, source_target_pairs={{0,28},{1,29},{2,30},{3,31},{4,8},{5,9},{6,10},{7,11},{8,4},{9,5},... | collective-permute-start | bytes 294920 | tf_op jit(solution)/shard_map/ppermute | solution.py:46
  37.8 5.2 %collective-permute-start.10 = (f32[96,256]{1,0:T(8,128)S(1)}, f32[96,256]{1,0:T(8,128)S(1)}, u32[]{:S(2)}, u32[]{:S(2)}) collective-permute-start(f32[96,256]{1,0:T(8,128)S(1)} %get-tuple-element.47.refs_2_), channel_id=1, source_target_pairs={{0,1},{1,2},{2,3},{3,7},{4,0},{5,4},{6,5},{7,6},{8,9},{9,10},{10,1... | collective-permute-start | bytes 294920 | tf_op jit(solution)/shard_map/ppermute | solution.py:46
  39.8 4.6 %collective-permute-start.11 = (f32[96,256]{1,0:T(8,128)S(1)}, f32[96,256]{1,0:T(8,128)S(1)}, u32[]{:S(2)}, u32[]{:S(2)}) collective-permute-start(f32[96,256]{1,0:T(8,128)S(1)} %get-tuple-element.48.refs_3_), channel_id=1, source_target_pairs={{0,4},{1,0},{2,1},{3,2},{4,5},{5,6},{6,7},{7,3},{8,12},{9,8},{10,9... | collective-permute-start | bytes 294920 | tf_op jit(solution)/shard_map/ppermute | solution.py:46
  47.0 12.5 %all-to-all-start.2 = ((f32[32,9,1,128]{3,2,1,0:T(1,128)}), f32[32,9,1,128]{3,2,1,0:T(1,128)S(1)}, u32[]{:S(2)}, u32[]{:S(2)}) async-start(f32[32,9,1,128]{3,2,1,0:T(1,128)} %bitcast.8), calls=%async_computation.2 | async-start | bytes 294912 | tf_op jit(solution)/shard_map/all_to_all | solution.py:359
  62.1 19.7 %copy-start.12 = (f32[96,1024]{1,0:T(8,128)S(1)}, f32[96,1024]{1,0:T(8,128)}, u32[]{:S(2)}) copy-start(f32[96,1024]{1,0:T(8,128)} %copy-done.11) | copy-start | bytes 1179652
  63.5 1.8 %collective-permute-start.12 = (f32[96,256]{1,0:T(8,128)S(1)}, f32[96,256]{1,0:T(8,128)S(1)}, u32[]{:S(2)}, u32[]{:S(2)}) collective-permute-start(f32[96,256]{1,0:T(8,128)S(1)} %get-tuple-element.52.refs_0_), channel_id=1, source_target_pairs={{0,4},{1,5},{2,6},{3,7},{4,0},{5,1},{6,2},{7,3},{8,12},{9,13},{10,... | collective-permute-start | bytes 294920 | tf_op jit(solution)/shard_map/ppermute | solution.py:46
  63.9 5.6 %collective-permute-start.13 = (f32[96,256]{1,0:T(8,128)S(1)}, f32[96,256]{1,0:T(8,128)S(1)}, u32[]{:S(2)}, u32[]{:S(2)}) collective-permute-start(f32[96,256]{1,0:T(8,128)S(1)} %get-tuple-element.53.refs_1_), channel_id=1, source_target_pairs={{0,28},{1,29},{2,30},{3,31},{4,8},{5,9},{6,10},{7,11},{8,4},{9,5},... | collective-permute-start | bytes 294920 | tf_op jit(solution)/shard_map/ppermute | solution.py:46
  64.7 4.9 %collective-permute-start.14 = (f32[96,256]{1,0:T(8,128)S(1)}, f32[96,256]{1,0:T(8,128)S(1)}, u32[]{:S(2)}, u32[]{:S(2)}) collective-permute-start(f32[96,256]{1,0:T(8,128)S(1)} %get-tuple-element.54.refs_2_), channel_id=1, source_target_pairs={{0,1},{1,2},{2,3},{3,7},{4,0},{5,4},{6,5},{7,6},{8,9},{9,10},{10,1... | collective-permute-start | bytes 294920 | tf_op jit(solution)/shard_map/ppermute | solution.py:46
  65.4 4.6 %collective-permute-start.15 = (f32[96,256]{1,0:T(8,128)S(1)}, f32[96,256]{1,0:T(8,128)S(1)}, u32[]{:S(2)}, u32[]{:S(2)}) collective-permute-start(f32[96,256]{1,0:T(8,128)S(1)} %get-tuple-element.55.refs_3_), channel_id=1, source_target_pairs={{0,4},{1,0},{2,1},{3,2},{4,5},{5,6},{6,7},{7,3},{8,12},{9,8},{10,9... | collective-permute-start | bytes 294920 | tf_op jit(solution)/shard_map/ppermute | solution.py:46
  81.8 19.7 %copy-start.2 = (bf16[1024,1024]{1,0:T(8,128)(2,1)S(1)}, bf16[1024,1024]{1,0:T(8,128)(2,1)}, u32[]{:S(2)}) copy-start(bf16[1024,1024]{1,0:T(8,128)(2,1)} %copy-done) | copy-start | bytes 6291460
  83.3 1.8 %collective-permute-start.16 = (f32[96,256]{1,0:T(8,128)S(1)}, f32[96,256]{1,0:T(8,128)S(1)}, u32[]{:S(2)}, u32[]{:S(2)}) collective-permute-start(f32[96,256]{1,0:T(8,128)S(1)} %get-tuple-element.59.refs_0_), channel_id=1, source_target_pairs={{0,4},{1,5},{2,6},{3,7},{4,0},{5,1},{6,2},{7,3},{8,12},{9,13},{10,... | collective-permute-start | bytes 294920 | tf_op jit(solution)/shard_map/ppermute | solution.py:46
  83.6 5.6 %collective-permute-start.17 = (f32[96,256]{1,0:T(8,128)S(1)}, f32[96,256]{1,0:T(8,128)S(1)}, u32[]{:S(2)}, u32[]{:S(2)}) collective-permute-start(f32[96,256]{1,0:T(8,128)S(1)} %get-tuple-element.60.refs_1_), channel_id=1, source_target_pairs={{0,28},{1,29},{2,30},{3,31},{4,8},{5,9},{6,10},{7,11},{8,4},{9,5},... | collective-permute-start | bytes 294920 | tf_op jit(solution)/shard_map/ppermute | solution.py:46
  84.4 4.9 %collective-permute-start.18 = (f32[96,256]{1,0:T(8,128)S(1)}, f32[96,256]{1,0:T(8,128)S(1)}, u32[]{:S(2)}, u32[]{:S(2)}) collective-permute-start(f32[96,256]{1,0:T(8,128)S(1)} %get-tuple-element.61.refs_2_), channel_id=1, source_target_pairs={{0,1},{1,2},{2,3},{3,7},{4,0},{5,4},{6,5},{7,6},{8,9},{9,10},{10,1... | collective-permute-start | bytes 294920 | tf_op jit(solution)/shard_map/ppermute | solution.py:46
  85.1 4.6 %collective-permute-start.19 = (f32[96,256]{1,0:T(8,128)S(1)}, f32[96,256]{1,0:T(8,128)S(1)}, u32[]{:S(2)}, u32[]{:S(2)}) collective-permute-start(f32[96,256]{1,0:T(8,128)S(1)} %get-tuple-element.62.refs_3_), channel_id=1, source_target_pairs={{0,4},{1,0},{2,1},{3,2},{4,5},{5,6},{6,7},{7,3},{8,12},{9,8},{10,9... | collective-permute-start | bytes 294920 | tf_op jit(solution)/shard_map/ppermute | solution.py:46
  101.5 20.7 %copy-start.6 = (f32[96,1024]{1,0:T(8,128)S(1)}, f32[96,1024]{1,0:T(8,128)}, u32[]{:S(2)}) copy-start(f32[96,1024]{1,0:T(8,128)} %copy-done.5) | copy-start | bytes 1179652
  103.0 1.8 %collective-permute-start.20 = (f32[96,256]{1,0:T(8,128)S(1)}, f32[96,256]{1,0:T(8,128)S(1)}, u32[]{:S(2)}, u32[]{:S(2)}) collective-permute-start(f32[96,256]{1,0:T(8,128)S(1)} %get-tuple-element.67.refs_0_), channel_id=1, source_target_pairs={{0,4},{1,5},{2,6},{3,7},{4,0},{5,1},{6,2},{7,3},{8,12},{9,13},{10,... | collective-permute-start | bytes 294920 | tf_op jit(solution)/shard_map/ppermute | solution.py:46
  103.4 5.6 %collective-permute-start.21 = (f32[96,256]{1,0:T(8,128)S(1)}, f32[96,256]{1,0:T(8,128)S(1)}, u32[]{:S(2)}, u32[]{:S(2)}) collective-permute-start(f32[96,256]{1,0:T(8,128)S(1)} %get-tuple-element.68.refs_1_), channel_id=1, source_target_pairs={{0,28},{1,29},{2,30},{3,31},{4,8},{5,9},{6,10},{7,11},{8,4},{9,5},... | collective-permute-start | bytes 294920 | tf_op jit(solution)/shard_map/ppermute | solution.py:46
  104.1 4.9 %collective-permute-start.22 = (f32[96,256]{1,0:T(8,128)S(1)}, f32[96,256]{1,0:T(8,128)S(1)}, u32[]{:S(2)}, u32[]{:S(2)}) collective-permute-start(f32[96,256]{1,0:T(8,128)S(1)} %get-tuple-element.69.refs_2_), channel_id=1, source_target_pairs={{0,1},{1,2},{2,3},{3,7},{4,0},{5,4},{6,5},{7,6},{8,9},{9,10},{10,1... | collective-permute-start | bytes 294920 | tf_op jit(solution)/shard_map/ppermute | solution.py:46
  104.8 4.6 %collective-permute-start.23 = (f32[96,256]{1,0:T(8,128)S(1)}, f32[96,256]{1,0:T(8,128)S(1)}, u32[]{:S(2)}, u32[]{:S(2)}) collective-permute-start(f32[96,256]{1,0:T(8,128)S(1)} %get-tuple-element.70.refs_3_), channel_id=1, source_target_pairs={{0,4},{1,0},{2,1},{3,2},{4,5},{5,6},{6,7},{7,3},{8,12},{9,8},{10,9... | collective-permute-start | bytes 294920 | tf_op jit(solution)/shard_map/ppermute | solution.py:46
  111.3 11.0 %all-to-all-start.5 = ((f32[32,9,1,128]{3,2,1,0:T(1,128)}), f32[32,9,1,128]{3,2,1,0:T(1,128)S(1)}, u32[]{:S(2)}, u32[]{:S(2)}) async-start(f32[32,9,1,128]{3,2,1,0:T(1,128)} %bitcast.16), calls=%async_computation.5 | async-start | bytes 294912 | tf_op jit(solution)/shard_map/all_to_all | solution.py:359
  (16 other events, 41.4 us)

commit v2 on v1

v2 whole, which is shorter than its diff:
```python
import functools

import jax
import jax.numpy as jnp
from jax import lax
from jax.experimental import pallas as pl
from jax.experimental.pallas import tpu as pltpu
from jax.sharding import PartitionSpec as P

f32 = jnp.float32
bf16 = jnp.bfloat16
precise = lax.Precision.HIGHEST
spectrum_low = 0.5
spectrum_high = 4.0

EVEN_FACES = (1, 0, 3, 2)
ODD_FACES = (0, 1, 2, 3)
ARRIVES = (0, 1, 3, 2)
REORDERED = (0, 2)


def round_up(value, unit):
    return -(-value // unit) * unit


def exchanges(rows, cols):
    def pairs(target):
        return [
            (a * cols + b, target(a, b)[0] * cols + target(a, b)[1])
            for a in range(rows)
            for b in range(cols)
        ]

    def along(a, b, step):
        return (a, b + step) if 0 <= b + step < cols else (a ^ 1, b)

    return (
        pairs(lambda a, b: (a ^ 1, b)),
        pairs(lambda a, b: ((a + 1 if a % 2 else a - 1) % rows, b)),
        pairs(lambda a, b: along(a, b, -1 if a % 2 else 1)),
        pairs(lambda a, b: along(a, b, 1 if a % 2 else -1)),
    )


def exchange(values, lists):
    return [lax.ppermute(value, ("gx", "gy"), pairs) for value, pairs in zip(values, lists)]


def chebyshev_coefficients():
    center = (spectrum_high + spectrum_low) / 2.0
    radius = (spectrum_high - spectrum_low) / 2.0
    center_ratio = center / radius
    factor_prev = 1.0 / center_ratio
    result = [(1.0 / center, 0.0)]
    factor = 1.0 / (2.0 * center_ratio - factor_prev)
    result.append((2.0 * factor / radius, factor * factor_prev))
    return result


def split3(value):
    high = value.astype(bf16)
    rest = value - high.astype(f32)
    middle = rest.astype(bf16)
    low = (rest - middle.astype(f32)).astype(bf16)
    return high, middle, low


def contract(left, right, left_dim, right_dim, precision=None):
    return lax.dot_general(
        left,
        right,
        (((left_dim,), (right_dim,)), ((), ())),
        precision=precision,
        preferred_element_type=f32,
    )


def by_parity(parity, even, odd):
    return jnp.where(parity == 0, even, odd)


def face_columns(value, slot, parity, width):
    even, odd = EVEN_FACES[slot], ODD_FACES[slot]
    return by_parity(
        parity,
        value[:, even * width : (even + 1) * width],
        value[:, odd * width : (odd + 1) * width],
    )


def reorder_matrix(partners, slot, parity, width, padded):
    plain = lax.broadcasted_iota(jnp.int32, (1, width), 1)

    def places(face):
        return partners[face : face + 1, :] if face in REORDERED else plain

    place = by_parity(parity, places(EVEN_FACES[slot]), places(ODD_FACES[slot]))
    rows = lax.broadcasted_iota(jnp.int32, (padded, width), 0)
    return jnp.where(rows == place, 1.0, 0.0).astype(bf16)


def reorder_exact(value, matrix, dim):
    count = value.shape[0]
    parts = contract(jnp.concatenate(split3(value), axis=0), matrix, 1, dim)
    return parts[:count] + (parts[count : 2 * count] + parts[2 * count :])


def row_parity():
    return lax.rem(lax.axis_index("gx"), 2)


def pack_counts(count):
    long = count * 3 // 4
    return long, count - long


def pack_coefficients(coeffs, count):
    long, short = pack_counts(count)
    pieces = long // short
    piece = coeffs.shape[1] // pieces
    tail = coeffs[long:count]
    side = jnp.concatenate([tail[:, i * piece : (i + 1) * piece] for i in range(pieces)], axis=0)
    return jnp.concatenate([coeffs[:long], side], axis=1)


def write_copies(out_ref, value):
    height = value.shape[0]
    copies = out_ref.shape[0] // height
    together = 8 if copies % 8 == 0 else 1
    block = jnp.concatenate([value] * together, axis=0)
    for i in range(copies // together):
        out_ref[i * together * height : (i + 1) * together * height, :] = block


def inverse_places(index, group, length, padded):
    block = round_up(length, 128)
    beside = max(padded // block, 1)
    below = -(-length // padded)
    return [
        (
            ((index // beside) * below + part) * group,
            (index % beside) * block,
            slice(part * padded, min(length, (part + 1) * padded)),
        )
        for part in range(below)
    ]


def inverse_lines(cols, group, length, padded):
    return max(
        place[0] + group
        for index in range(cols)
        for place in inverse_places(index, group, length, padded)
    )


def load_kernel(
    load_hbm, modes_hbm, partners_hbm, counts_hbm,
    face_0, face_1, face_2, face_3, live_ref, reorder_ref,
    load_ref, modes_ref, partners_ref, counts_ref, sems,
):
    copies = [
        pltpu.make_async_copy(source, target, sems.at[i])
        for i, (source, target) in enumerate(
            (
                (load_hbm.at[0, 0], load_ref),
                (modes_hbm.at[0, 0], modes_ref),
                (partners_hbm.at[0, 0], partners_ref),
                (counts_hbm.at[0], counts_ref),
            )
        )
    ]
    for copy in copies:
        copy.start()
    for copy in copies:
        copy.wait()
    parity = row_parity()
    width = partners_ref.shape[1]
    columns, count = load_ref.shape[0], modes_ref.shape[0]
    padded = face_0.shape[1]
    for slot, face_ref in enumerate((face_0, face_1, face_2, face_3)):
        matrix = reorder_matrix(partners_ref[...], slot, parity, width, padded)
        reorder_ref[slot] = matrix
        values = face_columns(load_ref[...], slot, parity, width)
        modes = face_columns(modes_ref[...], slot, parity, width)
        face_ref[columns:, :] = jnp.zeros((face_ref.shape[0] - columns, padded), f32)
        face_ref[:columns, :] = reorder_exact(values, matrix, 1)
        face_ref[columns : columns + count, :] = contract(modes, matrix, 1, 1)
        live = by_parity(
            parity, counts_ref[0, EVEN_FACES[slot]], counts_ref[0, ODD_FACES[slot]]
        )
        places = lax.broadcasted_iota(jnp.int32, (live_ref.shape[0], padded), 1)
        live_ref[:, slot * padded : (slot + 1) * padded] = jnp.where(places < live, 1.0, 0.0)


def matrix_kernel(matrix_hbm, reorder_ref, after_hbm, out_ref, matrix_ref, sems):
    width = matrix_ref.shape[0] // 4
    copies = [
        pltpu.make_async_copy(
            matrix_hbm.at[0, 0, pl.ds(face * width, width)],
            matrix_ref.at[pl.ds(face * width, width)],
            sems.at[face],
        )
        for face in range(4)
    ]
    for copy in copies:
        copy.start()
    parity = row_parity()
    padded = out_ref.shape[1] // 4
    for face, copy in enumerate(copies):
        copy.wait()
        rows = matrix_ref[face * width : (face + 1) * width, :]
        row_slot = by_parity(parity, EVEN_FACES.index(face), ODD_FACES.index(face))
        place = pl.ds(pl.multiple_of(row_slot * padded, padded), padded)
        for slot in range(4):
            block = face_columns(rows, slot, parity, width)
            block = contract(block, reorder_ref[slot], 1, 1).astype(bf16)
            out_ref[place, slot * padded : (slot + 1) * padded] = contract(
                reorder_ref[row_slot], block, 1, 0
            ).astype(bf16)


def rows_kernel(count, base, *refs):
    part_refs, (first_ref, second_ref, rows_ref) = refs[2:-3], refs[-3:]
    cols, here = len(part_refs), lax.axis_index("gy")
    group, length = rows_ref.shape[1:]
    rows_ref[...] = jnp.zeros(rows_ref.shape, f32)
    for step, part_ref in enumerate(part_refs):
        source = lax.rem(here + cols - step, cols)
        rows_ref[source, :count, :] = part_ref[0, pl.ds(here * count, count), 0, :]
    for face_ref in (first_ref, second_ref):
        for e in range(cols):
            for line, lane, part in inverse_places(e, group, length, face_ref.shape[1]):
                face_ref[
                    base + line : base + line + group, lane : lane + part.stop - part.start
                ] = rows_ref[e, :, part]


def inverse_kernel(count, base, *refs):
    face_refs = refs[:3]
    part_refs, (out_ref, rows_ref) = refs[3:-3], refs[-2:]
    cols = len(part_refs)
    parity, here = row_parity(), lax.axis_index("gy")
    north, south = jnp.minimum(here + 1, cols - 1), jnp.maximum(here - 1, 0)
    length = rows_ref.shape[2]
    group = round_up(count, 8)
    rows, height = length // count, rows_ref.shape[1]
    long, short = pack_counts(count)
    rows_ref[...] = jnp.zeros(rows_ref.shape, f32)
    for e in range(cols):
        for i, ref in enumerate(face_refs):
            for line, lane, part in inverse_places(e, group, length, ref.shape[1]):
                rows_ref[e, i * count : (i + 1) * count, part] = ref[
                    base + line : base + line + count, lane : lane + part.stop - part.start
                ]
    for step, part_ref in enumerate(part_refs):
        source_col = lax.rem(here + cols - step, cols)
        for i, row in ((3, jnp.where(parity == 0, north, south)), (4, jnp.where(parity == 0, south, north))):
            rows_ref[source_col, i * count : (i + 1) * count, :] = part_ref[
                0, pl.ds(row * count, count), 0, :
            ]
    wide = rows * long
    source = lax.broadcasted_iota(jnp.int32, (length, wide), 0)
    target = lax.broadcasted_iota(jnp.int32, (length, wide), 1)
    source_row, source_mode = lax.div(source, count), lax.rem(source, count)
    target_row, target_place = lax.div(target, long), lax.rem(target, long)
    same = source_row == target_row
    places = [jnp.where(same & (source_mode == target_place), 1.0, 0.0).astype(bf16)]
    for part in range(long // short):
        wanted = target_place - part * short
        inside = (wanted >= 0) & (wanted < short)
        places.append(
            jnp.where(same & inside & (source_mode == long + wanted), 1.0, 0.0).astype(bf16)
        )
    everything = cols * wide
    gathered = [[] for _ in places]
    for e in range(cols):
        high, middle, _ = split3(rows_ref[e])
        halves = jnp.concatenate([high, middle], axis=0)
        for part, place in enumerate(places):
            gathered[part].append(contract(halves, place, 1, 0))
    for part, pieces in enumerate(gathered):
        both = jnp.concatenate(pieces, axis=1).astype(bf16)
        place = slice(part * height, (part + 1) * height)
        out_ref[place, :] = jnp.concatenate([both[:height], both[:height], both[height:]], axis=1)


def coefficients(vector, columns_ref, count):
    high, middle, _ = split3(vector)
    terms = jnp.dot(
        jnp.concatenate([high, middle], axis=0), columns_ref[...], preferred_element_type=f32
    )
    columns = vector.shape[0]
    coeffs = (terms[:columns] + terms[columns:]).T
    return pack_coefficients(coeffs, count)


def join_faces(sent, arrived, live_ref, vector_ref):
    columns, padded = vector_ref.shape[0], sent[0].shape[1]
    for slot in range(4):
        place = slice(slot * padded, (slot + 1) * padded)
        own, other = sent[slot], arrived[ARRIVES.index(slot)]
        total = own[:columns, :] + other[:columns, :]
        vector_ref[:, place] = jnp.where(live_ref[:1, place] > 0.0, total, 0.0)


def first_join_kernel(count, *refs):
    sent, arrived, live_ref = refs[:4], refs[4:8], refs[8]
    vector_ref, coeff_ref, columns_ref, extended_ref, rows_ref = refs[-5:]
    columns, padded = vector_ref.shape[0], sent[0].shape[1]
    group = sent[3].shape[0] - columns
    half = rows_ref.shape[0]
    join_faces(sent, arrived, live_ref, vector_ref)
    rows_ref[...] = jnp.zeros(rows_ref.shape, f32)
    blank = jnp.zeros((columns_ref.shape[1] - group, padded), f32)
    for slot in range(4):
        place = slice(slot * padded, (slot + 1) * padded)
        live = live_ref[:1, place]
        own = sent[slot][columns : columns + group, :] * live
        other = arrived[ARRIVES.index(slot)][columns : columns + group, :] * live
        columns_ref[place, :] = jnp.concatenate([own, blank], axis=0).T.astype(bf16)
        rows_ref[:count, place] = own[:count]
        rows_ref[(1 + slot) * count : (2 + slot) * count, place] = other[:count]
    extended = rows_ref[...].astype(bf16)
    extended_ref[:half, :] = extended
    extended_ref[half:, :] = extended
    write_copies(coeff_ref, coefficients(vector_ref[...], columns_ref, count))


def join_kernel(count, *refs):
    sent, arrived, live_ref, columns_ref = refs[:4], refs[4:8], refs[8], refs[9]
    vector_ref, coeff_ref = refs[-2:]
    join_faces(sent, arrived, live_ref, vector_ref)
    write_copies(coeff_ref, coefficients(vector_ref[...], columns_ref, count))


def projected(coeff_ref, inverse_ref, extended_ref, vector_ref):
    columns, height = vector_ref.shape[0], extended_ref.shape[0] // 2
    high, middle, _ = split3(coeff_ref[...])
    terms = contract(inverse_ref[...], jnp.concatenate([high, middle, high], axis=0), 1, 0)
    solved = terms[:height, :columns] + jnp.concatenate(
        [
            terms[i * height : (i + 1) * height, columns:]
            for i in range(1, terms.shape[0] // height)
        ],
        axis=1,
    )
    high, middle, _ = split3(solved)
    parts = jnp.concatenate([high, middle], axis=0)
    return vector_ref[...] - contract(parts, extended_ref[...], 0, 0)


def apply_matrix(vector, matrix_ref, face_refs):
    rounded = vector.astype(bf16)
    padded = matrix_ref.shape[1] // 4
    for slot, face_ref in enumerate(face_refs):
        face_ref[...] = contract(
            rounded, matrix_ref[:, slot * padded : (slot + 1) * padded], 1, 0
        )


def start_kernel(coeff_ref, inverse_ref, extended_ref, vector_ref, matrix_ref, *refs):
    residual_ref, face_refs = refs[0], refs[1:]
    residual = projected(coeff_ref, inverse_ref, extended_ref, vector_ref)
    residual_ref[...] = residual
    apply_matrix(residual, matrix_ref, face_refs)


def residual_kernel(coeff_ref, inverse_ref, extended_ref, vector_ref, matrix_ref, old_ref, *refs):
    residual_ref, face_refs = refs[0], refs[1:]
    residual = old_ref[...] - projected(coeff_ref, inverse_ref, extended_ref, vector_ref)
    residual_ref[...] = residual
    apply_matrix(residual, matrix_ref, face_refs)


def first_direction_kernel(alpha, coeff_ref, inverse_ref, extended_ref, vector_ref, matrix_ref, *refs):
    direction_ref, face_refs = refs[0], refs[1:]
    direction = alpha * projected(coeff_ref, inverse_ref, extended_ref, vector_ref)
    direction_ref[...] = direction
    apply_matrix(direction, matrix_ref, face_refs)


def direction_kernel(
    alpha, beta, coeff_ref, inverse_ref, extended_ref, vector_ref, matrix_ref, old_ref, *refs
):
    multipliers_ref, face_refs = refs[0], refs[1:]
    old = old_ref[...]
    preconditioned = projected(coeff_ref, inverse_ref, extended_ref, vector_ref)
    direction = alpha * preconditioned + beta * old
    multipliers_ref[...] = old + direction
    apply_matrix(direction, matrix_ref, face_refs)


def face_order(value, reorder_ref):
    parity = row_parity()
    padded = value.shape[1] // 4
    slots = [
        reorder_exact(value[:, slot * padded : (slot + 1) * padded], reorder_ref[slot], 0)
        for slot in range(4)
    ]
    return jnp.concatenate(
        [
            by_parity(parity, slots[EVEN_FACES.index(face)], slots[ODD_FACES.index(face)])
            for face in range(4)
        ],
        axis=1,
    )


def last_kernel(coeff_ref, inverse_ref, extended_ref, vector_ref, old_ref, reorder_ref, out_ref):
    residual = old_ref[...] - projected(coeff_ref, inverse_ref, extended_ref, vector_ref)
    out_ref[...] = face_order(residual, reorder_ref)


def multipliers_kernel(vector_ref, reorder_ref, out_ref):
    out_ref[...] = face_order(vector_ref[...], reorder_ref)


def call(kernel, outs, args, hbm=(), after=(), scratch=(), aliases={}):
    vmem = pl.BlockSpec(memory_space=pltpu.VMEM)
    outside = pl.BlockSpec(memory_space=pltpu.HBM)
    anywhere = pl.BlockSpec(memory_space=pl.ANY)
    size = sum(o.size * o.dtype.itemsize for o in (*outs, *args))
    args = [
        pltpu.with_memory_space_constraint(arg, pltpu.HBM) if i in hbm else arg
        for i, arg in enumerate(args)
    ]
    return pl.pallas_call(
        kernel,
        out_shape=tuple(outs),
        in_specs=[
            outside if i in hbm else anywhere if i in after else vmem for i in range(len(args))
        ],
        out_specs=tuple([vmem] * len(outs)),
        scratch_shapes=list(scratch),
        input_output_aliases=aliases,
        compiler_params=pltpu.CompilerParams(vmem_limit_bytes=min(size + (8 << 20), 56 << 20)),
    )(*args)


def local(rows, cols, load, dual_operator, dirichlet, modes, coarse_inverse, face_counts, partners):
    devices = rows * cols
    columns, slots = load.shape[2:]
    width = partners.shape[3]
    padded = round_up(width, 128)
    count = modes.shape[2]
    group = round_up(count, 8)
    height = round_up(5 * count, 16)
    long, short = pack_counts(count)
    packed = columns + columns // (long // short)
    lists = exchanges(rows, cols)
    shape = jax.ShapeDtypeStruct
    vector = shape((columns, 4 * padded), f32)
    faces = [shape((columns, padded), f32)] * 4
    base = columns + group
    lines = inverse_lines(cols, group, rows * count, padded)
    tall_faces = [shape((base + extra, padded), f32) for extra in (lines, lines, 0, 0)]
    matrix = shape((4 * padded, 4 * padded), bf16)
    coeff = shape((devices * long, packed), f32)
    result = shape((columns, slots), f32)
    (alpha_0, _), (alpha_1, beta_1) = chebyshev_coefficients()

    def everywhere(values):
        chunks = values.reshape(devices, long, 1, packed)
        return lax.all_to_all(chunks, ("gy", "gx"), 0, 0).reshape(devices * long, packed)

    def reordered(values, after):
        return call(
            matrix_kernel,
            [matrix],
            (values, reorder, after),
            (0,),
            (2,),
            [pltpu.VMEM((slots, slots), bf16), pltpu.SemaphoreType.DMA((4,))],
        )[0]

    parts = [coarse_inverse] + [
        lax.ppermute(coarse_inverse, "gy", [(b, (b + step) % cols) for b in range(cols)])
        for step in range(1, cols)
    ]
    *sent, live, reorder = call(
        load_kernel,
        [
            *tall_faces,
            shape((8, 4 * padded), f32),
            shape((4, padded, width), bf16),
        ],
        (load, modes, partners, face_counts),
        (0, 1, 2, 3),
        (),
        [
            pltpu.VMEM((columns, slots), f32),
            pltpu.VMEM((count, slots), bf16),
            pltpu.VMEM((4, width), jnp.int32),
            pltpu.SMEM((1, 4), jnp.int32),
            pltpu.SemaphoreType.DMA((4,)),
        ],
    )
    sent[:2] = call(
        functools.partial(rows_kernel, count, base),
        tall_faces[:2],
        (*sent[:2], *parts),
        scratch=[pltpu.VMEM((cols, group, rows * count), f32)],
        aliases={0: 0, 1: 1},
    )
    arrived = exchange(sent, lists)
    smoother = reordered(dirichlet, sent[0])
    (inverse,) = call(
        functools.partial(inverse_kernel, count, base),
        [shape(((1 + long // short) * height, 3 * devices * long), bf16)],
        (sent[0], *arrived[:2], *parts, smoother),
        (),
        (3 + cols,),
        [pltpu.VMEM((cols, height, rows * count), f32)],
    )
    current, coeffs, mode_columns, extended = call(
        functools.partial(first_join_kernel, count),
        [vector, coeff, shape((4 * padded, 128), bf16), shape((2 * height, 4 * padded), bf16)],
        (*sent, *arrived, live, inverse),
        (),
        (9,),
        [pltpu.VMEM((height, 4 * padded), f32)],
    )

    def join(sent, *before, last=False):
        arrived = exchange(sent, lists)
        current, coeffs = call(
            functools.partial(join_kernel, count),
            [vector, coeff],
            (*sent, *arrived, live, mode_columns, *before),
            (10,) if last else (),
            (10,),
        )
        return everywhere(coeffs), inverse, extended, current

    residual, *sent = call(
        start_kernel,
        [vector, *faces],
        (everywhere(coeffs), inverse, extended, current, smoother),
    )
    operator = reordered(dual_operator, sent[0])
    direction, *sent = call(
        functools.partial(first_direction_kernel, alpha_0),
        [vector, *faces],
        (*join(sent, operator), operator),
    )
    residual, *sent = call(
        residual_kernel, [vector, *faces], (*join(sent), smoother, residual)
    )
    multipliers, *sent = call(
        functools.partial(direction_kernel, alpha_1, beta_1),
        [vector, *faces],
        (*join(sent), operator, direction),
    )
    (multipliers,) = call(multipliers_kernel, [result], (multipliers, reorder))
    (residual,) = call(
        last_kernel, [result], (*join(sent, multipliers, last=True), residual, reorder)
    )
    return (multipliers[None, None], residual[None, None])


def solution(mesh):
    return jax.shard_map(
        functools.partial(local, mesh.shape["gx"], mesh.shape["gy"]),
        mesh=mesh,
        in_specs=(
            P("gx", "gy", None, None),
            P("gx", "gy", None, None),
            P("gx", "gy", None, None),
            P("gx", "gy", None, None),
            P("gx", None, "gy", None),
            P("gx", "gy", None),
            P("gx", "gy", None, None),
        ),
        out_specs=(P("gx", "gy", None, None), P("gx", "gy", None, None)),
        check_vma=False,
    )
```

time: 125 us -> 108 us (0.86)
  blocking collectives: 21.3 us -> 54.5 us
  starting transfers between devices: 32.6 us -> 15.9 us
  waiting for transfers between devices: 31.8 us -> 16.9 us
  local copies, waits for them, and re-layouts: 14.2 us -> 0.74 us
  Pallas kernels: 22.1 us -> 19 us
  other arithmetic: 1.45 us -> 0 us
    all_to_all x2 -> x5, blocking collectives: 21.3 us -> 54.5 us  [everywhere(): lax.all_to_all(chunks, ('gy', 'gx'), 0, 0).reshape(devices * long, packed)]
    all_to_all x4 -> x0, starting transfers between devices: 14.5 us -> none  [the longest x3 9.19 us: everywhere(): lax.all_to_all(chunks, ('gy', 'gx'), 0, 0).reshape(devices * long, packed)]
    all_to_all x4 -> x0, waiting for transfers between devices: 13.4 us -> none  [the longest x3 11 us: everywhere(): lax.all_to_all(chunks, ('gy', 'gx'), 0, 0).reshape(devices * long, packed)]
    unnamed x41 -> x4, local copies, waits for them, and re-layouts: 13.6 us -> 0.74 us
    ppermute x24 -> x20, starting transfers between devices: 18.1 us -> 9.77 us  [exchange(): lax.ppermute(value, ('gx', 'gy'), pairs)]
    ppermute x0 -> x3, starting transfers between devices: none -> 6.12 us  [local(): lax.ppermute(coarse_inverse, 'gy', [(b, (b + step) % cols) for b in range...]
    ppermute x24 -> x20, waiting for transfers between devices: 18.5 us -> 13.7 us  [exchange(): lax.ppermute(value, ('gx', 'gy'), pairs)]
    ppermute x0 -> x3, waiting for transfers between devices: none -> 3.17 us  [local(): lax.ppermute(coarse_inverse, 'gy', [(b, (b + step) % cols) for b in range...]
  transfers between devices with their start and end apart: 28 -> 23, of which waited for: 11 -> 9; matrix products, arithmetic and copies ran while one was open for 2% -> 0% of each run, Pallas kernels for 6% -> 10%
where the time goes in v2:
time: 108 us
  blocking collectives  54.5 us (50%)
  Pallas kernels  19 us (18%)
  waiting for transfers between devices  16.9 us (16%)
  starting transfers between devices  15.9 us (15%)
    all_to_all x5, blocking collectives, everywhere(): lax.all_to_all(chunks, ('gy', 'gx'), 0, 0).reshape(devices * long, packed)  54.5 us
    pallas_call x16, Pallas kernels, call(): pl.pallas_call(kernel, out_shape=tuple(outs), in_specs=[outside if i in h...  19 us
    ppermute x20, waiting for transfers between devices, exchange(): lax.ppermute(value, ('gx', 'gy'), pairs)  13.7 us
    ppermute x20, starting transfers between devices, exchange(): lax.ppermute(value, ('gx', 'gy'), pairs)  9.77 us
    ppermute x3, starting transfers between devices, local(): lax.ppermute(coarse_inverse, 'gy', [(b, (b + step) % cols) for b in range...  6.12 us
    ppermute x3, waiting for transfers between devices, local(): lax.ppermute(coarse_inverse, 'gy', [(b, (b + step) % cols) for b in range...  3.17 us
  transfers between devices with their start and end apart: 23, of which 9 were waited for; matrix products, arithmetic and copies ran while one was open for 0% of the time, Pallas kernels for 10%

profile of v2, /device:TPU:0, one launch (start us, length us, event | category | flops | bytes accessed | tf_op | source)
XLA Modules:
  0.0 107.8 jit_solution(7318640956928235814)
XLA Ops:
  0.6 5.1 %collective-permute-start.2 = (f32[1,48,1,96]{3,2,1,0:T(1,128)}, f32[1,48,1,96]{3,2,1,0:T(1,128)S(1)}, u32[]{:S(2)}, u32[]{:S(2)}) collective-permute-start(f32[1,48,1,96]{3,2,1,0:T(1,128)} %refs_3_.1), channel_id=1, source_target_pairs={{0,3},{1,0},{2,1},{3,2},{4,7},{5,4},{6,5},{7,6},{8,11},{9,8},{10,9... | collective-permute-start | bytes 55304 | tf_op jit(solution)/shard_map/ppermute | solution.py:478
  5.7 1.0 collective-permute-start
  6.7 1.6 %shard_map.86 = (f32[144,256]{1,0:T(8,128)S(1)}, f32[144,256]{1,0:T(8,128)S(1)}, f32[112,256]{1,0:T(8,128)S(1)}, f32[112,256]{1,0:T(8,128)S(1)}, f32[8,1024]{1,0...) custom-call(f32[1,1,96,896]{3,2,1,0:T(8,128)} %load_hbm.1, bf16[1,1,12,896]{3,2,1,0:T(8,128)(2,1)} %modes_hbm.1, ...), custom_call_target="tpu_custom_call" | custom-call | tf_op jit(solution)/shard_map/pallas_call | solution.py:428
  8.4 2.3 %collective-permute-done.1.refs_4_.refs_5_ = f32[1,48,1,96]{3,2,1,0:T(1,128)S(1)} collective-permute-done((f32[1,48,1,96]{3,2,1,0:T(1,128)}, f32[1,48,1,96]{3,2,1,0:T(1,128)S(1)}, u32[]{:S(2)}, u32[]{:S(2)}) %collective-permute-start.1) | collective-permute-done | bytes 18464 | tf_op jit(solution)/shard_map/ppermute | solution.py:478
  10.7 0.9 collective-permute-done.refs_3_.refs_4_
  11.6 0.7 copy-done
  12.9 1.1 %collective-permute-start.3 = (f32[144,256]{1,0:T(8,128)S(1)}, f32[144,256]{1,0:T(8,128)S(1)}, u32[]{:S(2)}, u32[]{:S(2)}) collective-permute-start(f32[144,256]{1,0:T(8,128)S(1)} %get-tuple-element.44.after_hbm.refs_0_), channel_id=1, source_target_pairs={{0,4},{1,5},{2,6},{3,7},{4,0},{5,1},{6,2},{7,3},{8,12},{9,13},{10,... | collective-permute-start | bytes 442376 | tf_op jit(solution)/shard_map/ppermute | solution.py:46
  14.5 3.8 %shard_map.88.refs_7_.matrix_ref = bf16[1024,1024]{1,0:T(8,128)(2,1)S(1)} custom-call(bf16[1,1,896,896]{3,2,1,0:T(8,128)(2,1)} %matrix_hbm.2, bf16[4,256,224]{2,1,0:T(8,128)(2,1)S(1)} %get-tuple-element.49.reorder_ref, f32[144,256]{1,0:T(8,128)S(1)} %get-tuple-element.44.after_hbm.refs_0_), custom_call_target="tpu_custom_call" | custom-call | tf_op jit(solution)/shard_map/pallas_call | solution.py:428
  18.3 1.0 collective-permute-done.4.refs_2_.refs_5_
  20.5 11.2 %all_to_all.25 = f32[32,9,1,128]{3,2,1,0:T(1,128)S(1)} all-to-all(f32[32,9,1,128]{3,2,1,0:T(1,128)S(1)} %bitcast.17), channel_id=1, replica_groups=mesh['gx'=8,'gy'=4] {'gy','gx'}, dimensions={0} | all-to-all | bytes 294912 | tf_op jit(solution)/shard_map/all_to_all | solution.py:465
  31.7 1.0 shard_map.91
  33.1 0.7 collective-permute-start.9
  33.8 1.0 collective-permute-start.7
  34.8 3.8 %shard_map.92.refs_10_.matrix_ref = bf16[1024,1024]{1,0:T(8,128)(2,1)S(1)} custom-call(bf16[1,1,896,896]{3,2,1,0:T(8,128)(2,1)} %matrix_hbm.3, bf16[4,256,224]{2,1,0:T(8,128)(2,1)S(1)} %get-tuple-element.49.reorder_ref, f32[96,256]{1,0:T(8,128)S(1)} %get-tuple-element.53.after_hbm.refs_0_), custom_call_target="tpu_custom_call" | custom-call | tf_op jit(solution)/shard_map/pallas_call | solution.py:428
  39.1 11.3 %all_to_all.26 = f32[32,9,1,128]{3,2,1,0:T(1,128)S(1)} all-to-all(f32[32,9,1,128]{3,2,1,0:T(1,128)S(1)} %bitcast.19), channel_id=1, replica_groups=mesh['gx'=8,'gy'=4] {'gy','gx'}, dimensions={0} | all-to-all | bytes 294912 | tf_op jit(solution)/shard_map/all_to_all | solution.py:465
  50.4 1.0 shard_map.94
  51.8 0.8 collective-permute-start.12
  52.5 0.7 collective-permute-start.13
  53.2 4.2 %collective-permute-done.12.refs_5_ = f32[96,256]{1,0:T(8,128)S(1)} collective-permute-done((f32[96,256]{1,0:T(8,128)S(1)}, f32[96,256]{1,0:T(8,128)S(1)}, u32[]{:S(2)}, u32[]{:S(2)}) %collective-permute-start.12) | collective-permute-done | bytes 98336 | tf_op jit(solution)/shard_map/ppermute | solution.py:46
  58.3 10.7 %all_to_all.27 = f32[32,9,1,128]{3,2,1,0:T(1,128)S(1)} all-to-all(f32[32,9,1,128]{3,2,1,0:T(1,128)S(1)} %bitcast.20), channel_id=1, replica_groups=mesh['gx'=8,'gy'=4] {'gy','gx'}, dimensions={0} | all-to-all | bytes 294912 | tf_op jit(solution)/shard_map/all_to_all | solution.py:465
  69.0 1.0 shard_map.96
  70.3 0.8 collective-permute-start.16
  71.1 0.7 collective-permute-start.17
  71.8 4.2 %collective-permute-done.16.refs_5_ = f32[96,256]{1,0:T(8,128)S(1)} collective-permute-done((f32[96,256]{1,0:T(8,128)S(1)}, f32[96,256]{1,0:T(8,128)S(1)}, u32[]{:S(2)}, u32[]{:S(2)}) %collective-permute-start.16) | collective-permute-done | bytes 98336 | tf_op jit(solution)/shard_map/ppermute | solution.py:46
  76.9 10.7 %all_to_all.28 = f32[32,9,1,128]{3,2,1,0:T(1,128)S(1)} all-to-all(f32[32,9,1,128]{3,2,1,0:T(1,128)S(1)} %bitcast.21), channel_id=1, replica_groups=mesh['gx'=8,'gy'=4] {'gy','gx'}, dimensions={0} | all-to-all | bytes 294912 | tf_op jit(solution)/shard_map/all_to_all | solution.py:465
  87.5 1.0 shard_map.98
  88.9 0.8 collective-permute-start.20
  89.7 0.7 collective-permute-start.21
  90.4 1.2 %shard_map.99.refs_10_ = f32[96,896]{1,0:T(8,128)} custom-call(f32[96,1024]{1,0:T(8,128)S(1)} %get-tuple-element.74.vector_ref, bf16[4,256,224]{2,1,0:T(8,128)(2,1)S(1)} %get-tuple-element.49.reorder_ref), custom_call_target="tpu_custom_call" | custom-call | tf_op jit(solution)/shard_map/pallas_call | solution.py:428
  91.5 3.0 %collective-permute-done.20.refs_5_ = f32[96,256]{1,0:T(8,128)S(1)} collective-permute-done((f32[96,256]{1,0:T(8,128)S(1)}, f32[96,256]{1,0:T(8,128)S(1)}, u32[]{:S(2)}, u32[]{:S(2)}) %collective-permute-start.20) | collective-permute-done | bytes 98336 | tf_op jit(solution)/shard_map/ppermute | solution.py:46
  95.5 10.7 %all_to_all.29 = f32[32,9,1,128]{3,2,1,0:T(1,128)S(1)} all-to-all(f32[32,9,1,128]{3,2,1,0:T(1,128)S(1)} %bitcast.18), channel_id=1, replica_groups=mesh['gx'=8,'gy'=4] {'gy','gx'}, dimensions={0} | all-to-all | bytes 294912 | tf_op jit(solution)/shard_map/all_to_all | solution.py:465
  106.1 1.7 %shard_map.101 = f32[96,896]{1,0:T(8,128)} custom-call(f32[288,128]{1,0:T(8,128)S(1)} %bitcast.15, bf16[256,864]{1,0:T(8,128)(2,1)S(1)} %shard_map.89.refs_9_.inverse_ref, bf16[128,1024]{1,0:T(8,128)(2,1)S(1)} %get-tuple-element.51.extended_ref, f32[96,1024]{1,0:T(8,128)S(1)} %get-tuple-element.80.vector_ref, f32[96,1024]{1,0:T(8,128)S(1)} %get-tuple-element.81.old_ref, ...), custom_call_target="tpu_custom_call" | custom-call | tf_op jit(solution)/shard_map/pallas_call | solution.py:428
  (39 shorter events, 6.9 us)
Async XLA Ops:
  0.6 7.8 %collective-permute-start.2 = (f32[1,48,1,96]{3,2,1,0:T(1,128)}, f32[1,48,1,96]{3,2,1,0:T(1,128)S(1)}, u32[]{:S(2)}, u32[]{:S(2)}) collective-permute-start(f32[1,48,1,96]{3,2,1,0:T(1,128)} %refs_3_.1), channel_id=1, source_target_pairs={{0,3},{1,0},{2,1},{3,2},{4,7},{5,4},{6,5},{7,6},{8,11},{9,8},{10,9... | collective-permute-start | bytes 55304 | tf_op jit(solution)/shard_map/ppermute | solution.py:478
  5.7 4.9 %collective-permute-start.1 = (f32[1,48,1,96]{3,2,1,0:T(1,128)}, f32[1,48,1,96]{3,2,1,0:T(1,128)S(1)}, u32[]{:S(2)}, u32[]{:S(2)}) collective-permute-start(f32[1,48,1,96]{3,2,1,0:T(1,128)} %refs_3_.1), channel_id=1, source_target_pairs={{0,2},{1,3},{2,0},{3,1},{4,6},{5,7},{6,4},{7,5},{8,10},{9,11},{10,... | collective-permute-start | bytes 55304 | tf_op jit(solution)/shard_map/ppermute | solution.py:478
  5.7 5.8 %collective-permute-start = (f32[1,48,1,96]{3,2,1,0:T(1,128)}, f32[1,48,1,96]{3,2,1,0:T(1,128)S(1)}, u32[]{:S(2)}, u32[]{:S(2)}) collective-permute-start(f32[1,48,1,96]{3,2,1,0:T(1,128)} %refs_3_.1), channel_id=1, source_target_pairs={{0,1},{1,2},{2,3},{3,0},{4,5},{5,6},{6,7},{7,4},{8,9},{9,10},{10,1... | collective-permute-start | bytes 55304 | tf_op jit(solution)/shard_map/ppermute | solution.py:478
  11.6 0.7 copy-start
  12.3 7.0 %collective-permute-start.4 = (f32[144,256]{1,0:T(8,128)S(1)}, f32[144,256]{1,0:T(8,128)S(1)}, u32[]{:S(2)}, u32[]{:S(2)}) collective-permute-start(f32[144,256]{1,0:T(8,128)S(1)} %get-tuple-element.45.refs_1_), channel_id=1, source_target_pairs={{0,28},{1,29},{2,30},{3,31},{4,8},{5,9},{6,10},{7,11},{8,4},{9,5},... | collective-permute-start | bytes 442376 | tf_op jit(solution)/shard_map/ppermute | solution.py:46
  12.9 6.5 %collective-permute-start.3 = (f32[144,256]{1,0:T(8,128)S(1)}, f32[144,256]{1,0:T(8,128)S(1)}, u32[]{:S(2)}, u32[]{:S(2)}) collective-permute-start(f32[144,256]{1,0:T(8,128)S(1)} %get-tuple-element.44.after_hbm.refs_0_), channel_id=1, source_target_pairs={{0,4},{1,5},{2,6},{3,7},{4,0},{5,1},{6,2},{7,3},{8,12},{9,13},{10,... | collective-permute-start | bytes 442376 | tf_op jit(solution)/shard_map/ppermute | solution.py:46
  14.0 5.9 %collective-permute-start.5 = (f32[112,256]{1,0:T(8,128)S(1)}, f32[112,256]{1,0:T(8,128)S(1)}, u32[]{:S(2)}, u32[]{:S(2)}) collective-permute-start(f32[112,256]{1,0:T(8,128)S(1)} %get-tuple-element.46.refs_2_), channel_id=1, source_target_pairs={{0,1},{1,2},{2,3},{3,7},{4,0},{5,4},{6,5},{7,6},{8,9},{9,10},{10,1... | collective-permute-start | bytes 344072 | tf_op jit(solution)/shard_map/ppermute | solution.py:46
  14.0 5.9 %collective-permute-start.6 = (f32[112,256]{1,0:T(8,128)S(1)}, f32[112,256]{1,0:T(8,128)S(1)}, u32[]{:S(2)}, u32[]{:S(2)}) collective-permute-start(f32[112,256]{1,0:T(8,128)S(1)} %get-tuple-element.47.refs_3_), channel_id=1, source_target_pairs={{0,4},{1,0},{2,1},{3,2},{4,5},{5,6},{6,7},{7,3},{8,12},{9,8},{10,9... | collective-permute-start | bytes 344072 | tf_op jit(solution)/shard_map/ppermute | solution.py:46
  14.5 4.8 %copy-start.1 = (f32[1,48,1,96]{3,2,1,0:T(1,128)S(1)}, f32[1,48,1,96]{3,2,1,0:T(1,128)}, u32[]{:S(2)}) copy-start(f32[1,48,1,96]{3,2,1,0:T(1,128)} %refs_3_.1) | copy-start | bytes 55300
  32.7 5.9 %collective-permute-start.8 = (f32[96,256]{1,0:T(8,128)S(1)}, f32[96,256]{1,0:T(8,128)S(1)}, u32[]{:S(2)}, u32[]{:S(2)}) collective-permute-start(f32[96,256]{1,0:T(8,128)S(1)} %get-tuple-element.54.refs_1_), channel_id=1, source_target_pairs={{0,28},{1,29},{2,30},{3,31},{4,8},{5,9},{6,10},{7,11},{8,4},{9,5},... | collective-permute-start | bytes 294920 | tf_op jit(solution)/shard_map/ppermute | solution.py:46
  33.1 5.5 %collective-permute-start.9 = (f32[96,256]{1,0:T(8,128)S(1)}, f32[96,256]{1,0:T(8,128)S(1)}, u32[]{:S(2)}, u32[]{:S(2)}) collective-permute-start(f32[96,256]{1,0:T(8,128)S(1)} %get-tuple-element.55.refs_2_), channel_id=1, source_target_pairs={{0,1},{1,2},{2,3},{3,7},{4,0},{5,4},{6,5},{7,6},{8,9},{9,10},{10,1... | collective-permute-start | bytes 294920 | tf_op jit(solution)/shard_map/ppermute | solution.py:46
  33.8 4.8 %collective-permute-start.10 = (f32[96,256]{1,0:T(8,128)S(1)}, f32[96,256]{1,0:T(8,128)S(1)}, u32[]{:S(2)}, u32[]{:S(2)}) collective-permute-start(f32[96,256]{1,0:T(8,128)S(1)} %get-tuple-element.56.refs_3_), channel_id=1, source_target_pairs={{0,4},{1,0},{2,1},{3,2},{4,5},{5,6},{6,7},{7,3},{8,12},{9,8},{10,9... | collective-permute-start | bytes 294920 | tf_op jit(solution)/shard_map/ppermute | solution.py:46
  33.8 4.8 %collective-permute-start.7 = (f32[96,256]{1,0:T(8,128)S(1)}, f32[96,256]{1,0:T(8,128)S(1)}, u32[]{:S(2)}, u32[]{:S(2)}) collective-permute-start(f32[96,256]{1,0:T(8,128)S(1)} %get-tuple-element.53.after_hbm.refs_0_), channel_id=1, source_target_pairs={{0,4},{1,5},{2,6},{3,7},{4,0},{5,1},{6,2},{7,3},{8,12},{9,13},{10,... | collective-permute-start | bytes 294920 | tf_op jit(solution)/shard_map/ppermute | solution.py:46
  51.4 1.8 %collective-permute-start.11 = (f32[96,256]{1,0:T(8,128)S(1)}, f32[96,256]{1,0:T(8,128)S(1)}, u32[]{:S(2)}, u32[]{:S(2)}) collective-permute-start(f32[96,256]{1,0:T(8,128)S(1)} %get-tuple-element.60.refs_0_), channel_id=1, source_target_pairs={{0,4},{1,5},{2,6},{3,7},{4,0},{5,1},{6,2},{7,3},{8,12},{9,13},{10,... | collective-permute-start | bytes 294920 | tf_op jit(solution)/shard_map/ppermute | solution.py:46
  51.8 5.6 %collective-permute-start.12 = (f32[96,256]{1,0:T(8,128)S(1)}, f32[96,256]{1,0:T(8,128)S(1)}, u32[]{:S(2)}, u32[]{:S(2)}) collective-permute-start(f32[96,256]{1,0:T(8,128)S(1)} %get-tuple-element.61.refs_1_), channel_id=1, source_target_pairs={{0,28},{1,29},{2,30},{3,31},{4,8},{5,9},{6,10},{7,11},{8,4},{9,5},... | collective-permute-start | bytes 294920 | tf_op jit(solution)/shard_map/ppermute | solution.py:46
  52.5 4.9 %collective-permute-start.13 = (f32[96,256]{1,0:T(8,128)S(1)}, f32[96,256]{1,0:T(8,128)S(1)}, u32[]{:S(2)}, u32[]{:S(2)}) collective-permute-start(f32[96,256]{1,0:T(8,128)S(1)} %get-tuple-element.62.refs_2_), channel_id=1, source_target_pairs={{0,1},{1,2},{2,3},{3,7},{4,0},{5,4},{6,5},{7,6},{8,9},{9,10},{10,1... | collective-permute-start | bytes 294920 | tf_op jit(solution)/shard_map/ppermute | solution.py:46
  53.2 4.6 %collective-permute-start.14 = (f32[96,256]{1,0:T(8,128)S(1)}, f32[96,256]{1,0:T(8,128)S(1)}, u32[]{:S(2)}, u32[]{:S(2)}) collective-permute-start(f32[96,256]{1,0:T(8,128)S(1)} %get-tuple-element.63.refs_3_), channel_id=1, source_target_pairs={{0,4},{1,0},{2,1},{3,2},{4,5},{5,6},{6,7},{7,3},{8,12},{9,8},{10,9... | collective-permute-start | bytes 294920 | tf_op jit(solution)/shard_map/ppermute | solution.py:46
  70.0 1.8 %collective-permute-start.15 = (f32[96,256]{1,0:T(8,128)S(1)}, f32[96,256]{1,0:T(8,128)S(1)}, u32[]{:S(2)}, u32[]{:S(2)}) collective-permute-start(f32[96,256]{1,0:T(8,128)S(1)} %get-tuple-element.67.refs_0_), channel_id=1, source_target_pairs={{0,4},{1,5},{2,6},{3,7},{4,0},{5,1},{6,2},{7,3},{8,12},{9,13},{10,... | collective-permute-start | bytes 294920 | tf_op jit(solution)/shard_map/ppermute | solution.py:46
  70.3 5.6 %collective-permute-start.16 = (f32[96,256]{1,0:T(8,128)S(1)}, f32[96,256]{1,0:T(8,128)S(1)}, u32[]{:S(2)}, u32[]{:S(2)}) collective-permute-start(f32[96,256]{1,0:T(8,128)S(1)} %get-tuple-element.68.refs_1_), channel_id=1, source_target_pairs={{0,28},{1,29},{2,30},{3,31},{4,8},{5,9},{6,10},{7,11},{8,4},{9,5},... | collective-permute-start | bytes 294920 | tf_op jit(solution)/shard_map/ppermute | solution.py:46
  71.1 4.9 %collective-permute-start.17 = (f32[96,256]{1,0:T(8,128)S(1)}, f32[96,256]{1,0:T(8,128)S(1)}, u32[]{:S(2)}, u32[]{:S(2)}) collective-permute-start(f32[96,256]{1,0:T(8,128)S(1)} %get-tuple-element.69.refs_2_), channel_id=1, source_target_pairs={{0,1},{1,2},{2,3},{3,7},{4,0},{5,4},{6,5},{7,6},{8,9},{9,10},{10,1... | collective-permute-start | bytes 294920 | tf_op jit(solution)/shard_map/ppermute | solution.py:46
  71.8 4.6 %collective-permute-start.18 = (f32[96,256]{1,0:T(8,128)S(1)}, f32[96,256]{1,0:T(8,128)S(1)}, u32[]{:S(2)}, u32[]{:S(2)}) collective-permute-start(f32[96,256]{1,0:T(8,128)S(1)} %get-tuple-element.70.refs_3_), channel_id=1, source_target_pairs={{0,4},{1,0},{2,1},{3,2},{4,5},{5,6},{6,7},{7,3},{8,12},{9,8},{10,9... | collective-permute-start | bytes 294920 | tf_op jit(solution)/shard_map/ppermute | solution.py:46
  88.5 3.0 %collective-permute-start.19 = (f32[96,256]{1,0:T(8,128)S(1)}, f32[96,256]{1,0:T(8,128)S(1)}, u32[]{:S(2)}, u32[]{:S(2)}) collective-permute-start(f32[96,256]{1,0:T(8,128)S(1)} %get-tuple-element.75.refs_0_), channel_id=1, source_target_pairs={{0,4},{1,5},{2,6},{3,7},{4,0},{5,1},{6,2},{7,3},{8,12},{9,13},{10,... | collective-permute-start | bytes 294920 | tf_op jit(solution)/shard_map/ppermute | solution.py:46
  88.9 5.6 %collective-permute-start.20 = (f32[96,256]{1,0:T(8,128)S(1)}, f32[96,256]{1,0:T(8,128)S(1)}, u32[]{:S(2)}, u32[]{:S(2)}) collective-permute-start(f32[96,256]{1,0:T(8,128)S(1)} %get-tuple-element.76.refs_1_), channel_id=1, source_target_pairs={{0,28},{1,29},{2,30},{3,31},{4,8},{5,9},{6,10},{7,11},{8,4},{9,5},... | collective-permute-start | bytes 294920 | tf_op jit(solution)/shard_map/ppermute | solution.py:46
  89.7 4.9 %collective-permute-start.21 = (f32[96,256]{1,0:T(8,128)S(1)}, f32[96,256]{1,0:T(8,128)S(1)}, u32[]{:S(2)}, u32[]{:S(2)}) collective-permute-start(f32[96,256]{1,0:T(8,128)S(1)} %get-tuple-element.77.refs_2_), channel_id=1, source_target_pairs={{0,1},{1,2},{2,3},{3,7},{4,0},{5,4},{6,5},{7,6},{8,9},{9,10},{10,1... | collective-permute-start | bytes 294920 | tf_op jit(solution)/shard_map/ppermute | solution.py:46
  90.4 4.6 %collective-permute-start.22 = (f32[96,256]{1,0:T(8,128)S(1)}, f32[96,256]{1,0:T(8,128)S(1)}, u32[]{:S(2)}, u32[]{:S(2)}) collective-permute-start(f32[96,256]{1,0:T(8,128)S(1)} %get-tuple-element.78.refs_3_), channel_id=1, source_target_pairs={{0,4},{1,0},{2,1},{3,2},{4,5},{5,6},{6,7},{7,3},{8,12},{9,8},{10,9... | collective-permute-start | bytes 294920 | tf_op jit(solution)/shard_map/ppermute | solution.py:46

commit v3 on v2

--- a/solution.py
+++ b/solution.py
@@ -13,10 +13,13 @@
 spectrum_low = 0.5
 spectrum_high = 4.0
 
-EVEN_FACES = (1, 0, 3, 2)
-ODD_FACES = (0, 1, 2, 3)
-ARRIVES = (0, 1, 3, 2)
+EVEN_FACES = (0, 3, 2, 1)
+ODD_FACES = (1, 2, 3, 0)
+ARRIVES = (0, 2, 1, 3)
 REORDERED = (0, 2)
+
+
+PRODUCTS = ((0, 0), (0, 1), (1, 0), (1, 1), (0, 2), (2, 0))
 
 
 def round_up(value, unit):
@@ -35,10 +38,10 @@
         return (a, b + step) if 0 <= b + step < cols else (a ^ 1, b)
 
     return (
-        pairs(lambda a, b: (a ^ 1, b)),
         pairs(lambda a, b: ((a + 1 if a % 2 else a - 1) % rows, b)),
         pairs(lambda a, b: along(a, b, -1 if a % 2 else 1)),
         pairs(lambda a, b: along(a, b, 1 if a % 2 else -1)),
+        pairs(lambda a, b: (a ^ 1, b)),
     )
 
 
@@ -79,24 +82,22 @@
     return jnp.where(parity == 0, even, odd)
 
 
-def face_columns(value, slot, parity, width):
-    even, odd = EVEN_FACES[slot], ODD_FACES[slot]
-    return by_parity(
-        parity,
-        value[:, even * width : (even + 1) * width],
-        value[:, odd * width : (odd + 1) * width],
-    )
-
-
-def reorder_matrix(partners, slot, parity, width, padded):
-    plain = lax.broadcasted_iota(jnp.int32, (1, width), 1)
-
-    def places(face):
-        return partners[face : face + 1, :] if face in REORDERED else plain
-
-    place = by_parity(parity, places(EVEN_FACES[slot]), places(ODD_FACES[slot]))
-    rows = lax.broadcasted_iota(jnp.int32, (padded, width), 0)
+def slot_of(face, parity):
+    return by_parity(parity, EVEN_FACES.index(face), ODD_FACES.index(face))
+
+
+def slots_from(faces, parity):
+    return [by_parity(parity, faces[EVEN_FACES[j]], faces[ODD_FACES[j]]) for j in range(4)]
+
+
+def reorder_matrix(place, padded):
+    rows = lax.broadcasted_iota(jnp.int32, (padded, place.shape[1]), 0)
     return jnp.where(rows == place, 1.0, 0.0).astype(bf16)
+
+
+def widened(value, padded):
+    blank = jnp.zeros((value.shape[0], padded - value.shape[1]), value.dtype)
+    return jnp.concatenate([value, blank], axis=1)
 
 
 def reorder_exact(value, matrix, dim):
@@ -155,69 +156,89 @@
 
 
 def load_kernel(
-    load_hbm, modes_hbm, partners_hbm, counts_hbm,
-    face_0, face_1, face_2, face_3, live_ref, reorder_ref,
+    load_hbm, modes_hbm, partners_hbm, counts_hbm, matrix_hbm, inverse_hbm,
+    slot_0, slot_1, slot_2, slot_3, live_ref, reorder_ref, matrix_ref, inverse_ref,
     load_ref, modes_ref, partners_ref, counts_ref, sems,
 ):
     copies = [
         pltpu.make_async_copy(source, target, sems.at[i])
         for i, (source, target) in enumerate(
             (
+                (partners_hbm.at[0, 0], partners_ref),
                 (load_hbm.at[0, 0], load_ref),
                 (modes_hbm.at[0, 0], modes_ref),
-                (partners_hbm.at[0, 0], partners_ref),
                 (counts_hbm.at[0], counts_ref),
+                (inverse_hbm, inverse_ref),
+                (matrix_hbm.at[0, 0], matrix_ref),
             )
         )
     ]
     for copy in copies:
         copy.start()
-    for copy in copies:
+    for copy in copies[:4]:
         copy.wait()
     parity = row_parity()
     width = partners_ref.shape[1]
     columns, count = load_ref.shape[0], modes_ref.shape[0]
-    padded = face_0.shape[1]
-    for slot, face_ref in enumerate((face_0, face_1, face_2, face_3)):
-        matrix = reorder_matrix(partners_ref[...], slot, parity, width, padded)
-        reorder_ref[slot] = matrix
-        values = face_columns(load_ref[...], slot, parity, width)
-        modes = face_columns(modes_ref[...], slot, parity, width)
-        face_ref[columns:, :] = jnp.zeros((face_ref.shape[0] - columns, padded), f32)
-        face_ref[:columns, :] = reorder_exact(values, matrix, 1)
-        face_ref[columns : columns + count, :] = contract(modes, matrix, 1, 1)
+    padded = slot_0.shape[1]
+    values, modes = [], []
+    for face in range(4):
+        place = slice(face * width, (face + 1) * width)
+        if face in REORDERED:
+            matrix = reorder_matrix(partners_ref[face : face + 1, :], padded)
+            reorder_ref[REORDERED.index(face)] = matrix
+            values.append(reorder_exact(load_ref[:, place], matrix, 1))
+            modes.append(contract(modes_ref[:, place], matrix, 1, 1))
+        else:
+            values.append(widened(load_ref[:, place], padded))
+            modes.append(widened(modes_ref[:, place], padded).astype(f32))
+    values, modes = slots_from(values, parity), slots_from(modes, parity)
+    for slot, slot_ref in enumerate((slot_0, slot_1, slot_2, slot_3)):
+        slot_ref[columns:, :] = jnp.zeros((slot_ref.shape[0] - columns, padded), f32)
+        slot_ref[:columns, :] = values[slot]
+        slot_ref[columns : columns + count, :] = modes[slot]
         live = by_parity(
             parity, counts_ref[0, EVEN_FACES[slot]], counts_ref[0, ODD_FACES[slot]]
         )
         places = lax.broadcasted_iota(jnp.int32, (live_ref.shape[0], padded), 1)
         live_ref[:, slot * padded : (slot + 1) * padded] = jnp.where(places < live, 1.0, 0.0)
-
-
-def matrix_kernel(matrix_hbm, reorder_ref, after_hbm, out_ref, matrix_ref, sems):
-    width = matrix_ref.shape[0] // 4
-    copies = [
-        pltpu.make_async_copy(
-            matrix_hbm.at[0, 0, pl.ds(face * width, width)],
-            matrix_ref.at[pl.ds(face * width, width)],
-            sems.at[face],
-        )
-        for face in range(4)
-    ]
-    for copy in copies:
-        copy.start()
+    for copy in copies[4:]:
+        copy.wait()
+
+
+def reorder_operator(matrix_ref, reorder_ref, out_ref, columns_ref):
     parity = row_parity()
-    padded = out_ref.shape[1] // 4
-    for face, copy in enumerate(copies):
-        copy.wait()
-        rows = matrix_ref[face * width : (face + 1) * width, :]
-        row_slot = by_parity(parity, EVEN_FACES.index(face), ODD_FACES.index(face))
-        place = pl.ds(pl.multiple_of(row_slot * padded, padded), padded)
-        for slot in range(4):
-            block = face_columns(rows, slot, parity, width)
-            block = contract(block, reorder_ref[slot], 1, 1).astype(bf16)
-            out_ref[place, slot * padded : (slot + 1) * padded] = contract(
-                reorder_ref[row_slot], block, 1, 0
-            ).astype(bf16)
+    width, padded = matrix_ref.shape[1] // 4, out_ref.shape[1] // 4
+
+    def slot_place(face):
+        return pl.ds(pl.multiple_of(slot_of(face, parity) * padded, padded), padded)
+
+    for face in range(4):
+        block = matrix_ref[:, face * width : (face + 1) * width]
+        if face in REORDERED:
+            block = contract(block, reorder_ref[REORDERED.index(face)], 1, 1).astype(bf16)
+        else:
+            block = widened(block, padded)
+        columns_ref[:, slot_place(face)] = block
+    for face in range(4):
+        block = columns_ref[face * width : (face + 1) * width, :]
+        if face in REORDERED:
+            block = contract(reorder_ref[REORDERED.index(face)], block, 1, 0).astype(bf16)
+        else:
+            blank = jnp.zeros((padded - width, block.shape[1]), bf16)
+            block = jnp.concatenate([block, blank], axis=0)
+        out_ref[slot_place(face), :] = block
+
+
+def smoother_kernel(matrix_ref, reorder_ref, next_hbm, after_hbm, out_ref, next_ref, columns_ref, sem):
+    copy = pltpu.make_async_copy(next_hbm.at[0, 0], next_ref, sem)
+    copy.start()
+    reorder_operator(matrix_ref, reorder_ref, out_ref, columns_ref)
+    copy.wait()
+
+
+def operator_kernel(matrix_ref, reorder_ref, after_hbm, out_ref, columns_ref):
+    reorder_operator(matrix_ref, reorder_ref, out_ref, columns_ref)
 
 
 def rows_kernel(count, base, *refs):
@@ -248,14 +269,14 @@
     long, short = pack_counts(count)
     rows_ref[...] = jnp.zeros(rows_ref.shape, f32)
     for e in range(cols):
-        for i, ref in enumerate(face_refs):
+        for i, ref in zip((0, 1, 4), face_refs):
             for line, lane, part in inverse_places(e, group, length, ref.shape[1]):
                 rows_ref[e, i * count : (i + 1) * count, part] = ref[
                     base + line : base + line + count, lane : lane + part.stop - part.start
                 ]
     for step, part_ref in enumerate(part_refs):
         source_col = lax.rem(here + cols - step, cols)
-        for i, row in ((3, jnp.where(parity == 0, north, south)), (4, jnp.where(parity == 0, south, north))):
+        for i, row in ((2, jnp.where(parity == 0, north, south)), (3, jnp.where(parity == 0, south, north))):
             rows_ref[source_col, i * count : (i + 1) * count, :] = part_ref[
                 0, pl.ds(row * count, count), 0, :
             ]
@@ -272,26 +293,30 @@
         places.append(
             jnp.where(same & inside & (source_mode == long + wanted), 1.0, 0.0).astype(bf16)
         )
-    everything = cols * wide
+    place = jnp.concatenate(places, axis=1)
     gathered = [[] for _ in places]
     for e in range(cols):
-        high, middle, _ = split3(rows_ref[e])
-        halves = jnp.concatenate([high, middle], axis=0)
-        for part, place in enumerate(places):
-            gathered[part].append(contract(halves, place, 1, 0))
+        pieces = jnp.concatenate(split3(rows_ref[e]), axis=0)
+        moved = contract(pieces, place, 1, 0)
+        for part in range(len(places)):
+            gathered[part].append(moved[:, part * wide : (part + 1) * wide])
     for part, pieces in enumerate(gathered):
-        both = jnp.concatenate(pieces, axis=1).astype(bf16)
-        place = slice(part * height, (part + 1) * height)
-        out_ref[place, :] = jnp.concatenate([both[:height], both[:height], both[height:]], axis=1)
+        high, middle, low = (
+            jnp.concatenate([p[k * height : (k + 1) * height] for p in pieces], axis=1)
+            for k in range(3)
+        )
+        factors = [(high, middle, low)[k] for k, _ in PRODUCTS]
+        out_ref[part * height : (part + 1) * height, :] = jnp.concatenate(factors, axis=1).astype(
+            bf16
+        )
 
 
 def coefficients(vector, columns_ref, count):
-    high, middle, _ = split3(vector)
     terms = jnp.dot(
-        jnp.concatenate([high, middle], axis=0), columns_ref[...], preferred_element_type=f32
+        jnp.concatenate(split3(vector), axis=0), columns_ref[...], preferred_element_type=f32
     )
     columns = vector.shape[0]
-    coeffs = (terms[:columns] + terms[columns:]).T
+    coeffs = (terms[:columns] + (terms[columns : 2 * columns] + terms[2 * columns :])).T
     return pack_coefficients(coeffs, count)
 
 
@@ -308,7 +333,7 @@
     sent, arrived, live_ref = refs[:4], refs[4:8], refs[8]
     vector_ref, coeff_ref, columns_ref, extended_ref, rows_ref = refs[-5:]
     columns, padded = vector_ref.shape[0], sent[0].shape[1]
-    group = sent[3].shape[0] - columns
+    group = sent[1].shape[0] - columns
     half = rows_ref.shape[0]
     join_faces(sent, arrived, live_ref, vector_ref)
     rows_ref[...] = jnp.zeros(rows_ref.shape, f32)
@@ -322,8 +347,8 @@
         rows_ref[:count, place] = own[:count]
         rows_ref[(1 + slot) * count : (2 + slot) * count, place] = other[:count]
     extended = rows_ref[...].astype(bf16)
-    extended_ref[:half, :] = extended
-    extended_ref[half:, :] = extended
+    for copy in range(3):
+        extended_ref[copy * half : (copy + 1) * half, :] = extended
     write_copies(coeff_ref, coefficients(vector_ref[...], columns_ref, count))
 
 
@@ -335,9 +360,10 @@
 
 
 def projected(coeff_ref, inverse_ref, extended_ref, vector_ref):
-    columns, height = vector_ref.shape[0], extended_ref.shape[0] // 2
-    high, middle, _ = split3(coeff_ref[...])
-    terms = contract(inverse_ref[...], jnp.concatenate([high, middle, high], axis=0), 1, 0)
+    columns, height = vector_ref.shape[0], extended_ref.shape[0] // 3
+    pieces = split3(coeff_ref[...])
+    factors = jnp.concatenate([pieces[k] for _, k in PRODUCTS], axis=0)
+    terms = contract(inverse_ref[...], factors, 1, 0)
     solved = terms[:height, :columns] + jnp.concatenate(
         [
             terms[i * height : (i + 1) * height, columns:]
@@ -345,8 +371,7 @@
         ],
         axis=1,
     )
-    high, middle, _ = split3(solved)
-    parts = jnp.concatenate([high, middle], axis=0)
+    parts = jnp.concatenate(split3(solved), axis=0)
     return vector_ref[...] - contract(parts, extended_ref[...], 0, 0)
 
 
@@ -393,18 +418,18 @@
 
 def face_order(value, reorder_ref):
     parity = row_parity()
-    padded = value.shape[1] // 4
-    slots = [
-        reorder_exact(value[:, slot * padded : (slot + 1) * padded], reorder_ref[slot], 0)
-        for slot in range(4)
-    ]
-    return jnp.concatenate(
-        [
-            by_parity(parity, slots[EVEN_FACES.index(face)], slots[ODD_FACES.index(face)])
-            for face in range(4)
-        ],
-        axis=1,
-    )
+    padded, width = value.shape[1] // 4, reorder_ref.shape[2]
+    slots = [value[:, slot * padded : (slot + 1) * padded] for slot in range(4)]
+    faces = []
+    for face in range(4):
+        block = by_parity(
+            parity, slots[EVEN_FACES.index(face)], slots[ODD_FACES.index(face)]
+        )
+        if face in REORDERED:
+            faces.append(reorder_exact(block, reorder_ref[REORDERED.index(face)], 0))
+        else:
+            faces.append(block[:, :width])
+    return jnp.concatenate(faces, axis=1)
 
 
 def last_kernel(coeff_ref, inverse_ref, extended_ref, vector_ref, old_ref, reorder_ref, out_ref):
@@ -454,7 +479,7 @@
     faces = [shape((columns, padded), f32)] * 4
     base = columns + group
     lines = inverse_lines(cols, group, rows * count, padded)
-    tall_faces = [shape((base + extra, padded), f32) for extra in (lines, lines, 0, 0)]
+    tall_faces = [shape((base + extra, padded), f32) for extra in (lines, 0, 0, lines)]
     matrix = shape((4 * padded, 4 * padded), bf16)
     coeff = shape((devices * long, packed), f32)
     result = shape((columns, slots), f32)
@@ -464,58 +489,59 @@
         chunks = values.reshape(devices, long, 1, packed)
         return lax.all_to_all(chunks, ("gy", "gx"), 0, 0).reshape(devices * long, packed)
 
-    def reordered(values, after):
-        return call(
-            matrix_kernel,
-            [matrix],
-            (values, reorder, after),
-            (0,),
-            (2,),
-            [pltpu.VMEM((slots, slots), bf16), pltpu.SemaphoreType.DMA((4,))],
-        )[0]
-
-    parts = [coarse_inverse] + [
-        lax.ppermute(coarse_inverse, "gy", [(b, (b + step) % cols) for b in range(cols)])
-        for step in range(1, cols)
-    ]
-    *sent, live, reorder = call(
+    raw = shape((slots, slots), bf16)
+    wide = pltpu.VMEM((slots, 4 * padded), bf16)
+    *sent, live, reorder, smoother, own_part = call(
         load_kernel,
         [
             *tall_faces,
             shape((8, 4 * padded), f32),
-            shape((4, padded, width), bf16),
+            shape((len(REORDERED), padded, width), bf16),
+            raw,
+            shape(coarse_inverse.shape, f32),
         ],
-        (load, modes, partners, face_counts),
-        (0, 1, 2, 3),
+        (load, modes, partners, face_counts, dirichlet, coarse_inverse),
+        (0, 1, 2, 3, 4, 5),
         (),
         [
             pltpu.VMEM((columns, slots), f32),
             pltpu.VMEM((count, slots), bf16),
             pltpu.VMEM((4, width), jnp.int32),
             pltpu.SMEM((1, 4), jnp.int32),
-            pltpu.SemaphoreType.DMA((4,)),
+            pltpu.SemaphoreType.DMA((6,)),
         ],
     )
-    sent[:2] = call(
+    parts = [own_part] + [
+        lax.ppermute(coarse_inverse, "gy", [(b, (b + step) % cols) for b in range(cols)])
+        for step in range(1, cols)
+    ]
+    sent[0], sent[3] = call(
         functools.partial(rows_kernel, count, base),
-        tall_faces[:2],
-        (*sent[:2], *parts),
+        [tall_faces[0], tall_faces[3]],
+        (sent[0], sent[3], *parts),
         scratch=[pltpu.VMEM((cols, group, rows * count), f32)],
         aliases={0: 0, 1: 1},
     )
     arrived = exchange(sent, lists)
-    smoother = reordered(dirichlet, sent[0])
+    smoother, operator = call(
+        smoother_kernel,
+        [matrix, raw],
+        (smoother, reorder, dual_operator, sent[0]),
+        (2,),
+        (3,),
+        [wide, pltpu.SemaphoreType.DMA],
+    )
     (inverse,) = call(
         functools.partial(inverse_kernel, count, base),
-        [shape(((1 + long // short) * height, 3 * devices * long), bf16)],
-        (sent[0], *arrived[:2], *parts, smoother),
+        [shape(((1 + long // short) * height, len(PRODUCTS) * devices * long), bf16)],
+        (sent[0], arrived[0], arrived[3], *parts, smoother),
         (),
         (3 + cols,),
         [pltpu.VMEM((cols, height, rows * count), f32)],
     )
     current, coeffs, mode_columns, extended = call(
         functools.partial(first_join_kernel, count),
-        [vector, coeff, shape((4 * padded, 128), bf16), shape((2 * height, 4 * padded), bf16)],
+        [vector, coeff, shape((4 * padded, 128), bf16), shape((3 * height, 4 * padded), bf16)],
         (*sent, *arrived, live, inverse),
         (),
         (9,),
@@ -538,7 +564,9 @@
         [vector, *faces],
         (everywhere(coeffs), inverse, extended, current, smoother),
     )
-    operator = reordered(dual_operator, sent[0])
+    (operator,) = call(
+        operator_kernel, [matrix], (operator, reorder, residual), (), (2,), [wide]
+    )
     direction, *sent = call(
         functools.partial(first_direction_kernel, alpha_0),
         [vector, *faces],

time: 108 us -> 107 us (level)
  Pallas kernels: 19 us -> 15.1 us
  starting transfers between devices: 15.9 us -> 17.4 us
    pallas_call x16, Pallas kernels: 19 us -> 15.1 us  [call(): pl.pallas_call(kernel, out_shape=tuple(outs), in_specs=[outside if i in h...]
    ppermute x20, waiting for transfers between devices: 13.7 us -> 16.7 us  [exchange(): lax.ppermute(value, ('gx', 'gy'), pairs)]
    ppermute x3, waiting for transfers between devices: 3.17 us -> 1.03 us  [local(): lax.ppermute(coarse_inverse, 'gy', [(b, (b + step) % cols) for b in range...]
  transfers between devices with their start and end apart: 23 -> 23, of which waited for: 9 -> 10; matrix products, arithmetic and copies ran while one was open for 0% -> 0% of each run, Pallas kernels for 10% -> 6%
where the time goes in v3:
time: 107 us; the launch traced here: 106 us
  blocking collectives  55.3 us (52%)
  waiting for transfers between devices  17.8 us (17%)
  starting transfers between devices  17.4 us (16%)
  Pallas kernels  15.1 us (14%)
    all_to_all x5, blocking collectives, everywhere(): lax.all_to_all(chunks, ('gy', 'gx'), 0, 0).reshape(devices * long, packed)  55.3 us
    ppermute x20, waiting for transfers between devices, exchange(): lax.ppermute(value, ('gx', 'gy'), pairs)  16.7 us
    pallas_call x16, Pallas kernels, call(): pl.pallas_call(kernel, out_shape=tuple(outs), in_specs=[outside if i in h...  15.1 us
    ppermute x20, starting transfers between devices, exchange(): lax.ppermute(value, ('gx', 'gy'), pairs)  10.4 us
    ppermute x3, starting transfers between devices, local(): lax.ppermute(coarse_inverse, 'gy', [(b, (b + step) % cols) for b in range...  7.01 us
  transfers between devices with their start and end apart: 23, of which 10 were waited for; matrix products, arithmetic and copies ran while one was open for 0% of the time, Pallas kernels for 6%

profile of v3, /device:TPU:0, one launch (start us, length us, event | category | flops | bytes accessed | tf_op | source)
XLA Modules:
  0.0 106.4 jit_solution(3164916063188692115)
XLA Ops:
  0.6 3.1 %collective-permute-start = (f32[1,48,1,96]{3,2,1,0:T(1,128)}, f32[1,48,1,96]{3,2,1,0:T(1,128)S(1)}, u32[]{:S(2)}, u32[]{:S(2)}) collective-permute-start(f32[1,48,1,96]{3,2,1,0:T(1,128)} %inverse_hbm.1), channel_id=1, source_target_pairs={{0,1},{1,2},{2,3},{3,0},{4,5},{5,6},{6,7},{7,4},{8,9},{9,10},{10,1... | collective-permute-start | bytes 55304 | tf_op jit(solution)/shard_map/ppermute | solution.py:515
  3.7 2.6 %collective-permute-start.1 = (f32[1,48,1,96]{3,2,1,0:T(1,128)}, f32[1,48,1,96]{3,2,1,0:T(1,128)S(1)}, u32[]{:S(2)}, u32[]{:S(2)}) collective-permute-start(f32[1,48,1,96]{3,2,1,0:T(1,128)} %inverse_hbm.1), channel_id=1, source_target_pairs={{0,2},{1,3},{2,0},{3,1},{4,6},{5,7},{6,4},{7,5},{8,10},{9,11},{10,... | collective-permute-start | bytes 55304 | tf_op jit(solution)/shard_map/ppermute | solution.py:515
  6.3 1.3 %collective-permute-start.2 = (f32[1,48,1,96]{3,2,1,0:T(1,128)}, f32[1,48,1,96]{3,2,1,0:T(1,128)S(1)}, u32[]{:S(2)}, u32[]{:S(2)}) collective-permute-start(f32[1,48,1,96]{3,2,1,0:T(1,128)} %inverse_hbm.1), channel_id=1, source_target_pairs={{0,3},{1,0},{2,1},{3,2},{4,7},{5,4},{6,5},{7,6},{8,11},{9,8},{10,9... | collective-permute-start | bytes 55304 | tf_op jit(solution)/shard_map/ppermute | solution.py:515
  7.6 1.6 %shard_map.86 = (f32[144,256]{1,0:T(8,128)S(1)}, f32[112,256]{1,0:T(8,128)S(1)}, f32[112,256]{1,0:T(8,128)S(1)}, f32[144,256]{1,0:T(8,128)S(1)}, f32[8,1024]{1,0...) custom-call(f32[1,1,96,896]{3,2,1,0:T(8,128)} %load_hbm.1, ...), custom_call_target="tpu_custom_call" | custom-call | tf_op jit(solution)/shard_map/pallas_call | solution.py:453
  9.3 1.0 collective-permute-done.2.refs_5_.refs_6_
  11.0 1.0 collective-permute-start.6
  12.5 1.5 %shard_map.88 = (bf16[1024,1024]{1,0:T(8,128)(2,1)S(1)}, bf16[896,896]{1,0:T(8,128)(2,1)S(1)}) custom-call(bf16[896,896]{1,0:T(8,128)(2,1)S(1)} %get-tuple-element.54.matrix_ref, bf16[2,256,224]{2,1,0:T(8,128)(2,1)S(1)} %get-tuple-element.55.reorder_ref, bf16[1,1,896,896]{3,2,1,0:T(8,128)(2,1)} %next_hbm.1, f32[144,256]{1,0:T(8,128)S(1)} %get-tuple-element.49.after_hbm.refs_0_), custom_call_target="tpu_custom_call" | custom-call | tf_op jit(solution)/shard_map/pallas_call | solution.py:453
  14.0 3.4 %collective-permute-done.3.refs_1_.refs_4_ = f32[144,256]{1,0:T(8,128)S(1)} collective-permute-done((f32[144,256]{1,0:T(8,128)S(1)}, f32[144,256]{1,0:T(8,128)S(1)}, u32[]{:S(2)}, u32[]{:S(2)}) %collective-permute-start.3) | collective-permute-done | bytes 147488 | tf_op jit(solution)/shard_map/ppermute | solution.py:49
  17.4 0.8 shard_map.89.refs_9_.inverse_ref
  18.8 11.9 %all_to_all.25 = f32[32,9,1,128]{3,2,1,0:T(1,128)S(1)} all-to-all(f32[32,9,1,128]{3,2,1,0:T(1,128)S(1)} %bitcast.17), channel_id=1, replica_groups=mesh['gx'=8,'gy'=4] {'gy','gx'}, dimensions={0} | all-to-all | bytes 294912 | tf_op jit(solution)/shard_map/all_to_all | solution.py:490
  30.8 1.1 %shard_map.91 = (f32[96,1024]{1,0:T(8,128)S(1)}, f32[96,256]{1,0:T(8,128)S(1)}, f32[96,256]{1,0:T(8,128)S(1)}, f32[96,256]{1,0:T(8,128)S(1)}, f32[96,256]{1,0:T(8,128)S(1)}) custom-call(f32[288,128]{1,0:T(8,128)S(1)} %bitcast.16, bf16[256,1728]{1,0:T(8,128)(2,1)S(1)} %shard_map.89.refs_9_.inverse_ref, bf16[192,1024]{1,0:T(8,128)(2,1)S(1)} %get-tuple-element.58.extended_ref, ...), custom_call_target="tpu_custom_call" | custom-call | tf_op jit(solution)/shard_map/pallas_call | solution.py:453
  32.2 0.8 collective-permute-start.7
  33.0 0.7 collective-permute-start.8
  33.7 1.0 shard_map.92.refs_10_.matrix_ref
  34.8 3.1 %collective-permute-done.7.refs_4_ = f32[96,256]{1,0:T(8,128)S(1)} collective-permute-done((f32[96,256]{1,0:T(8,128)S(1)}, f32[96,256]{1,0:T(8,128)S(1)}, u32[]{:S(2)}, u32[]{:S(2)}) %collective-permute-start.7) | collective-permute-done | bytes 98336 | tf_op jit(solution)/shard_map/ppermute | solution.py:49
  38.9 10.7 %all_to_all.26 = f32[32,9,1,128]{3,2,1,0:T(1,128)S(1)} all-to-all(f32[32,9,1,128]{3,2,1,0:T(1,128)S(1)} %bitcast.19), channel_id=1, replica_groups=mesh['gx'=8,'gy'=4] {'gy','gx'}, dimensions={0} | all-to-all | bytes 294912 | tf_op jit(solution)/shard_map/all_to_all | solution.py:490
  49.5 1.1 %shard_map.94 = (f32[96,1024]{1,0:T(8,128)S(1)}, f32[96,256]{1,0:T(8,128)S(1)}, f32[96,256]{1,0:T(8,128)S(1)}, f32[96,256]{1,0:T(8,128)S(1)}, f32[96,256]{1,0:T(8,128)S(1)}) custom-call(f32[288,128]{1,0:T(8,128)S(1)} %bitcast.14, bf16[256,1728]{1,0:T(8,128)(2,1)S(1)} %shard_map.89.refs_9_.inverse_ref, bf16[192,1024]{1,0:T(8,128)(2,1)S(1)} %get-tuple-element.58.extended_ref, ...), custom_call_target="tpu_custom_call" | custom-call | tf_op jit(solution)/shard_map/pallas_call | solution.py:453
  51.1 0.7 collective-permute-start.12
  51.8 1.0 collective-permute-start.14
  52.8 3.1 %collective-permute-done.11.refs_4_ = f32[96,256]{1,0:T(8,128)S(1)} collective-permute-done((f32[96,256]{1,0:T(8,128)S(1)}, f32[96,256]{1,0:T(8,128)S(1)}, u32[]{:S(2)}, u32[]{:S(2)}) %collective-permute-start.11) | collective-permute-done | bytes 98336 | tf_op jit(solution)/shard_map/ppermute | solution.py:49
  57.0 10.9 %all_to_all.27 = f32[32,9,1,128]{3,2,1,0:T(1,128)S(1)} all-to-all(f32[32,9,1,128]{3,2,1,0:T(1,128)S(1)} %bitcast.20), channel_id=1, replica_groups=mesh['gx'=8,'gy'=4] {'gy','gx'}, dimensions={0} | all-to-all | bytes 294912 | tf_op jit(solution)/shard_map/all_to_all | solution.py:490
  67.9 1.1 %shard_map.96 = (f32[96,1024]{1,0:T(8,128)S(1)}, f32[96,256]{1,0:T(8,128)S(1)}, f32[96,256]{1,0:T(8,128)S(1)}, f32[96,256]{1,0:T(8,128)S(1)}, f32[96,256]{1,0:T(8,128)S(1)}) custom-call(f32[288,128]{1,0:T(8,128)S(1)} %bitcast.13, bf16[256,1728]{1,0:T(8,128)(2,1)S(1)} %shard_map.89.refs_9_.inverse_ref, bf16[192,1024]{1,0:T(8,128)(2,1)S(1)} %get-tuple-element.58.extended_ref, ...), custom_call_target="tpu_custom_call" | custom-call | tf_op jit(solution)/shard_map/pallas_call | solution.py:453
  69.5 0.7 collective-permute-start.16
  70.2 1.0 collective-permute-start.18
  71.2 3.1 %collective-permute-done.15.refs_4_ = f32[96,256]{1,0:T(8,128)S(1)} collective-permute-done((f32[96,256]{1,0:T(8,128)S(1)}, f32[96,256]{1,0:T(8,128)S(1)}, u32[]{:S(2)}, u32[]{:S(2)}) %collective-permute-start.15) | collective-permute-done | bytes 98336 | tf_op jit(solution)/shard_map/ppermute | solution.py:49
  75.4 10.9 %all_to_all.28 = f32[32,9,1,128]{3,2,1,0:T(1,128)S(1)} all-to-all(f32[32,9,1,128]{3,2,1,0:T(1,128)S(1)} %bitcast.21), channel_id=1, replica_groups=mesh['gx'=8,'gy'=4] {'gy','gx'}, dimensions={0} | all-to-all | bytes 294912 | tf_op jit(solution)/shard_map/all_to_all | solution.py:490
  86.3 1.1 %shard_map.98 = (f32[96,1024]{1,0:T(8,128)S(1)}, f32[96,256]{1,0:T(8,128)S(1)}, f32[96,256]{1,0:T(8,128)S(1)}, f32[96,256]{1,0:T(8,128)S(1)}, f32[96,256]{1,0:T(8,128)S(1)}) custom-call(f32[288,128]{1,0:T(8,128)S(1)} %bitcast.12, bf16[256,1728]{1,0:T(8,128)(2,1)S(1)} %shard_map.89.refs_9_.inverse_ref, bf16[192,1024]{1,0:T(8,128)(2,1)S(1)} %get-tuple-element.58.extended_ref, ...), custom_call_target="tpu_custom_call" | custom-call | tf_op jit(solution)/shard_map/pallas_call | solution.py:453
  88.6 1.0 collective-permute-start.22
  89.6 1.1 shard_map.99.refs_10_
  90.7 2.1 %collective-permute-done.19.refs_4_ = f32[96,256]{1,0:T(8,128)S(1)} collective-permute-done((f32[96,256]{1,0:T(8,128)S(1)}, f32[96,256]{1,0:T(8,128)S(1)}, u32[]{:S(2)}, u32[]{:S(2)}) %collective-permute-start.19) | collective-permute-done | bytes 98336 | tf_op jit(solution)/shard_map/ppermute | solution.py:49
  93.8 10.9 %all_to_all.29 = f32[32,9,1,128]{3,2,1,0:T(1,128)S(1)} all-to-all(f32[32,9,1,128]{3,2,1,0:T(1,128)S(1)} %bitcast.18), channel_id=1, replica_groups=mesh['gx'=8,'gy'=4] {'gy','gx'}, dimensions={0} | all-to-all | bytes 294912 | tf_op jit(solution)/shard_map/all_to_all | solution.py:490
  104.7 1.7 %shard_map.101 = f32[96,896]{1,0:T(8,128)} custom-call(f32[288,128]{1,0:T(8,128)S(1)} %bitcast.15, bf16[256,1728]{1,0:T(8,128)(2,1)S(1)} %shard_map.89.refs_9_.inverse_ref, bf16[192,1024]{1,0:T(8,128)(2,1)S(1)} %get-tuple-element.58.extended_ref, f32[96,1024]{1,0:T(8,128)S(1)} %get-tuple-element.88.vector_ref, f32[96,1024]{1,0:T(8,128)S(1)} %get-tuple-element.89.old_ref, ...), custom_call_target="tpu_custom_call" | custom-call | tf_op jit(solution)/shard_map/pallas_call | solution.py:453
  (35 shorter events, 8.5 us)
Async XLA Ops:
  0.6 8.7 %collective-permute-start = (f32[1,48,1,96]{3,2,1,0:T(1,128)}, f32[1,48,1,96]{3,2,1,0:T(1,128)S(1)}, u32[]{:S(2)}, u32[]{:S(2)}) collective-permute-start(f32[1,48,1,96]{3,2,1,0:T(1,128)} %inverse_hbm.1), channel_id=1, source_target_pairs={{0,1},{1,2},{2,3},{3,0},{4,5},{5,6},{6,7},{7,4},{8,9},{9,10},{10,1... | collective-permute-start | bytes 55304 | tf_op jit(solution)/shard_map/ppermute | solution.py:515
  3.7 5.6 %collective-permute-start.1 = (f32[1,48,1,96]{3,2,1,0:T(1,128)}, f32[1,48,1,96]{3,2,1,0:T(1,128)S(1)}, u32[]{:S(2)}, u32[]{:S(2)}) collective-permute-start(f32[1,48,1,96]{3,2,1,0:T(1,128)} %inverse_hbm.1), channel_id=1, source_target_pairs={{0,2},{1,3},{2,0},{3,1},{4,6},{5,7},{6,4},{7,5},{8,10},{9,11},{10,... | collective-permute-start | bytes 55304 | tf_op jit(solution)/shard_map/ppermute | solution.py:515
  6.3 4.0 %collective-permute-start.2 = (f32[1,48,1,96]{3,2,1,0:T(1,128)}, f32[1,48,1,96]{3,2,1,0:T(1,128)S(1)}, u32[]{:S(2)}, u32[]{:S(2)}) collective-permute-start(f32[1,48,1,96]{3,2,1,0:T(1,128)} %inverse_hbm.1), channel_id=1, source_target_pairs={{0,3},{1,0},{2,1},{3,2},{4,7},{5,4},{6,5},{7,6},{8,11},{9,8},{10,9... | collective-permute-start | bytes 55304 | tf_op jit(solution)/shard_map/ppermute | solution.py:515
  10.4 7.0 %collective-permute-start.3 = (f32[144,256]{1,0:T(8,128)S(1)}, f32[144,256]{1,0:T(8,128)S(1)}, u32[]{:S(2)}, u32[]{:S(2)}) collective-permute-start(f32[144,256]{1,0:T(8,128)S(1)} %get-tuple-element.49.after_hbm.refs_0_), channel_id=1, source_target_pairs={{0,28},{1,29},{2,30},{3,31},{4,8},{5,9},{6,10},{7,11},{8,4},{9,5},... | collective-permute-start | bytes 442376 | tf_op jit(solution)/shard_map/ppermute | solution.py:49
  11.0 6.3 %collective-permute-start.6 = (f32[144,256]{1,0:T(8,128)S(1)}, f32[144,256]{1,0:T(8,128)S(1)}, u32[]{:S(2)}, u32[]{:S(2)}) collective-permute-start(f32[144,256]{1,0:T(8,128)S(1)} %get-tuple-element.52.refs_3_), channel_id=1, source_target_pairs={{0,4},{1,5},{2,6},{3,7},{4,0},{5,1},{6,2},{7,3},{8,12},{9,13},{10,... | collective-permute-start | bytes 442376 | tf_op jit(solution)/shard_map/ppermute | solution.py:49
  12.0 6.1 %collective-permute-start.4 = (f32[112,256]{1,0:T(8,128)S(1)}, f32[112,256]{1,0:T(8,128)S(1)}, u32[]{:S(2)}, u32[]{:S(2)}) collective-permute-start(f32[112,256]{1,0:T(8,128)S(1)} %get-tuple-element.50.refs_1_), channel_id=1, source_target_pairs={{0,1},{1,2},{2,3},{3,7},{4,0},{5,4},{6,5},{7,6},{8,9},{9,10},{10,1... | collective-permute-start | bytes 344072 | tf_op jit(solution)/shard_map/ppermute | solution.py:49
  12.3 5.9 %collective-permute-start.5 = (f32[112,256]{1,0:T(8,128)S(1)}, f32[112,256]{1,0:T(8,128)S(1)}, u32[]{:S(2)}, u32[]{:S(2)}) collective-permute-start(f32[112,256]{1,0:T(8,128)S(1)} %get-tuple-element.51.refs_2_), channel_id=1, source_target_pairs={{0,4},{1,0},{2,1},{3,2},{4,5},{5,6},{6,7},{7,3},{8,12},{9,8},{10,9... | collective-permute-start | bytes 344072 | tf_op jit(solution)/shard_map/ppermute | solution.py:49
  31.9 2.9 %collective-permute-start.10 = (f32[96,256]{1,0:T(8,128)S(1)}, f32[96,256]{1,0:T(8,128)S(1)}, u32[]{:S(2)}, u32[]{:S(2)}) collective-permute-start(f32[96,256]{1,0:T(8,128)S(1)} %get-tuple-element.63.refs_3_), channel_id=1, source_target_pairs={{0,4},{1,5},{2,6},{3,7},{4,0},{5,1},{6,2},{7,3},{8,12},{9,13},{10,... | collective-permute-start | bytes 294920 | tf_op jit(solution)/shard_map/ppermute | solution.py:49
  32.2 5.6 %collective-permute-start.7 = (f32[96,256]{1,0:T(8,128)S(1)}, f32[96,256]{1,0:T(8,128)S(1)}, u32[]{:S(2)}, u32[]{:S(2)}) collective-permute-start(f32[96,256]{1,0:T(8,128)S(1)} %get-tuple-element.60.refs_0_), channel_id=1, source_target_pairs={{0,28},{1,29},{2,30},{3,31},{4,8},{5,9},{6,10},{7,11},{8,4},{9,5},... | collective-permute-start | bytes 294920 | tf_op jit(solution)/shard_map/ppermute | solution.py:49
  33.0 4.9 %collective-permute-start.8 = (f32[96,256]{1,0:T(8,128)S(1)}, f32[96,256]{1,0:T(8,128)S(1)}, u32[]{:S(2)}, u32[]{:S(2)}) collective-permute-start(f32[96,256]{1,0:T(8,128)S(1)} %get-tuple-element.61.refs_1_), channel_id=1, source_target_pairs={{0,1},{1,2},{2,3},{3,7},{4,0},{5,4},{6,5},{7,6},{8,9},{9,10},{10,1... | collective-permute-start | bytes 294920 | tf_op jit(solution)/shard_map/ppermute | solution.py:49
  33.7 4.6 %collective-permute-start.9 = (f32[96,256]{1,0:T(8,128)S(1)}, f32[96,256]{1,0:T(8,128)S(1)}, u32[]{:S(2)}, u32[]{:S(2)}) collective-permute-start(f32[96,256]{1,0:T(8,128)S(1)} %get-tuple-element.62.refs_2_), channel_id=1, source_target_pairs={{0,4},{1,0},{2,1},{3,2},{4,5},{5,6},{6,7},{7,3},{8,12},{9,8},{10,9... | collective-permute-start | bytes 294920 | tf_op jit(solution)/shard_map/ppermute | solution.py:49
  50.7 5.2 %collective-permute-start.11 = (f32[96,256]{1,0:T(8,128)S(1)}, f32[96,256]{1,0:T(8,128)S(1)}, u32[]{:S(2)}, u32[]{:S(2)}) collective-permute-start(f32[96,256]{1,0:T(8,128)S(1)} %get-tuple-element.69.refs_0_), channel_id=1, source_target_pairs={{0,28},{1,29},{2,30},{3,31},{4,8},{5,9},{6,10},{7,11},{8,4},{9,5},... | collective-permute-start | bytes 294920 | tf_op jit(solution)/shard_map/ppermute | solution.py:49
  51.1 4.8 %collective-permute-start.12 = (f32[96,256]{1,0:T(8,128)S(1)}, f32[96,256]{1,0:T(8,128)S(1)}, u32[]{:S(2)}, u32[]{:S(2)}) collective-permute-start(f32[96,256]{1,0:T(8,128)S(1)} %get-tuple-element.70.refs_1_), channel_id=1, source_target_pairs={{0,1},{1,2},{2,3},{3,7},{4,0},{5,4},{6,5},{7,6},{8,9},{9,10},{10,1... | collective-permute-start | bytes 294920 | tf_op jit(solution)/shard_map/ppermute | solution.py:49
  51.8 4.6 %collective-permute-start.13 = (f32[96,256]{1,0:T(8,128)S(1)}, f32[96,256]{1,0:T(8,128)S(1)}, u32[]{:S(2)}, u32[]{:S(2)}) collective-permute-start(f32[96,256]{1,0:T(8,128)S(1)} %get-tuple-element.71.refs_2_), channel_id=1, source_target_pairs={{0,4},{1,0},{2,1},{3,2},{4,5},{5,6},{6,7},{7,3},{8,12},{9,8},{10,9... | collective-permute-start | bytes 294920 | tf_op jit(solution)/shard_map/ppermute | solution.py:49
  51.8 4.6 %collective-permute-start.14 = (f32[96,256]{1,0:T(8,128)S(1)}, f32[96,256]{1,0:T(8,128)S(1)}, u32[]{:S(2)}, u32[]{:S(2)}) collective-permute-start(f32[96,256]{1,0:T(8,128)S(1)} %get-tuple-element.72.refs_3_), channel_id=1, source_target_pairs={{0,4},{1,5},{2,6},{3,7},{4,0},{5,1},{6,2},{7,3},{8,12},{9,13},{10,... | collective-permute-start | bytes 294920 | tf_op jit(solution)/shard_map/ppermute | solution.py:49
  69.1 5.2 %collective-permute-start.15 = (f32[96,256]{1,0:T(8,128)S(1)}, f32[96,256]{1,0:T(8,128)S(1)}, u32[]{:S(2)}, u32[]{:S(2)}) collective-permute-start(f32[96,256]{1,0:T(8,128)S(1)} %get-tuple-element.75.refs_0_), channel_id=1, source_target_pairs={{0,28},{1,29},{2,30},{3,31},{4,8},{5,9},{6,10},{7,11},{8,4},{9,5},... | collective-permute-start | bytes 294920 | tf_op jit(solution)/shard_map/ppermute | solution.py:49
  69.5 4.8 %collective-permute-start.16 = (f32[96,256]{1,0:T(8,128)S(1)}, f32[96,256]{1,0:T(8,128)S(1)}, u32[]{:S(2)}, u32[]{:S(2)}) collective-permute-start(f32[96,256]{1,0:T(8,128)S(1)} %get-tuple-element.76.refs_1_), channel_id=1, source_target_pairs={{0,1},{1,2},{2,3},{3,7},{4,0},{5,4},{6,5},{7,6},{8,9},{9,10},{10,1... | collective-permute-start | bytes 294920 | tf_op jit(solution)/shard_map/ppermute | solution.py:49
  70.2 4.6 %collective-permute-start.17 = (f32[96,256]{1,0:T(8,128)S(1)}, f32[96,256]{1,0:T(8,128)S(1)}, u32[]{:S(2)}, u32[]{:S(2)}) collective-permute-start(f32[96,256]{1,0:T(8,128)S(1)} %get-tuple-element.77.refs_2_), channel_id=1, source_target_pairs={{0,4},{1,0},{2,1},{3,2},{4,5},{5,6},{6,7},{7,3},{8,12},{9,8},{10,9... | collective-permute-start | bytes 294920 | tf_op jit(solution)/shard_map/ppermute | solution.py:49
  70.2 4.6 %collective-permute-start.18 = (f32[96,256]{1,0:T(8,128)S(1)}, f32[96,256]{1,0:T(8,128)S(1)}, u32[]{:S(2)}, u32[]{:S(2)}) collective-permute-start(f32[96,256]{1,0:T(8,128)S(1)} %get-tuple-element.78.refs_3_), channel_id=1, source_target_pairs={{0,4},{1,5},{2,6},{3,7},{4,0},{5,1},{6,2},{7,3},{8,12},{9,13},{10,... | collective-permute-start | bytes 294920 | tf_op jit(solution)/shard_map/ppermute | solution.py:49
  87.5 5.2 %collective-permute-start.19 = (f32[96,256]{1,0:T(8,128)S(1)}, f32[96,256]{1,0:T(8,128)S(1)}, u32[]{:S(2)}, u32[]{:S(2)}) collective-permute-start(f32[96,256]{1,0:T(8,128)S(1)} %get-tuple-element.83.refs_0_), channel_id=1, source_target_pairs={{0,28},{1,29},{2,30},{3,31},{4,8},{5,9},{6,10},{7,11},{8,4},{9,5},... | collective-permute-start | bytes 294920 | tf_op jit(solution)/shard_map/ppermute | solution.py:49
  87.9 4.8 %collective-permute-start.20 = (f32[96,256]{1,0:T(8,128)S(1)}, f32[96,256]{1,0:T(8,128)S(1)}, u32[]{:S(2)}, u32[]{:S(2)}) collective-permute-start(f32[96,256]{1,0:T(8,128)S(1)} %get-tuple-element.84.refs_1_), channel_id=1, source_target_pairs={{0,1},{1,2},{2,3},{3,7},{4,0},{5,4},{6,5},{7,6},{8,9},{9,10},{10,1... | collective-permute-start | bytes 294920 | tf_op jit(solution)/shard_map/ppermute | solution.py:49
  88.6 4.6 %collective-permute-start.21 = (f32[96,256]{1,0:T(8,128)S(1)}, f32[96,256]{1,0:T(8,128)S(1)}, u32[]{:S(2)}, u32[]{:S(2)}) collective-permute-start(f32[96,256]{1,0:T(8,128)S(1)} %get-tuple-element.85.refs_2_), channel_id=1, source_target_pairs={{0,4},{1,0},{2,1},{3,2},{4,5},{5,6},{6,7},{7,3},{8,12},{9,8},{10,9... | collective-permute-start | bytes 294920 | tf_op jit(solution)/shard_map/ppermute | solution.py:49
  88.6 4.6 %collective-permute-start.22 = (f32[96,256]{1,0:T(8,128)S(1)}, f32[96,256]{1,0:T(8,128)S(1)}, u32[]{:S(2)}, u32[]{:S(2)}) collective-permute-start(f32[96,256]{1,0:T(8,128)S(1)} %get-tuple-element.86.refs_3_), channel_id=1, source_target_pairs={{0,4},{1,5},{2,6},{3,7},{4,0},{5,1},{6,2},{7,3},{8,12},{9,13},{10,... | collective-permute-start | bytes 294920 | tf_op jit(solution)/shard_map/ppermute | solution.py:49

commit v4 on v3

--- a/solution.py
+++ b/solution.py
@@ -13,9 +13,9 @@
 spectrum_low = 0.5
 spectrum_high = 4.0
 
-EVEN_FACES = (0, 3, 2, 1)
-ODD_FACES = (1, 2, 3, 0)
-ARRIVES = (0, 2, 1, 3)
+EVEN_FACES = (3, 0, 2, 1)
+ODD_FACES = (2, 1, 3, 0)
+ARRIVES = (2, 1, 0, 3)
 REORDERED = (0, 2)
 
 
@@ -38,11 +38,17 @@
         return (a, b + step) if 0 <= b + step < cols else (a ^ 1, b)
 
     return (
+        pairs(lambda a, b: along(a, b, -1 if a % 2 else 1)),
         pairs(lambda a, b: ((a + 1 if a % 2 else a - 1) % rows, b)),
-        pairs(lambda a, b: along(a, b, -1 if a % 2 else 1)),
         pairs(lambda a, b: along(a, b, 1 if a % 2 else -1)),
         pairs(lambda a, b: (a ^ 1, b)),
     )
+
+
+def column_met(here, step, cols):
+    if cols & (cols - 1) == 0:
+        return here ^ step
+    return (here + cols - step) % cols
 
 
 def exchange(values, lists):
@@ -122,6 +128,50 @@
     tail = coeffs[long:count]
     side = jnp.concatenate([tail[:, i * piece : (i + 1) * piece] for i in range(pieces)], axis=0)
     return jnp.concatenate([coeffs[:long], side], axis=1)
+
+
+def packed_shape(columns, width, padded):
+    tail = width % 128
+    free = 128 - tail
+    pieces = tail // free if tail else 0
+    if padded != 256 or not pieces or tail % free or columns % (8 * (pieces + 1)):
+        return columns, padded
+    return columns + columns * pieces // (pieces + 1), 128
+
+
+def packed_parts(columns, rows):
+    kept = rows - columns
+    moved = columns - kept
+    pieces = kept // moved
+    free = 128 // (pieces + 1)
+    return kept, moved, pieces, free, 128 - free
+
+
+def pack_face(value, shape):
+    if value.shape == shape:
+        return value
+    kept, _, pieces, free, tail = packed_parts(value.shape[0], shape[0])
+    first, second = value[:, :128], value[:, 128:]
+    lowest = second[kept:]
+    side = [pltpu.roll(lowest, tail - i * free, 1) for i in range(pieces)]
+    lanes = lax.broadcasted_iota(jnp.int32, (kept, 128), 1)
+    second = jnp.where(lanes < tail, second[:kept], jnp.concatenate(side, axis=0))
+    return jnp.concatenate([first, second], axis=0)
+
+
+def unpack_face(value, columns):
+    if value.shape[0] == columns:
+        return value
+    _, moved, pieces, free, tail = packed_parts(columns, value.shape[0])
+    first, second = value[:columns], value[columns:]
+    lanes = lax.broadcasted_iota(jnp.int32, (moved, 128), 1)
+    lowest = jnp.zeros((moved, 128), value.dtype)
+    for i in range(pieces):
+        piece = pltpu.roll(second[i * moved : (i + 1) * moved], 128 - tail + i * free, 1)
+        inside = (lanes >= i * free) & (lanes < (i + 1) * free)
+        lowest = jnp.where(inside, piece, lowest)
+    second = jnp.concatenate([second, lowest], axis=0)
+    return jnp.concatenate([first, second], axis=1)
 
 
 def write_copies(out_ref, value):
@@ -230,24 +280,17 @@
         out_ref[slot_place(face), :] = block
 
 
-def smoother_kernel(matrix_ref, reorder_ref, next_hbm, after_hbm, out_ref, next_ref, columns_ref, sem):
-    copy = pltpu.make_async_copy(next_hbm.at[0, 0], next_ref, sem)
-    copy.start()
-    reorder_operator(matrix_ref, reorder_ref, out_ref, columns_ref)
-    copy.wait()
-
-
 def operator_kernel(matrix_ref, reorder_ref, after_hbm, out_ref, columns_ref):
     reorder_operator(matrix_ref, reorder_ref, out_ref, columns_ref)
 
 
 def rows_kernel(count, base, *refs):
-    part_refs, (first_ref, second_ref, rows_ref) = refs[2:-3], refs[-3:]
+    part_refs, (first_ref, second_ref, rows_ref) = refs[2:-4], refs[-3:]
     cols, here = len(part_refs), lax.axis_index("gy")
     group, length = rows_ref.shape[1:]
     rows_ref[...] = jnp.zeros(rows_ref.shape, f32)
     for step, part_ref in enumerate(part_refs):
-        source = lax.rem(here + cols - step, cols)
+        source = column_met(here, step, cols)
         rows_ref[source, :count, :] = part_ref[0, pl.ds(here * count, count), 0, :]
     for face_ref in (first_ref, second_ref):
         for e in range(cols):
@@ -269,14 +312,14 @@
     long, short = pack_counts(count)
     rows_ref[...] = jnp.zeros(rows_ref.shape, f32)
     for e in range(cols):
-        for i, ref in zip((0, 1, 4), face_refs):
+        for i, ref in zip((0, 2, 4), face_refs):
             for line, lane, part in inverse_places(e, group, length, ref.shape[1]):
                 rows_ref[e, i * count : (i + 1) * count, part] = ref[
                     base + line : base + line + count, lane : lane + part.stop - part.start
                 ]
     for step, part_ref in enumerate(part_refs):
-        source_col = lax.rem(here + cols - step, cols)
-        for i, row in ((2, jnp.where(parity == 0, north, south)), (3, jnp.where(parity == 0, south, north))):
+        source_col = column_met(here, step, cols)
+        for i, row in ((1, jnp.where(parity == 0, north, south)), (3, jnp.where(parity == 0, south, north))):
             rows_ref[source_col, i * count : (i + 1) * count, :] = part_ref[
                 0, pl.ds(row * count, count), 0, :
             ]
@@ -321,11 +364,12 @@
 
 
 def join_faces(sent, arrived, live_ref, vector_ref):
-    columns, padded = vector_ref.shape[0], sent[0].shape[1]
+    columns, padded = vector_ref.shape[0], vector_ref.shape[1] // 4
     for slot in range(4):
         place = slice(slot * padded, (slot + 1) * padded)
         own, other = sent[slot], arrived[ARRIVES.index(slot)]
-        total = own[:columns, :] + other[:columns, :]
+        height = columns if own.shape[1] == padded else own.shape[0]
+        total = unpack_face(own[:height, :] + other[:height, :], columns)
         vector_ref[:, place] = jnp.where(live_ref[:1, place] > 0.0, total, 0.0)
 
 
@@ -333,7 +377,7 @@
     sent, arrived, live_ref = refs[:4], refs[4:8], refs[8]
     vector_ref, coeff_ref, columns_ref, extended_ref, rows_ref = refs[-5:]
     columns, padded = vector_ref.shape[0], sent[0].shape[1]
-    group = sent[1].shape[0] - columns
+    group = sent[0].shape[0] - columns
     half = rows_ref.shape[0]
     join_faces(sent, arrived, live_ref, vector_ref)
     rows_ref[...] = jnp.zeros(rows_ref.shape, f32)
@@ -355,8 +399,17 @@
 def join_kernel(count, *refs):
     sent, arrived, live_ref, columns_ref = refs[:4], refs[4:8], refs[8], refs[9]
     vector_ref, coeff_ref = refs[-2:]
-    join_faces(sent, arrived, live_ref, vector_ref)
-    write_copies(coeff_ref, coefficients(vector_ref[...], columns_ref, count))
+    columns, padded = vector_ref.shape[0], vector_ref.shape[1] // 4
+    terms = jnp.zeros((3 * columns, columns_ref.shape[1]), f32)
+    for slot in range(4):
+        place = slice(slot * padded, (slot + 1) * padded)
+        total = unpack_face(sent[slot][...] + arrived[ARRIVES.index(slot)][...], columns)
+        total = jnp.where(live_ref[:1, place] > 0.0, total, 0.0)
+        vector_ref[:, place] = total
+        pieces = jnp.concatenate(split3(total), axis=0)
+        terms = terms + jnp.dot(pieces, columns_ref[place, :], preferred_element_type=f32)
+    coeffs = terms[:columns] + (terms[columns : 2 * columns] + terms[2 * columns :])
+    write_copies(coeff_ref, pack_coefficients(coeffs.T, count))
 
 
 def projected(coeff_ref, inverse_ref, extended_ref, vector_ref):
@@ -379,9 +432,8 @@
     rounded = vector.astype(bf16)
     padded = matrix_ref.shape[1] // 4
     for slot, face_ref in enumerate(face_refs):
-        face_ref[...] = contract(
-            rounded, matrix_ref[:, slot * padded : (slot + 1) * padded], 1, 0
-        )
+        product = contract(rounded, matrix_ref[:, slot * padded : (slot + 1) * padded], 1, 0)
+        face_ref[...] = pack_face(product, face_ref.shape)
 
 
 def start_kernel(coeff_ref, inverse_ref, extended_ref, vector_ref, matrix_ref, *refs):
@@ -432,16 +484,27 @@
     return jnp.concatenate(faces, axis=1)
 
 
-def last_kernel(coeff_ref, inverse_ref, extended_ref, vector_ref, old_ref, reorder_ref, out_ref):
+def last_kernel(
+    coeff_ref, inverse_ref, extended_ref, vector_ref, old_ref, reorder_ref, out_hbm, out_ref, sems
+):
     residual = old_ref[...] - projected(coeff_ref, inverse_ref, extended_ref, vector_ref)
-    out_ref[...] = face_order(residual, reorder_ref)
+    parts = sems.shape[0]
+    share = residual.shape[0] // parts
+    copies = []
+    for i in range(parts):
+        out_ref[i] = face_order(residual[i * share : (i + 1) * share], reorder_ref)
+        target = out_hbm.at[pl.ds(i * share, share)]
+        copies.append(pltpu.make_async_copy(out_ref.at[i], target, sems.at[i]))
+        copies[-1].start()
+    for copy in copies:
+        copy.wait()
 
 
 def multipliers_kernel(vector_ref, reorder_ref, out_ref):
     out_ref[...] = face_order(vector_ref[...], reorder_ref)
 
 
-def call(kernel, outs, args, hbm=(), after=(), scratch=(), aliases={}):
+def call(kernel, outs, args, hbm=(), after=(), scratch=(), aliases={}, out_space=pltpu.VMEM):
     vmem = pl.BlockSpec(memory_space=pltpu.VMEM)
     outside = pl.BlockSpec(memory_space=pltpu.HBM)
     anywhere = pl.BlockSpec(memory_space=pl.ANY)
@@ -456,7 +519,7 @@
         in_specs=[
             outside if i in hbm else anywhere if i in after else vmem for i in range(len(args))
         ],
-        out_specs=tuple([vmem] * len(outs)),
+        out_specs=tuple([pl.BlockSpec(memory_space=out_space)] * len(outs)),
         scratch_shapes=list(scratch),
         input_output_aliases=aliases,
         compiler_params=pltpu.CompilerParams(vmem_limit_bytes=min(size + (8 << 20), 56 << 20)),
@@ -476,10 +539,10 @@
     lists = exchanges(rows, cols)
     shape = jax.ShapeDtypeStruct
     vector = shape((columns, 4 * padded), f32)
-    faces = [shape((columns, padded), f32)] * 4
+    faces = [shape(packed_shape(columns, width, padded), f32)] * 4
     base = columns + group
     lines = inverse_lines(cols, group, rows * count, padded)
-    tall_faces = [shape((base + extra, padded), f32) for extra in (lines, 0, 0, lines)]
+    tall_faces = [shape((base + extra, padded), f32) for extra in (0, lines, 0, lines)]
     matrix = shape((4 * padded, 4 * padded), bf16)
     coeff = shape((devices * long, packed), f32)
     result = shape((columns, slots), f32)
@@ -512,29 +575,26 @@
         ],
     )
     parts = [own_part] + [
-        lax.ppermute(coarse_inverse, "gy", [(b, (b + step) % cols) for b in range(cols)])
+        lax.ppermute(coarse_inverse, "gy", [(column_met(b, step, cols), b) for b in range(cols)])
         for step in range(1, cols)
     ]
-    sent[0], sent[3] = call(
+    (smoother,) = call(operator_kernel, [matrix], (smoother, reorder, live), (), (2,), [wide])
+    sent[1], sent[3] = call(
         functools.partial(rows_kernel, count, base),
-        [tall_faces[0], tall_faces[3]],
-        (sent[0], sent[3], *parts),
+        [tall_faces[1], tall_faces[3]],
+        (sent[1], sent[3], *parts, smoother),
+        after=(2 + cols,),
         scratch=[pltpu.VMEM((cols, group, rows * count), f32)],
         aliases={0: 0, 1: 1},
     )
     arrived = exchange(sent, lists)
-    smoother, operator = call(
-        smoother_kernel,
-        [matrix, raw],
-        (smoother, reorder, dual_operator, sent[0]),
-        (2,),
-        (3,),
-        [wide, pltpu.SemaphoreType.DMA],
+    (operator,) = call(
+        operator_kernel, [matrix], (dual_operator[0, 0], reorder, sent[1]), (), (2,), [wide]
     )
     (inverse,) = call(
         functools.partial(inverse_kernel, count, base),
         [shape(((1 + long // short) * height, len(PRODUCTS) * devices * long), bf16)],
-        (sent[0], arrived[0], arrived[3], *parts, smoother),
+        (sent[1], arrived[1], arrived[3], *parts, operator),
         (),
         (3 + cols,),
         [pltpu.VMEM((cols, height, rows * count), f32)],
@@ -564,13 +624,10 @@
         [vector, *faces],
         (everywhere(coeffs), inverse, extended, current, smoother),
     )
-    (operator,) = call(
-        operator_kernel, [matrix], (operator, reorder, residual), (), (2,), [wide]
-    )
     direction, *sent = call(
         functools.partial(first_direction_kernel, alpha_0),
         [vector, *faces],
-        (*join(sent, operator), operator),
+        (*join(sent), operator),
     )
     residual, *sent = call(
         residual_kernel, [vector, *faces], (*join(sent), smoother, residual)
@@ -582,7 +639,11 @@
     )
     (multipliers,) = call(multipliers_kernel, [result], (multipliers, reorder))
     (residual,) = call(
-        last_kernel, [result], (*join(sent, multipliers, last=True), residual, reorder)
+        last_kernel,
+        [result],
+        (*join(sent, multipliers, last=True), residual, reorder),
+        scratch=[pltpu.VMEM((2, columns // 2, slots), f32), pltpu.SemaphoreType.DMA((2,))],
+        out_space=pl.ANY,
     )
     return (multipliers[None, None], residual[None, None])
 

time: 107 us -> 104 us (0.972)
  blocking collectives: 55.3 us -> 52.5 us
  waiting for transfers between devices: 17.8 us -> 19.9 us
  starting transfers between devices: 17.4 us -> 15.9 us
    all_to_all x5, blocking collectives: 55.3 us -> 52.5 us  [everywhere(): lax.all_to_all(chunks, ('gy', 'gx'), 0, 0).reshape(devices * long, packed)]
    ppermute x3, starting transfers between devices: 7.01 us -> 5.68 us  [local(): lax.ppermute(coarse_inverse, 'gy', [(column_met(b, step, cols), b) for b...]
    ppermute x3, waiting for transfers between devices: 1.03 us -> 2.35 us  [local(): lax.ppermute(coarse_inverse, 'gy', [(column_met(b, step, cols), b) for b...]
  transfers between devices with their start and end apart: 23 -> 23, of which waited for: 10 -> 12; matrix products, arithmetic and copies ran while one was open for 0% -> 0% of each run, Pallas kernels for 6% -> 5%
where the time goes in v4:
time: 104 us
  blocking collectives  52.5 us (50%)
  waiting for transfers between devices  19.9 us (19%)
  starting transfers between devices  15.9 us (15%)
  Pallas kernels  15 us (14%)
    all_to_all x5, blocking collectives, everywhere(): lax.all_to_all(chunks, ('gy', 'gx'), 0, 0).reshape(devices * long, packed)  52.5 us
    ppermute x20, waiting for transfers between devices, exchange(): lax.ppermute(value, ('gx', 'gy'), pairs)  17.5 us
    pallas_call x16, Pallas kernels, call(): pl.pallas_call(kernel, out_shape=tuple(outs), in_specs=[outside if i in h...  15 us
    ppermute x20, starting transfers between devices, exchange(): lax.ppermute(value, ('gx', 'gy'), pairs)  10.2 us
    ppermute x3, starting transfers between devices, local(): lax.ppermute(coarse_inverse, 'gy', [(column_met(b, step, cols), b) for b...  5.68 us
    ppermute x3, waiting for transfers between devices, local(): lax.ppermute(coarse_inverse, 'gy', [(column_met(b, step, cols), b) for b...  2.35 us
  transfers between devices with their start and end apart: 23, of which 12 were waited for; matrix products, arithmetic and copies ran while one was open for 0% of the time, Pallas kernels for 5%

profile of v4, /device:TPU:0, one launch (start us, length us, event | category | flops | bytes accessed | tf_op | source)
XLA Modules:
  0.0 104.0 jit_solution(13281049917568850185)
XLA Ops:
  0.6 3.1 %collective-permute-start = (f32[1,48,1,96]{3,2,1,0:T(1,128)}, f32[1,48,1,96]{3,2,1,0:T(1,128)S(1)}, u32[]{:S(2)}, u32[]{:S(2)}) collective-permute-start(f32[1,48,1,96]{3,2,1,0:T(1,128)} %inverse_hbm.1), channel_id=1, source_target_pairs={{1,0},{0,1},{3,2},{2,3},{5,4},{4,5},{7,6},{6,7},{9,8},{8,9},{11,10... | collective-permute-start | bytes 55304 | tf_op jit(solution)/shard_map/ppermute | solution.py:578
  3.7 2.5 %collective-permute-start.2 = (f32[1,48,1,96]{3,2,1,0:T(1,128)}, f32[1,48,1,96]{3,2,1,0:T(1,128)S(1)}, u32[]{:S(2)}, u32[]{:S(2)}) collective-permute-start(f32[1,48,1,96]{3,2,1,0:T(1,128)} %inverse_hbm.1), channel_id=1, source_target_pairs={{3,0},{2,1},{1,2},{0,3},{7,4},{6,5},{5,6},{4,7},{11,8},{10,9},{9,1... | collective-permute-start | bytes 55304 | tf_op jit(solution)/shard_map/ppermute | solution.py:578
  6.3 1.6 %shard_map.86 = (f32[112,256]{1,0:T(8,128)S(1)}, f32[144,256]{1,0:T(8,128)S(1)}, f32[112,256]{1,0:T(8,128)S(1)}, f32[144,256]{1,0:T(8,128)S(1)}, f32[8,1024]{1,0...) custom-call(f32[1,1,96,896]{3,2,1,0:T(8,128)} %load_hbm.1, ...), custom_call_target="tpu_custom_call" | custom-call | tf_op jit(solution)/shard_map/pallas_call | solution.py:516
  8.0 1.1 %shard_map.87.refs_6_.matrix_ref = bf16[1024,1024]{1,0:T(8,128)(2,1)S(1)} custom-call(bf16[896,896]{1,0:T(8,128)(2,1)S(1)} %get-tuple-element.48.matrix_ref, bf16[2,256,224]{2,1,0:T(8,128)(2,1)S(1)} %get-tuple-element.49.reorder_ref, f32[8,1024]{1,0:T(8,128)S(1)} %get-tuple-element.50.after_hbm.refs_8_), custom_call_target="tpu_custom_call" | custom-call | tf_op jit(solution)/shard_map/pallas_call | solution.py:516
  9.0 0.9 collective-permute-done.2.refs_5_.refs_6_
  9.9 1.5 %collective-permute-done.1.refs_4_.refs_5_ = f32[1,48,1,96]{3,2,1,0:T(1,128)S(1)} collective-permute-done((f32[1,48,1,96]{3,2,1,0:T(1,128)}, f32[1,48,1,96]{3,2,1,0:T(1,128)S(1)}, u32[]{:S(2)}, u32[]{:S(2)}) %collective-permute-start.1) | collective-permute-done | bytes 18464 | tf_op jit(solution)/shard_map/ppermute | solution.py:578
  11.5 2.5 %collective-permute-start.4 = (f32[144,256]{1,0:T(8,128)S(1)}, f32[144,256]{1,0:T(8,128)S(1)}, u32[]{:S(2)}, u32[]{:S(2)}) collective-permute-start(f32[144,256]{1,0:T(8,128)S(1)} %get-tuple-element.51.after_hbm.refs_0_.refs_1_), channel_id=1, source_target_pairs={{0,28},{1,29},{2,30},{3,31},{4,8},{5,9},{6,10},{7,11},{8,4},{9,5},... | collective-permute-start | bytes 442376 | tf_op jit(solution)/shard_map/ppermute | solution.py:55
  14.6 1.0 %shard_map.89.refs_7_.matrix_ref = bf16[1024,1024]{1,0:T(8,128)(2,1)S(1)} custom-call(bf16[896,896]{1,0:T(8,128)(2,1)S(1)} %bitcast.13, bf16[2,256,224]{2,1,0:T(8,128)(2,1)S(1)} %get-tuple-element.49.reorder_ref, f32[144,256]{1,0:T(8,128)S(1)} %get-tuple-element.51.after_hbm.refs_0_.refs_1_), custom_call_target="tpu_custom_call" | custom-call | tf_op jit(solution)/shard_map/pallas_call | solution.py:516
  15.6 2.4 %collective-permute-done.4.refs_1_.refs_5_ = f32[144,256]{1,0:T(8,128)S(1)} collective-permute-done((f32[144,256]{1,0:T(8,128)S(1)}, f32[144,256]{1,0:T(8,128)S(1)}, u32[]{:S(2)}, u32[]{:S(2)}) %collective-permute-start.4) | collective-permute-done | bytes 147488 | tf_op jit(solution)/shard_map/ppermute | solution.py:55
  18.0 0.8 shard_map.90.refs_9_.inverse_ref
  20.0 10.4 %all_to_all.25 = f32[32,9,1,128]{3,2,1,0:T(1,128)S(1)} all-to-all(f32[32,9,1,128]{3,2,1,0:T(1,128)S(1)} %bitcast.19), channel_id=1, replica_groups=mesh['gx'=8,'gy'=4] {'gy','gx'}, dimensions={0} | all-to-all | bytes 294912 | tf_op jit(solution)/shard_map/all_to_all | solution.py:553
  30.4 1.2 %shard_map.92 = (f32[96,1024]{1,0:T(8,128)S(1)}, f32[168,128]{1,0:T(8,128)S(1)}, f32[168,128]{1,0:T(8,128)S(1)}, f32[168,128]{1,0:T(8,128)S(1)}, f32[168,128]{1,0:T(8,128)S(1)}) custom-call(f32[288,128]{1,0:T(8,128)S(1)} %bitcast.18, bf16[256,1728]{1,0:T(8,128)(2,1)S(1)} %shard_map.90.refs_9_.inverse_ref, ...), custom_call_target="tpu_custom_call" | custom-call | tf_op jit(solution)/shard_map/pallas_call | solution.py:516
  32.7 0.7 collective-permute-start.10
  33.4 1.6 %collective-permute-done.7.refs_4_ = f32[168,128]{1,0:T(8,128)S(1)} collective-permute-done((f32[168,128]{1,0:T(8,128)S(1)}, f32[168,128]{1,0:T(8,128)S(1)}, u32[]{:S(2)}, u32[]{:S(2)}) %collective-permute-start.7) | collective-permute-done | bytes 86048 | tf_op jit(solution)/shard_map/ppermute | solution.py:55
  35.0 2.3 %collective-permute-done.8.refs_5_ = f32[168,128]{1,0:T(8,128)S(1)} collective-permute-done((f32[168,128]{1,0:T(8,128)S(1)}, f32[168,128]{1,0:T(8,128)S(1)}, u32[]{:S(2)}, u32[]{:S(2)}) %collective-permute-start.8) | collective-permute-done | bytes 86048 | tf_op jit(solution)/shard_map/ppermute | solution.py:55
  37.9 10.5 %all_to_all.26 = f32[32,9,1,128]{3,2,1,0:T(1,128)S(1)} all-to-all(f32[32,9,1,128]{3,2,1,0:T(1,128)S(1)} %bitcast.21), channel_id=1, replica_groups=mesh['gx'=8,'gy'=4] {'gy','gx'}, dimensions={0} | all-to-all | bytes 294912 | tf_op jit(solution)/shard_map/all_to_all | solution.py:553
  48.4 1.2 %shard_map.94 = (f32[96,1024]{1,0:T(8,128)S(1)}, f32[168,128]{1,0:T(8,128)S(1)}, f32[168,128]{1,0:T(8,128)S(1)}, f32[168,128]{1,0:T(8,128)S(1)}, f32[168,128]{1,0:T(8,128)S(1)}) custom-call(f32[288,128]{1,0:T(8,128)S(1)} %bitcast.16, bf16[256,1728]{1,0:T(8,128)(2,1)S(1)} %shard_map.90.refs_9_.inverse_ref, ...), custom_call_target="tpu_custom_call" | custom-call | tf_op jit(solution)/shard_map/pallas_call | solution.py:516
  50.7 0.7 collective-permute-start.14
  51.4 1.6 %collective-permute-done.11.refs_4_ = f32[168,128]{1,0:T(8,128)S(1)} collective-permute-done((f32[168,128]{1,0:T(8,128)S(1)}, f32[168,128]{1,0:T(8,128)S(1)}, u32[]{:S(2)}, u32[]{:S(2)}) %collective-permute-start.11) | collective-permute-done | bytes 86048 | tf_op jit(solution)/shard_map/ppermute | solution.py:55
  52.9 2.3 %collective-permute-done.12.refs_5_ = f32[168,128]{1,0:T(8,128)S(1)} collective-permute-done((f32[168,128]{1,0:T(8,128)S(1)}, f32[168,128]{1,0:T(8,128)S(1)}, u32[]{:S(2)}, u32[]{:S(2)}) %collective-permute-start.12) | collective-permute-done | bytes 86048 | tf_op jit(solution)/shard_map/ppermute | solution.py:55
  55.9 10.5 %all_to_all.27 = f32[32,9,1,128]{3,2,1,0:T(1,128)S(1)} all-to-all(f32[32,9,1,128]{3,2,1,0:T(1,128)S(1)} %bitcast.22), channel_id=1, replica_groups=mesh['gx'=8,'gy'=4] {'gy','gx'}, dimensions={0} | all-to-all | bytes 294912 | tf_op jit(solution)/shard_map/all_to_all | solution.py:553
  66.4 1.2 %shard_map.96 = (f32[96,1024]{1,0:T(8,128)S(1)}, f32[168,128]{1,0:T(8,128)S(1)}, f32[168,128]{1,0:T(8,128)S(1)}, f32[168,128]{1,0:T(8,128)S(1)}, f32[168,128]{1,0:T(8,128)S(1)}) custom-call(f32[288,128]{1,0:T(8,128)S(1)} %bitcast.14, bf16[256,1728]{1,0:T(8,128)(2,1)S(1)} %shard_map.90.refs_9_.inverse_ref, ...), custom_call_target="tpu_custom_call" | custom-call | tf_op jit(solution)/shard_map/pallas_call | solution.py:516
  68.7 0.7 collective-permute-start.18
  69.4 1.6 %collective-permute-done.15.refs_4_ = f32[168,128]{1,0:T(8,128)S(1)} collective-permute-done((f32[168,128]{1,0:T(8,128)S(1)}, f32[168,128]{1,0:T(8,128)S(1)}, u32[]{:S(2)}, u32[]{:S(2)}) %collective-permute-start.15) | collective-permute-done | bytes 86048 | tf_op jit(solution)/shard_map/ppermute | solution.py:55
  70.9 2.3 %collective-permute-done.16.refs_5_ = f32[168,128]{1,0:T(8,128)S(1)} collective-permute-done((f32[168,128]{1,0:T(8,128)S(1)}, f32[168,128]{1,0:T(8,128)S(1)}, u32[]{:S(2)}, u32[]{:S(2)}) %collective-permute-start.16) | collective-permute-done | bytes 86048 | tf_op jit(solution)/shard_map/ppermute | solution.py:55
  73.8 10.5 %all_to_all.28 = f32[32,9,1,128]{3,2,1,0:T(1,128)S(1)} all-to-all(f32[32,9,1,128]{3,2,1,0:T(1,128)S(1)} %bitcast.23), channel_id=1, replica_groups=mesh['gx'=8,'gy'=4] {'gy','gx'}, dimensions={0} | all-to-all | bytes 294912 | tf_op jit(solution)/shard_map/all_to_all | solution.py:553
  84.3 1.2 %shard_map.98 = (f32[96,1024]{1,0:T(8,128)S(1)}, f32[168,128]{1,0:T(8,128)S(1)}, f32[168,128]{1,0:T(8,128)S(1)}, f32[168,128]{1,0:T(8,128)S(1)}, f32[168,128]{1,0:T(8,128)S(1)}) custom-call(f32[288,128]{1,0:T(8,128)S(1)} %bitcast.15, bf16[256,1728]{1,0:T(8,128)(2,1)S(1)} %shard_map.90.refs_9_.inverse_ref, ...), custom_call_target="tpu_custom_call" | custom-call | tf_op jit(solution)/shard_map/pallas_call | solution.py:516
  86.6 0.7 collective-permute-start.22
  87.3 1.1 %shard_map.99.refs_10_ = f32[96,896]{1,0:T(8,128)} custom-call(f32[96,1024]{1,0:T(8,128)S(1)} %get-tuple-element.78.vector_ref, bf16[2,256,224]{2,1,0:T(8,128)(2,1)S(1)} %get-tuple-element.49.reorder_ref), custom_call_target="tpu_custom_call" | custom-call | tf_op jit(solution)/shard_map/pallas_call | solution.py:516
  88.9 2.3 %collective-permute-done.20.refs_5_ = f32[168,128]{1,0:T(8,128)S(1)} collective-permute-done((f32[168,128]{1,0:T(8,128)S(1)}, f32[168,128]{1,0:T(8,128)S(1)}, u32[]{:S(2)}, u32[]{:S(2)}) %collective-permute-start.20) | collective-permute-done | bytes 86048 | tf_op jit(solution)/shard_map/ppermute | solution.py:55
  91.8 10.5 %all_to_all.29 = f32[32,9,1,128]{3,2,1,0:T(1,128)S(1)} all-to-all(f32[32,9,1,128]{3,2,1,0:T(1,128)S(1)} %bitcast.20), channel_id=1, replica_groups=mesh['gx'=8,'gy'=4] {'gy','gx'}, dimensions={0} | all-to-all | bytes 294912 | tf_op jit(solution)/shard_map/all_to_all | solution.py:553
  102.3 1.7 %shard_map.101 = f32[96,896]{1,0:T(8,128)} custom-call(f32[288,128]{1,0:T(8,128)S(1)} %bitcast.17, bf16[256,1728]{1,0:T(8,128)(2,1)S(1)} %shard_map.90.refs_9_.inverse_ref, bf16[192,1024]{1,0:T(8,128)(2,1)S(1)} %get-tuple-element.55.extended_ref, f32[96,1024]{1,0:T(8,128)S(1)} %get-tuple-element.84.vector_ref, f32[96,1024]{1,0:T(8,128)S(1)} %get-tuple-element.85.old_ref, ...), custom_call_target="tpu_custom_call" | custom-call | tf_op jit(solution)/shard_map/pallas_call | solution.py:516
  (37 shorter events, 9.0 us)
Async XLA Ops:
  0.6 8.4 %collective-permute-start = (f32[1,48,1,96]{3,2,1,0:T(1,128)}, f32[1,48,1,96]{3,2,1,0:T(1,128)S(1)}, u32[]{:S(2)}, u32[]{:S(2)}) collective-permute-start(f32[1,48,1,96]{3,2,1,0:T(1,128)} %inverse_hbm.1), channel_id=1, source_target_pairs={{1,0},{0,1},{3,2},{2,3},{5,4},{4,5},{7,6},{6,7},{9,8},{8,9},{11,10... | collective-permute-start | bytes 55304 | tf_op jit(solution)/shard_map/ppermute | solution.py:578
  3.7 6.2 %collective-permute-start.2 = (f32[1,48,1,96]{3,2,1,0:T(1,128)}, f32[1,48,1,96]{3,2,1,0:T(1,128)S(1)}, u32[]{:S(2)}, u32[]{:S(2)}) collective-permute-start(f32[1,48,1,96]{3,2,1,0:T(1,128)} %inverse_hbm.1), channel_id=1, source_target_pairs={{3,0},{2,1},{1,2},{0,3},{7,4},{6,5},{5,6},{4,7},{11,8},{10,9},{9,1... | collective-permute-start | bytes 55304 | tf_op jit(solution)/shard_map/ppermute | solution.py:578
  6.2 5.2 %collective-permute-start.1 = (f32[1,48,1,96]{3,2,1,0:T(1,128)}, f32[1,48,1,96]{3,2,1,0:T(1,128)S(1)}, u32[]{:S(2)}, u32[]{:S(2)}) collective-permute-start(f32[1,48,1,96]{3,2,1,0:T(1,128)} %inverse_hbm.1), channel_id=1, source_target_pairs={{2,0},{3,1},{0,2},{1,3},{6,4},{7,5},{4,6},{5,7},{10,8},{11,9},{8,1... | collective-permute-start | bytes 55304 | tf_op jit(solution)/shard_map/ppermute | solution.py:578
  9.0 5.5 %copy-start = (bf16[1,1,896,896]{3,2,1,0:T(8,128)(2,1)S(1)}, bf16[1,1,896,896]{3,2,1,0:T(8,128)(2,1)}, u32[]{:S(2)}) copy-start(bf16[1,1,896,896]{3,2,1,0:T(8,128)(2,1)} %param.8) | copy-start | bytes 4816900
  11.4 4.2 %collective-permute-start.6 = (f32[144,256]{1,0:T(8,128)S(1)}, f32[144,256]{1,0:T(8,128)S(1)}, u32[]{:S(2)}, u32[]{:S(2)}) collective-permute-start(f32[144,256]{1,0:T(8,128)S(1)} %get-tuple-element.53.refs_3_), channel_id=1, source_target_pairs={{0,4},{1,5},{2,6},{3,7},{4,0},{5,1},{6,2},{7,3},{8,12},{9,13},{10,... | collective-permute-start | bytes 442376 | tf_op jit(solution)/shard_map/ppermute | solution.py:55
  11.5 6.5 %collective-permute-start.4 = (f32[144,256]{1,0:T(8,128)S(1)}, f32[144,256]{1,0:T(8,128)S(1)}, u32[]{:S(2)}, u32[]{:S(2)}) collective-permute-start(f32[144,256]{1,0:T(8,128)S(1)} %get-tuple-element.51.after_hbm.refs_0_.refs_1_), channel_id=1, source_target_pairs={{0,28},{1,29},{2,30},{3,31},{4,8},{5,9},{6,10},{7,11},{8,4},{9,5},... | collective-permute-start | bytes 442376 | tf_op jit(solution)/shard_map/ppermute | solution.py:55
  14.1 4.7 %collective-permute-start.3 = (f32[112,256]{1,0:T(8,128)S(1)}, f32[112,256]{1,0:T(8,128)S(1)}, u32[]{:S(2)}, u32[]{:S(2)}) collective-permute-start(f32[112,256]{1,0:T(8,128)S(1)} %get-tuple-element.44.refs_0_), channel_id=1, source_target_pairs={{0,1},{1,2},{2,3},{3,7},{4,0},{5,4},{6,5},{7,6},{8,9},{9,10},{10,1... | collective-permute-start | bytes 344072 | tf_op jit(solution)/shard_map/ppermute | solution.py:55
  14.6 4.8 %collective-permute-start.5 = (f32[112,256]{1,0:T(8,128)S(1)}, f32[112,256]{1,0:T(8,128)S(1)}, u32[]{:S(2)}, u32[]{:S(2)}) collective-permute-start(f32[112,256]{1,0:T(8,128)S(1)} %get-tuple-element.52.refs_2_), channel_id=1, source_target_pairs={{0,4},{1,0},{2,1},{3,2},{4,5},{5,6},{6,7},{7,3},{8,12},{9,8},{10,9... | collective-permute-start | bytes 344072 | tf_op jit(solution)/shard_map/ppermute | solution.py:55
  31.6 3.3 %collective-permute-start.7 = (f32[168,128]{1,0:T(8,128)S(1)}, f32[168,128]{1,0:T(8,128)S(1)}, u32[]{:S(2)}, u32[]{:S(2)}) collective-permute-start(f32[168,128]{1,0:T(8,128)S(1)} %get-tuple-element.57.refs_0_), channel_id=1, source_target_pairs={{0,1},{1,2},{2,3},{3,7},{4,0},{5,4},{6,5},{7,6},{8,9},{9,10},{10,1... | collective-permute-start | bytes 258056 | tf_op jit(solution)/shard_map/ppermute | solution.py:55
  32.3 5.0 %collective-permute-start.8 = (f32[168,128]{1,0:T(8,128)S(1)}, f32[168,128]{1,0:T(8,128)S(1)}, u32[]{:S(2)}, u32[]{:S(2)}) collective-permute-start(f32[168,128]{1,0:T(8,128)S(1)} %get-tuple-element.58.refs_1_), channel_id=1, source_target_pairs={{0,28},{1,29},{2,30},{3,31},{4,8},{5,9},{6,10},{7,11},{8,4},{9,5},... | collective-permute-start | bytes 258056 | tf_op jit(solution)/shard_map/ppermute | solution.py:55
  32.7 4.6 %collective-permute-start.9 = (f32[168,128]{1,0:T(8,128)S(1)}, f32[168,128]{1,0:T(8,128)S(1)}, u32[]{:S(2)}, u32[]{:S(2)}) collective-permute-start(f32[168,128]{1,0:T(8,128)S(1)} %get-tuple-element.59.refs_2_), channel_id=1, source_target_pairs={{0,4},{1,0},{2,1},{3,2},{4,5},{5,6},{6,7},{7,3},{8,12},{9,8},{10,9... | collective-permute-start | bytes 258056 | tf_op jit(solution)/shard_map/ppermute | solution.py:55
  32.7 4.6 %collective-permute-start.10 = (f32[168,128]{1,0:T(8,128)S(1)}, f32[168,128]{1,0:T(8,128)S(1)}, u32[]{:S(2)}, u32[]{:S(2)}) collective-permute-start(f32[168,128]{1,0:T(8,128)S(1)} %get-tuple-element.60.refs_3_), channel_id=1, source_target_pairs={{0,4},{1,5},{2,6},{3,7},{4,0},{5,1},{6,2},{7,3},{8,12},{9,13},{10,... | collective-permute-start | bytes 258056 | tf_op jit(solution)/shard_map/ppermute | solution.py:55
  49.6 3.3 %collective-permute-start.11 = (f32[168,128]{1,0:T(8,128)S(1)}, f32[168,128]{1,0:T(8,128)S(1)}, u32[]{:S(2)}, u32[]{:S(2)}) collective-permute-start(f32[168,128]{1,0:T(8,128)S(1)} %get-tuple-element.64.refs_0_), channel_id=1, source_target_pairs={{0,1},{1,2},{2,3},{3,7},{4,0},{5,4},{6,5},{7,6},{8,9},{9,10},{10,1... | collective-permute-start | bytes 258056 | tf_op jit(solution)/shard_map/ppermute | solution.py:55
  50.3 5.0 %collective-permute-start.12 = (f32[168,128]{1,0:T(8,128)S(1)}, f32[168,128]{1,0:T(8,128)S(1)}, u32[]{:S(2)}, u32[]{:S(2)}) collective-permute-start(f32[168,128]{1,0:T(8,128)S(1)} %get-tuple-element.65.refs_1_), channel_id=1, source_target_pairs={{0,28},{1,29},{2,30},{3,31},{4,8},{5,9},{6,10},{7,11},{8,4},{9,5},... | collective-permute-start | bytes 258056 | tf_op jit(solution)/shard_map/ppermute | solution.py:55
  50.7 4.6 %collective-permute-start.13 = (f32[168,128]{1,0:T(8,128)S(1)}, f32[168,128]{1,0:T(8,128)S(1)}, u32[]{:S(2)}, u32[]{:S(2)}) collective-permute-start(f32[168,128]{1,0:T(8,128)S(1)} %get-tuple-element.66.refs_2_), channel_id=1, source_target_pairs={{0,4},{1,0},{2,1},{3,2},{4,5},{5,6},{6,7},{7,3},{8,12},{9,8},{10,9... | collective-permute-start | bytes 258056 | tf_op jit(solution)/shard_map/ppermute | solution.py:55
  50.7 4.6 %collective-permute-start.14 = (f32[168,128]{1,0:T(8,128)S(1)}, f32[168,128]{1,0:T(8,128)S(1)}, u32[]{:S(2)}, u32[]{:S(2)}) collective-permute-start(f32[168,128]{1,0:T(8,128)S(1)} %get-tuple-element.67.refs_3_), channel_id=1, source_target_pairs={{0,4},{1,5},{2,6},{3,7},{4,0},{5,1},{6,2},{7,3},{8,12},{9,13},{10,... | collective-permute-start | bytes 258056 | tf_op jit(solution)/shard_map/ppermute | solution.py:55
  67.6 3.3 %collective-permute-start.15 = (f32[168,128]{1,0:T(8,128)S(1)}, f32[168,128]{1,0:T(8,128)S(1)}, u32[]{:S(2)}, u32[]{:S(2)}) collective-permute-start(f32[168,128]{1,0:T(8,128)S(1)} %get-tuple-element.71.refs_0_), channel_id=1, source_target_pairs={{0,1},{1,2},{2,3},{3,7},{4,0},{5,4},{6,5},{7,6},{8,9},{9,10},{10,1... | collective-permute-start | bytes 258056 | tf_op jit(solution)/shard_map/ppermute | solution.py:55
  68.3 5.0 %collective-permute-start.16 = (f32[168,128]{1,0:T(8,128)S(1)}, f32[168,128]{1,0:T(8,128)S(1)}, u32[]{:S(2)}, u32[]{:S(2)}) collective-permute-start(f32[168,128]{1,0:T(8,128)S(1)} %get-tuple-element.72.refs_1_), channel_id=1, source_target_pairs={{0,28},{1,29},{2,30},{3,31},{4,8},{5,9},{6,10},{7,11},{8,4},{9,5},... | collective-permute-start | bytes 258056 | tf_op jit(solution)/shard_map/ppermute | solution.py:55
  68.6 4.6 %collective-permute-start.17 = (f32[168,128]{1,0:T(8,128)S(1)}, f32[168,128]{1,0:T(8,128)S(1)}, u32[]{:S(2)}, u32[]{:S(2)}) collective-permute-start(f32[168,128]{1,0:T(8,128)S(1)} %get-tuple-element.73.refs_2_), channel_id=1, source_target_pairs={{0,4},{1,0},{2,1},{3,2},{4,5},{5,6},{6,7},{7,3},{8,12},{9,8},{10,9... | collective-permute-start | bytes 258056 | tf_op jit(solution)/shard_map/ppermute | solution.py:55
  68.7 4.6 %collective-permute-start.18 = (f32[168,128]{1,0:T(8,128)S(1)}, f32[168,128]{1,0:T(8,128)S(1)}, u32[]{:S(2)}, u32[]{:S(2)}) collective-permute-start(f32[168,128]{1,0:T(8,128)S(1)} %get-tuple-element.74.refs_3_), channel_id=1, source_target_pairs={{0,4},{1,5},{2,6},{3,7},{4,0},{5,1},{6,2},{7,3},{8,12},{9,13},{10,... | collective-permute-start | bytes 258056 | tf_op jit(solution)/shard_map/ppermute | solution.py:55
  85.5 3.3 %collective-permute-start.19 = (f32[168,128]{1,0:T(8,128)S(1)}, f32[168,128]{1,0:T(8,128)S(1)}, u32[]{:S(2)}, u32[]{:S(2)}) collective-permute-start(f32[168,128]{1,0:T(8,128)S(1)} %get-tuple-element.79.refs_0_), channel_id=1, source_target_pairs={{0,1},{1,2},{2,3},{3,7},{4,0},{5,4},{6,5},{7,6},{8,9},{9,10},{10,1... | collective-permute-start | bytes 258056 | tf_op jit(solution)/shard_map/ppermute | solution.py:55
  86.2 5.0 %collective-permute-start.20 = (f32[168,128]{1,0:T(8,128)S(1)}, f32[168,128]{1,0:T(8,128)S(1)}, u32[]{:S(2)}, u32[]{:S(2)}) collective-permute-start(f32[168,128]{1,0:T(8,128)S(1)} %get-tuple-element.80.refs_1_), channel_id=1, source_target_pairs={{0,28},{1,29},{2,30},{3,31},{4,8},{5,9},{6,10},{7,11},{8,4},{9,5},... | collective-permute-start | bytes 258056 | tf_op jit(solution)/shard_map/ppermute | solution.py:55
  86.6 4.6 %collective-permute-start.21 = (f32[168,128]{1,0:T(8,128)S(1)}, f32[168,128]{1,0:T(8,128)S(1)}, u32[]{:S(2)}, u32[]{:S(2)}) collective-permute-start(f32[168,128]{1,0:T(8,128)S(1)} %get-tuple-element.81.refs_2_), channel_id=1, source_target_pairs={{0,4},{1,0},{2,1},{3,2},{4,5},{5,6},{6,7},{7,3},{8,12},{9,8},{10,9... | collective-permute-start | bytes 258056 | tf_op jit(solution)/shard_map/ppermute | solution.py:55
  86.6 4.6 %collective-permute-start.22 = (f32[168,128]{1,0:T(8,128)S(1)}, f32[168,128]{1,0:T(8,128)S(1)}, u32[]{:S(2)}, u32[]{:S(2)}) collective-permute-start(f32[168,128]{1,0:T(8,128)S(1)} %get-tuple-element.82.refs_3_), channel_id=1, source_target_pairs={{0,4},{1,5},{2,6},{3,7},{4,0},{5,1},{6,2},{7,3},{8,12},{9,13},{10,... | collective-permute-start | bytes 258056 | tf_op jit(solution)/shard_map/ppermute | solution.py:55

commit v5 on v4

--- a/solution.py
+++ b/solution.py
@@ -174,6 +174,25 @@
     return jnp.concatenate([first, second], axis=1)
 
 
+def write_places(out_ref, count):
+    long, short = pack_counts(count)
+    length = out_ref.shape[0]
+    wide = length // count * long
+    source = lax.broadcasted_iota(jnp.int32, (length, wide), 0)
+    target = lax.broadcasted_iota(jnp.int32, (length, wide), 1)
+    source_row, source_mode = lax.div(source, count), lax.rem(source, count)
+    target_row, target_place = lax.div(target, long), lax.rem(target, long)
+    same = source_row == target_row
+    places = [jnp.where(same & (source_mode == target_place), 1.0, 0.0).astype(bf16)]
+    for part in range(long // short):
+        wanted = target_place - part * short
+        inside = (wanted >= 0) & (wanted < short)
+        places.append(
+            jnp.where(same & inside & (source_mode == long + wanted), 1.0, 0.0).astype(bf16)
+        )
+    out_ref[...] = jnp.concatenate(places, axis=1)
+
+
 def write_copies(out_ref, value):
     height = value.shape[0]
     copies = out_ref.shape[0] // height
@@ -207,7 +226,7 @@
 
 def load_kernel(
     load_hbm, modes_hbm, partners_hbm, counts_hbm, matrix_hbm, inverse_hbm,
-    slot_0, slot_1, slot_2, slot_3, live_ref, reorder_ref, matrix_ref, inverse_ref,
+    slot_0, slot_1, slot_2, slot_3, live_ref, reorder_ref, places_ref, matrix_ref, inverse_ref,
     load_ref, modes_ref, partners_ref, counts_ref, sems,
 ):
     copies = [
@@ -252,6 +271,7 @@
         )
         places = lax.broadcasted_iota(jnp.int32, (live_ref.shape[0], padded), 1)
         live_ref[:, slot * padded : (slot + 1) * padded] = jnp.where(places < live, 1.0, 0.0)
+    write_places(places_ref, count)
     for copy in copies[4:]:
         copy.wait()
 
@@ -301,8 +321,8 @@
 
 
 def inverse_kernel(count, base, *refs):
-    face_refs = refs[:3]
-    part_refs, (out_ref, rows_ref) = refs[3:-3], refs[-2:]
+    face_refs, places_ref = refs[:3], refs[3]
+    part_refs, (out_ref, rows_ref) = refs[4:-3], refs[-2:]
     cols = len(part_refs)
     parity, here = row_parity(), lax.axis_index("gy")
     north, south = jnp.minimum(here + 1, cols - 1), jnp.maximum(here - 1, 0)
@@ -323,25 +343,13 @@
             rows_ref[source_col, i * count : (i + 1) * count, :] = part_ref[
                 0, pl.ds(row * count, count), 0, :
             ]
+    ratio = 1 + long // short
     wide = rows * long
-    source = lax.broadcasted_iota(jnp.int32, (length, wide), 0)
-    target = lax.broadcasted_iota(jnp.int32, (length, wide), 1)
-    source_row, source_mode = lax.div(source, count), lax.rem(source, count)
-    target_row, target_place = lax.div(target, long), lax.rem(target, long)
-    same = source_row == target_row
-    places = [jnp.where(same & (source_mode == target_place), 1.0, 0.0).astype(bf16)]
-    for part in range(long // short):
-        wanted = target_place - part * short
-        inside = (wanted >= 0) & (wanted < short)
-        places.append(
-            jnp.where(same & inside & (source_mode == long + wanted), 1.0, 0.0).astype(bf16)
-        )
-    place = jnp.concatenate(places, axis=1)
-    gathered = [[] for _ in places]
+    gathered = [[] for _ in range(ratio)]
     for e in range(cols):
         pieces = jnp.concatenate(split3(rows_ref[e]), axis=0)
-        moved = contract(pieces, place, 1, 0)
-        for part in range(len(places)):
+        moved = contract(pieces, places_ref[...], 1, 0)
+        for part in range(ratio):
             gathered[part].append(moved[:, part * wide : (part + 1) * wide])
     for part, pieces in enumerate(gathered):
         high, middle, low = (
@@ -355,9 +363,12 @@
 
 
 def coefficients(vector, columns_ref, count):
-    terms = jnp.dot(
-        jnp.concatenate(split3(vector), axis=0), columns_ref[...], preferred_element_type=f32
-    )
+    padded = vector.shape[1] // 4
+    terms = jnp.zeros((3 * vector.shape[0], columns_ref.shape[1]), f32)
+    for slot in range(4):
+        place = slice(slot * padded, (slot + 1) * padded)
+        pieces = jnp.concatenate(split3(vector[:, place]), axis=0)
+        terms = terms + jnp.dot(pieces, columns_ref[place, :], preferred_element_type=f32)
     columns = vector.shape[0]
     coeffs = (terms[:columns] + (terms[columns : 2 * columns] + terms[2 * columns :])).T
     return pack_coefficients(coeffs, count)
@@ -554,12 +565,13 @@
 
     raw = shape((slots, slots), bf16)
     wide = pltpu.VMEM((slots, 4 * padded), bf16)
-    *sent, live, reorder, smoother, own_part = call(
+    *sent, live, reorder, places, smoother, own_part = call(
         load_kernel,
         [
             *tall_faces,
             shape((8, 4 * padded), f32),
             shape((len(REORDERED), padded, width), bf16),
+            shape((rows * count, (1 + long // short) * rows * long), bf16),
             raw,
             shape(coarse_inverse.shape, f32),
         ],
@@ -594,9 +606,9 @@
     (inverse,) = call(
         functools.partial(inverse_kernel, count, base),
         [shape(((1 + long // short) * height, len(PRODUCTS) * devices * long), bf16)],
-        (sent[1], arrived[1], arrived[3], *parts, operator),
+        (sent[1], arrived[1], arrived[3], places, *parts, operator),
         (),
-        (3 + cols,),
+        (4 + cols,),
         [pltpu.VMEM((cols, height, rows * count), f32)],
     )
     current, coeffs, mode_columns, extended = call(

time: 104 us -> 104 us (level)
  no operation moved by 1% of the time
where the time goes in v5:
time: 104 us
  blocking collectives  52.4 us (50%)
  waiting for transfers between devices  19.9 us (19%)
  starting transfers between devices  15.9 us (15%)
  Pallas kernels  15 us (14%)
    all_to_all x5, blocking collectives, everywhere(): lax.all_to_all(chunks, ('gy', 'gx'), 0, 0).reshape(devices * long, packed)  52.4 us
    ppermute x20, waiting for transfers between devices, exchange(): lax.ppermute(value, ('gx', 'gy'), pairs)  17.5 us
    pallas_call x16, Pallas kernels, call(): pl.pallas_call(kernel, out_shape=tuple(outs), in_specs=[outside if i in h...  15 us
    ppermute x20, starting transfers between devices, exchange(): lax.ppermute(value, ('gx', 'gy'), pairs)  10.2 us
    ppermute x3, starting transfers between devices, local(): lax.ppermute(coarse_inverse, 'gy', [(column_met(b, step, cols), b) for b...  5.68 us
    ppermute x3, waiting for transfers between devices, local(): lax.ppermute(coarse_inverse, 'gy', [(column_met(b, step, cols), b) for b...  2.35 us
  transfers between devices with their start and end apart: 23, of which 12 were waited for; matrix products, arithmetic and copies ran while one was open for 0% of the time, Pallas kernels for 5%

profile of v5, /device:TPU:0, one launch (start us, length us, event | category | flops | bytes accessed | tf_op | source)
XLA Modules:
  0.0 104.0 jit_solution(1949922992218883001)
XLA Ops:
  0.6 3.1 %collective-permute-start = (f32[1,48,1,96]{3,2,1,0:T(1,128)}, f32[1,48,1,96]{3,2,1,0:T(1,128)S(1)}, u32[]{:S(2)}, u32[]{:S(2)}) collective-permute-start(f32[1,48,1,96]{3,2,1,0:T(1,128)} %inverse_hbm.1), channel_id=1, source_target_pairs={{1,0},{0,1},{3,2},{2,3},{5,4},{4,5},{7,6},{6,7},{9,8},{8,9},{11,10... | collective-permute-start | bytes 55304 | tf_op jit(solution)/shard_map/ppermute | solution.py:590
  3.7 2.5 %collective-permute-start.2 = (f32[1,48,1,96]{3,2,1,0:T(1,128)}, f32[1,48,1,96]{3,2,1,0:T(1,128)S(1)}, u32[]{:S(2)}, u32[]{:S(2)}) collective-permute-start(f32[1,48,1,96]{3,2,1,0:T(1,128)} %inverse_hbm.1), channel_id=1, source_target_pairs={{3,0},{2,1},{1,2},{0,3},{7,4},{6,5},{5,6},{4,7},{11,8},{10,9},{9,1... | collective-permute-start | bytes 55304 | tf_op jit(solution)/shard_map/ppermute | solution.py:590
  6.3 1.6 %shard_map.86 = (f32[112,256]{1,0:T(8,128)S(1)}, f32[144,256]{1,0:T(8,128)S(1)}, f32[112,256]{1,0:T(8,128)S(1)}, f32[144,256]{1,0:T(8,128)S(1)}, f32[8,1024]{1,0...) custom-call(f32[1,1,96,896]{3,2,1,0:T(8,128)} %load_hbm.1, ...), custom_call_target="tpu_custom_call" | custom-call | tf_op jit(solution)/shard_map/pallas_call | solution.py:527
  8.0 1.1 %shard_map.87.refs_6_.matrix_ref = bf16[1024,1024]{1,0:T(8,128)(2,1)S(1)} custom-call(bf16[896,896]{1,0:T(8,128)(2,1)S(1)} %get-tuple-element.49.matrix_ref, bf16[2,256,224]{2,1,0:T(8,128)(2,1)S(1)} %get-tuple-element.50.reorder_ref, f32[8,1024]{1,0:T(8,128)S(1)} %get-tuple-element.51.after_hbm.refs_8_), custom_call_target="tpu_custom_call" | custom-call | tf_op jit(solution)/shard_map/pallas_call | solution.py:527
  9.0 0.9 collective-permute-done.2.refs_5_.refs_7_
  9.9 1.5 %collective-permute-done.1.refs_4_.refs_6_ = f32[1,48,1,96]{3,2,1,0:T(1,128)S(1)} collective-permute-done((f32[1,48,1,96]{3,2,1,0:T(1,128)}, f32[1,48,1,96]{3,2,1,0:T(1,128)S(1)}, u32[]{:S(2)}, u32[]{:S(2)}) %collective-permute-start.1) | collective-permute-done | bytes 18464 | tf_op jit(solution)/shard_map/ppermute | solution.py:590
  11.5 2.5 %collective-permute-start.4 = (f32[144,256]{1,0:T(8,128)S(1)}, f32[144,256]{1,0:T(8,128)S(1)}, u32[]{:S(2)}, u32[]{:S(2)}) collective-permute-start(f32[144,256]{1,0:T(8,128)S(1)} %get-tuple-element.52.after_hbm.refs_0_.refs_1_), channel_id=1, source_target_pairs={{0,28},{1,29},{2,30},{3,31},{4,8},{5,9},{6,10},{7,11},{8,4},{9,5},... | collective-permute-start | bytes 442376 | tf_op jit(solution)/shard_map/ppermute | solution.py:55
  14.6 1.1 %shard_map.89.refs_8_.matrix_ref = bf16[1024,1024]{1,0:T(8,128)(2,1)S(1)} custom-call(bf16[896,896]{1,0:T(8,128)(2,1)S(1)} %bitcast.13, bf16[2,256,224]{2,1,0:T(8,128)(2,1)S(1)} %get-tuple-element.50.reorder_ref, f32[144,256]{1,0:T(8,128)S(1)} %get-tuple-element.52.after_hbm.refs_0_.refs_1_), custom_call_target="tpu_custom_call" | custom-call | tf_op jit(solution)/shard_map/pallas_call | solution.py:527
  15.6 2.4 %collective-permute-done.4.refs_1_.refs_5_ = f32[144,256]{1,0:T(8,128)S(1)} collective-permute-done((f32[144,256]{1,0:T(8,128)S(1)}, f32[144,256]{1,0:T(8,128)S(1)}, u32[]{:S(2)}, u32[]{:S(2)}) %collective-permute-start.4) | collective-permute-done | bytes 147488 | tf_op jit(solution)/shard_map/ppermute | solution.py:55
  18.0 0.7 shard_map.90.refs_9_.inverse_ref
  20.0 10.4 %all_to_all.25 = f32[32,9,1,128]{3,2,1,0:T(1,128)S(1)} all-to-all(f32[32,9,1,128]{3,2,1,0:T(1,128)S(1)} %bitcast.19), channel_id=1, replica_groups=mesh['gx'=8,'gy'=4] {'gy','gx'}, dimensions={0} | all-to-all | bytes 294912 | tf_op jit(solution)/shard_map/all_to_all | solution.py:564
  30.4 1.2 %shard_map.92 = (f32[96,1024]{1,0:T(8,128)S(1)}, f32[168,128]{1,0:T(8,128)S(1)}, f32[168,128]{1,0:T(8,128)S(1)}, f32[168,128]{1,0:T(8,128)S(1)}, f32[168,128]{1,0:T(8,128)S(1)}) custom-call(f32[288,128]{1,0:T(8,128)S(1)} %bitcast.18, bf16[256,1728]{1,0:T(8,128)(2,1)S(1)} %shard_map.90.refs_9_.inverse_ref, ...), custom_call_target="tpu_custom_call" | custom-call | tf_op jit(solution)/shard_map/pallas_call | solution.py:527
  32.7 0.7 collective-permute-start.10
  33.4 1.6 %collective-permute-done.7.refs_4_ = f32[168,128]{1,0:T(8,128)S(1)} collective-permute-done((f32[168,128]{1,0:T(8,128)S(1)}, f32[168,128]{1,0:T(8,128)S(1)}, u32[]{:S(2)}, u32[]{:S(2)}) %collective-permute-start.7) | collective-permute-done | bytes 86048 | tf_op jit(solution)/shard_map/ppermute | solution.py:55
  34.9 2.3 %collective-permute-done.8.refs_5_ = f32[168,128]{1,0:T(8,128)S(1)} collective-permute-done((f32[168,128]{1,0:T(8,128)S(1)}, f32[168,128]{1,0:T(8,128)S(1)}, u32[]{:S(2)}, u32[]{:S(2)}) %collective-permute-start.8) | collective-permute-done | bytes 86048 | tf_op jit(solution)/shard_map/ppermute | solution.py:55
  37.9 10.5 %all_to_all.26 = f32[32,9,1,128]{3,2,1,0:T(1,128)S(1)} all-to-all(f32[32,9,1,128]{3,2,1,0:T(1,128)S(1)} %bitcast.21), channel_id=1, replica_groups=mesh['gx'=8,'gy'=4] {'gy','gx'}, dimensions={0} | all-to-all | bytes 294912 | tf_op jit(solution)/shard_map/all_to_all | solution.py:564
  48.4 1.2 %shard_map.94 = (f32[96,1024]{1,0:T(8,128)S(1)}, f32[168,128]{1,0:T(8,128)S(1)}, f32[168,128]{1,0:T(8,128)S(1)}, f32[168,128]{1,0:T(8,128)S(1)}, f32[168,128]{1,0:T(8,128)S(1)}) custom-call(f32[288,128]{1,0:T(8,128)S(1)} %bitcast.16, bf16[256,1728]{1,0:T(8,128)(2,1)S(1)} %shard_map.90.refs_9_.inverse_ref, ...), custom_call_target="tpu_custom_call" | custom-call | tf_op jit(solution)/shard_map/pallas_call | solution.py:527
  50.6 0.7 collective-permute-start.14
  51.4 1.6 %collective-permute-done.11.refs_4_ = f32[168,128]{1,0:T(8,128)S(1)} collective-permute-done((f32[168,128]{1,0:T(8,128)S(1)}, f32[168,128]{1,0:T(8,128)S(1)}, u32[]{:S(2)}, u32[]{:S(2)}) %collective-permute-start.11) | collective-permute-done | bytes 86048 | tf_op jit(solution)/shard_map/ppermute | solution.py:55
  52.9 2.3 %collective-permute-done.12.refs_5_ = f32[168,128]{1,0:T(8,128)S(1)} collective-permute-done((f32[168,128]{1,0:T(8,128)S(1)}, f32[168,128]{1,0:T(8,128)S(1)}, u32[]{:S(2)}, u32[]{:S(2)}) %collective-permute-start.12) | collective-permute-done | bytes 86048 | tf_op jit(solution)/shard_map/ppermute | solution.py:55
  55.8 10.5 %all_to_all.27 = f32[32,9,1,128]{3,2,1,0:T(1,128)S(1)} all-to-all(f32[32,9,1,128]{3,2,1,0:T(1,128)S(1)} %bitcast.22), channel_id=1, replica_groups=mesh['gx'=8,'gy'=4] {'gy','gx'}, dimensions={0} | all-to-all | bytes 294912 | tf_op jit(solution)/shard_map/all_to_all | solution.py:564
  66.3 1.2 %shard_map.96 = (f32[96,1024]{1,0:T(8,128)S(1)}, f32[168,128]{1,0:T(8,128)S(1)}, f32[168,128]{1,0:T(8,128)S(1)}, f32[168,128]{1,0:T(8,128)S(1)}, f32[168,128]{1,0:T(8,128)S(1)}) custom-call(f32[288,128]{1,0:T(8,128)S(1)} %bitcast.14, bf16[256,1728]{1,0:T(8,128)(2,1)S(1)} %shard_map.90.refs_9_.inverse_ref, ...), custom_call_target="tpu_custom_call" | custom-call | tf_op jit(solution)/shard_map/pallas_call | solution.py:527
  68.6 0.7 collective-permute-start.18
  69.3 1.6 %collective-permute-done.15.refs_4_ = f32[168,128]{1,0:T(8,128)S(1)} collective-permute-done((f32[168,128]{1,0:T(8,128)S(1)}, f32[168,128]{1,0:T(8,128)S(1)}, u32[]{:S(2)}, u32[]{:S(2)}) %collective-permute-start.15) | collective-permute-done | bytes 86048 | tf_op jit(solution)/shard_map/ppermute | solution.py:55
  70.9 2.3 %collective-permute-done.16.refs_5_ = f32[168,128]{1,0:T(8,128)S(1)} collective-permute-done((f32[168,128]{1,0:T(8,128)S(1)}, f32[168,128]{1,0:T(8,128)S(1)}, u32[]{:S(2)}, u32[]{:S(2)}) %collective-permute-start.16) | collective-permute-done | bytes 86048 | tf_op jit(solution)/shard_map/ppermute | solution.py:55
  73.8 10.5 %all_to_all.28 = f32[32,9,1,128]{3,2,1,0:T(1,128)S(1)} all-to-all(f32[32,9,1,128]{3,2,1,0:T(1,128)S(1)} %bitcast.23), channel_id=1, replica_groups=mesh['gx'=8,'gy'=4] {'gy','gx'}, dimensions={0} | all-to-all | bytes 294912 | tf_op jit(solution)/shard_map/all_to_all | solution.py:564
  84.3 1.2 %shard_map.98 = (f32[96,1024]{1,0:T(8,128)S(1)}, f32[168,128]{1,0:T(8,128)S(1)}, f32[168,128]{1,0:T(8,128)S(1)}, f32[168,128]{1,0:T(8,128)S(1)}, f32[168,128]{1,0:T(8,128)S(1)}) custom-call(f32[288,128]{1,0:T(8,128)S(1)} %bitcast.15, bf16[256,1728]{1,0:T(8,128)(2,1)S(1)} %shard_map.90.refs_9_.inverse_ref, ...), custom_call_target="tpu_custom_call" | custom-call | tf_op jit(solution)/shard_map/pallas_call | solution.py:527
  86.6 0.7 collective-permute-start.22
  87.3 1.0 %shard_map.99.refs_10_ = f32[96,896]{1,0:T(8,128)} custom-call(f32[96,1024]{1,0:T(8,128)S(1)} %get-tuple-element.80.vector_ref, bf16[2,256,224]{2,1,0:T(8,128)(2,1)S(1)} %get-tuple-element.50.reorder_ref), custom_call_target="tpu_custom_call" | custom-call | tf_op jit(solution)/shard_map/pallas_call | solution.py:527
  88.9 2.3 %collective-permute-done.20.refs_5_ = f32[168,128]{1,0:T(8,128)S(1)} collective-permute-done((f32[168,128]{1,0:T(8,128)S(1)}, f32[168,128]{1,0:T(8,128)S(1)}, u32[]{:S(2)}, u32[]{:S(2)}) %collective-permute-start.20) | collective-permute-done | bytes 86048 | tf_op jit(solution)/shard_map/ppermute | solution.py:55
  91.8 10.5 %all_to_all.29 = f32[32,9,1,128]{3,2,1,0:T(1,128)S(1)} all-to-all(f32[32,9,1,128]{3,2,1,0:T(1,128)S(1)} %bitcast.20), channel_id=1, replica_groups=mesh['gx'=8,'gy'=4] {'gy','gx'}, dimensions={0} | all-to-all | bytes 294912 | tf_op jit(solution)/shard_map/all_to_all | solution.py:564
  102.3 1.7 %shard_map.101 = f32[96,896]{1,0:T(8,128)} custom-call(f32[288,128]{1,0:T(8,128)S(1)} %bitcast.17, bf16[256,1728]{1,0:T(8,128)(2,1)S(1)} %shard_map.90.refs_9_.inverse_ref, bf16[192,1024]{1,0:T(8,128)(2,1)S(1)} %get-tuple-element.57.extended_ref, f32[96,1024]{1,0:T(8,128)S(1)} %get-tuple-element.86.vector_ref, f32[96,1024]{1,0:T(8,128)S(1)} %get-tuple-element.87.old_ref, ...), custom_call_target="tpu_custom_call" | custom-call | tf_op jit(solution)/shard_map/pallas_call | solution.py:527
  (37 shorter events, 9.1 us)
Async XLA Ops:
  0.6 8.4 %collective-permute-start = (f32[1,48,1,96]{3,2,1,0:T(1,128)}, f32[1,48,1,96]{3,2,1,0:T(1,128)S(1)}, u32[]{:S(2)}, u32[]{:S(2)}) collective-permute-start(f32[1,48,1,96]{3,2,1,0:T(1,128)} %inverse_hbm.1), channel_id=1, source_target_pairs={{1,0},{0,1},{3,2},{2,3},{5,4},{4,5},{7,6},{6,7},{9,8},{8,9},{11,10... | collective-permute-start | bytes 55304 | tf_op jit(solution)/shard_map/ppermute | solution.py:590
  3.7 6.2 %collective-permute-start.2 = (f32[1,48,1,96]{3,2,1,0:T(1,128)}, f32[1,48,1,96]{3,2,1,0:T(1,128)S(1)}, u32[]{:S(2)}, u32[]{:S(2)}) collective-permute-start(f32[1,48,1,96]{3,2,1,0:T(1,128)} %inverse_hbm.1), channel_id=1, source_target_pairs={{3,0},{2,1},{1,2},{0,3},{7,4},{6,5},{5,6},{4,7},{11,8},{10,9},{9,1... | collective-permute-start | bytes 55304 | tf_op jit(solution)/shard_map/ppermute | solution.py:590
  6.2 5.2 %collective-permute-start.1 = (f32[1,48,1,96]{3,2,1,0:T(1,128)}, f32[1,48,1,96]{3,2,1,0:T(1,128)S(1)}, u32[]{:S(2)}, u32[]{:S(2)}) collective-permute-start(f32[1,48,1,96]{3,2,1,0:T(1,128)} %inverse_hbm.1), channel_id=1, source_target_pairs={{2,0},{3,1},{0,2},{1,3},{6,4},{7,5},{4,6},{5,7},{10,8},{11,9},{8,1... | collective-permute-start | bytes 55304 | tf_op jit(solution)/shard_map/ppermute | solution.py:590
  9.0 5.5 %copy-start = (bf16[1,1,896,896]{3,2,1,0:T(8,128)(2,1)S(1)}, bf16[1,1,896,896]{3,2,1,0:T(8,128)(2,1)}, u32[]{:S(2)}) copy-start(bf16[1,1,896,896]{3,2,1,0:T(8,128)(2,1)} %param.8) | copy-start | bytes 4816900
  11.4 4.2 %collective-permute-start.6 = (f32[144,256]{1,0:T(8,128)S(1)}, f32[144,256]{1,0:T(8,128)S(1)}, u32[]{:S(2)}, u32[]{:S(2)}) collective-permute-start(f32[144,256]{1,0:T(8,128)S(1)} %get-tuple-element.54.refs_3_), channel_id=1, source_target_pairs={{0,4},{1,5},{2,6},{3,7},{4,0},{5,1},{6,2},{7,3},{8,12},{9,13},{10,... | collective-permute-start | bytes 442376 | tf_op jit(solution)/shard_map/ppermute | solution.py:55
  11.5 6.5 %collective-permute-start.4 = (f32[144,256]{1,0:T(8,128)S(1)}, f32[144,256]{1,0:T(8,128)S(1)}, u32[]{:S(2)}, u32[]{:S(2)}) collective-permute-start(f32[144,256]{1,0:T(8,128)S(1)} %get-tuple-element.52.after_hbm.refs_0_.refs_1_), channel_id=1, source_target_pairs={{0,28},{1,29},{2,30},{3,31},{4,8},{5,9},{6,10},{7,11},{8,4},{9,5},... | collective-permute-start | bytes 442376 | tf_op jit(solution)/shard_map/ppermute | solution.py:55
  14.1 4.7 %collective-permute-start.3 = (f32[112,256]{1,0:T(8,128)S(1)}, f32[112,256]{1,0:T(8,128)S(1)}, u32[]{:S(2)}, u32[]{:S(2)}) collective-permute-start(f32[112,256]{1,0:T(8,128)S(1)} %get-tuple-element.45.refs_0_), channel_id=1, source_target_pairs={{0,1},{1,2},{2,3},{3,7},{4,0},{5,4},{6,5},{7,6},{8,9},{9,10},{10,1... | collective-permute-start | bytes 344072 | tf_op jit(solution)/shard_map/ppermute | solution.py:55
  14.6 4.8 %collective-permute-start.5 = (f32[112,256]{1,0:T(8,128)S(1)}, f32[112,256]{1,0:T(8,128)S(1)}, u32[]{:S(2)}, u32[]{:S(2)}) collective-permute-start(f32[112,256]{1,0:T(8,128)S(1)} %get-tuple-element.53.refs_2_), channel_id=1, source_target_pairs={{0,4},{1,0},{2,1},{3,2},{4,5},{5,6},{6,7},{7,3},{8,12},{9,8},{10,9... | collective-permute-start | bytes 344072 | tf_op jit(solution)/shard_map/ppermute | solution.py:55
  31.6 3.3 %collective-permute-start.7 = (f32[168,128]{1,0:T(8,128)S(1)}, f32[168,128]{1,0:T(8,128)S(1)}, u32[]{:S(2)}, u32[]{:S(2)}) collective-permute-start(f32[168,128]{1,0:T(8,128)S(1)} %get-tuple-element.59.refs_0_), channel_id=1, source_target_pairs={{0,1},{1,2},{2,3},{3,7},{4,0},{5,4},{6,5},{7,6},{8,9},{9,10},{10,1... | collective-permute-start | bytes 258056 | tf_op jit(solution)/shard_map/ppermute | solution.py:55
  32.3 5.0 %collective-permute-start.8 = (f32[168,128]{1,0:T(8,128)S(1)}, f32[168,128]{1,0:T(8,128)S(1)}, u32[]{:S(2)}, u32[]{:S(2)}) collective-permute-start(f32[168,128]{1,0:T(8,128)S(1)} %get-tuple-element.60.refs_1_), channel_id=1, source_target_pairs={{0,28},{1,29},{2,30},{3,31},{4,8},{5,9},{6,10},{7,11},{8,4},{9,5},... | collective-permute-start | bytes 258056 | tf_op jit(solution)/shard_map/ppermute | solution.py:55
  32.7 4.6 %collective-permute-start.9 = (f32[168,128]{1,0:T(8,128)S(1)}, f32[168,128]{1,0:T(8,128)S(1)}, u32[]{:S(2)}, u32[]{:S(2)}) collective-permute-start(f32[168,128]{1,0:T(8,128)S(1)} %get-tuple-element.61.refs_2_), channel_id=1, source_target_pairs={{0,4},{1,0},{2,1},{3,2},{4,5},{5,6},{6,7},{7,3},{8,12},{9,8},{10,9... | collective-permute-start | bytes 258056 | tf_op jit(solution)/shard_map/ppermute | solution.py:55
  32.7 4.6 %collective-permute-start.10 = (f32[168,128]{1,0:T(8,128)S(1)}, f32[168,128]{1,0:T(8,128)S(1)}, u32[]{:S(2)}, u32[]{:S(2)}) collective-permute-start(f32[168,128]{1,0:T(8,128)S(1)} %get-tuple-element.62.refs_3_), channel_id=1, source_target_pairs={{0,4},{1,5},{2,6},{3,7},{4,0},{5,1},{6,2},{7,3},{8,12},{9,13},{10,... | collective-permute-start | bytes 258056 | tf_op jit(solution)/shard_map/ppermute | solution.py:55
  49.6 3.3 %collective-permute-start.11 = (f32[168,128]{1,0:T(8,128)S(1)}, f32[168,128]{1,0:T(8,128)S(1)}, u32[]{:S(2)}, u32[]{:S(2)}) collective-permute-start(f32[168,128]{1,0:T(8,128)S(1)} %get-tuple-element.66.refs_0_), channel_id=1, source_target_pairs={{0,1},{1,2},{2,3},{3,7},{4,0},{5,4},{6,5},{7,6},{8,9},{9,10},{10,1... | collective-permute-start | bytes 258056 | tf_op jit(solution)/shard_map/ppermute | solution.py:55
  50.3 5.0 %collective-permute-start.12 = (f32[168,128]{1,0:T(8,128)S(1)}, f32[168,128]{1,0:T(8,128)S(1)}, u32[]{:S(2)}, u32[]{:S(2)}) collective-permute-start(f32[168,128]{1,0:T(8,128)S(1)} %get-tuple-element.67.refs_1_), channel_id=1, source_target_pairs={{0,28},{1,29},{2,30},{3,31},{4,8},{5,9},{6,10},{7,11},{8,4},{9,5},... | collective-permute-start | bytes 258056 | tf_op jit(solution)/shard_map/ppermute | solution.py:55
  50.6 4.6 %collective-permute-start.13 = (f32[168,128]{1,0:T(8,128)S(1)}, f32[168,128]{1,0:T(8,128)S(1)}, u32[]{:S(2)}, u32[]{:S(2)}) collective-permute-start(f32[168,128]{1,0:T(8,128)S(1)} %get-tuple-element.68.refs_2_), channel_id=1, source_target_pairs={{0,4},{1,0},{2,1},{3,2},{4,5},{5,6},{6,7},{7,3},{8,12},{9,8},{10,9... | collective-permute-start | bytes 258056 | tf_op jit(solution)/shard_map/ppermute | solution.py:55
  50.6 4.6 %collective-permute-start.14 = (f32[168,128]{1,0:T(8,128)S(1)}, f32[168,128]{1,0:T(8,128)S(1)}, u32[]{:S(2)}, u32[]{:S(2)}) collective-permute-start(f32[168,128]{1,0:T(8,128)S(1)} %get-tuple-element.69.refs_3_), channel_id=1, source_target_pairs={{0,4},{1,5},{2,6},{3,7},{4,0},{5,1},{6,2},{7,3},{8,12},{9,13},{10,... | collective-permute-start | bytes 258056 | tf_op jit(solution)/shard_map/ppermute | solution.py:55
  67.5 3.3 %collective-permute-start.15 = (f32[168,128]{1,0:T(8,128)S(1)}, f32[168,128]{1,0:T(8,128)S(1)}, u32[]{:S(2)}, u32[]{:S(2)}) collective-permute-start(f32[168,128]{1,0:T(8,128)S(1)} %get-tuple-element.73.refs_0_), channel_id=1, source_target_pairs={{0,1},{1,2},{2,3},{3,7},{4,0},{5,4},{6,5},{7,6},{8,9},{9,10},{10,1... | collective-permute-start | bytes 258056 | tf_op jit(solution)/shard_map/ppermute | solution.py:55
  68.2 5.0 %collective-permute-start.16 = (f32[168,128]{1,0:T(8,128)S(1)}, f32[168,128]{1,0:T(8,128)S(1)}, u32[]{:S(2)}, u32[]{:S(2)}) collective-permute-start(f32[168,128]{1,0:T(8,128)S(1)} %get-tuple-element.74.refs_1_), channel_id=1, source_target_pairs={{0,28},{1,29},{2,30},{3,31},{4,8},{5,9},{6,10},{7,11},{8,4},{9,5},... | collective-permute-start | bytes 258056 | tf_op jit(solution)/shard_map/ppermute | solution.py:55
  68.6 4.6 %collective-permute-start.17 = (f32[168,128]{1,0:T(8,128)S(1)}, f32[168,128]{1,0:T(8,128)S(1)}, u32[]{:S(2)}, u32[]{:S(2)}) collective-permute-start(f32[168,128]{1,0:T(8,128)S(1)} %get-tuple-element.75.refs_2_), channel_id=1, source_target_pairs={{0,4},{1,0},{2,1},{3,2},{4,5},{5,6},{6,7},{7,3},{8,12},{9,8},{10,9... | collective-permute-start | bytes 258056 | tf_op jit(solution)/shard_map/ppermute | solution.py:55
  68.6 4.6 %collective-permute-start.18 = (f32[168,128]{1,0:T(8,128)S(1)}, f32[168,128]{1,0:T(8,128)S(1)}, u32[]{:S(2)}, u32[]{:S(2)}) collective-permute-start(f32[168,128]{1,0:T(8,128)S(1)} %get-tuple-element.76.refs_3_), channel_id=1, source_target_pairs={{0,4},{1,5},{2,6},{3,7},{4,0},{5,1},{6,2},{7,3},{8,12},{9,13},{10,... | collective-permute-start | bytes 258056 | tf_op jit(solution)/shard_map/ppermute | solution.py:55
  85.5 3.3 %collective-permute-start.19 = (f32[168,128]{1,0:T(8,128)S(1)}, f32[168,128]{1,0:T(8,128)S(1)}, u32[]{:S(2)}, u32[]{:S(2)}) collective-permute-start(f32[168,128]{1,0:T(8,128)S(1)} %get-tuple-element.81.refs_0_), channel_id=1, source_target_pairs={{0,1},{1,2},{2,3},{3,7},{4,0},{5,4},{6,5},{7,6},{8,9},{9,10},{10,1... | collective-permute-start | bytes 258056 | tf_op jit(solution)/shard_map/ppermute | solution.py:55
  86.2 5.0 %collective-permute-start.20 = (f32[168,128]{1,0:T(8,128)S(1)}, f32[168,128]{1,0:T(8,128)S(1)}, u32[]{:S(2)}, u32[]{:S(2)}) collective-permute-start(f32[168,128]{1,0:T(8,128)S(1)} %get-tuple-element.82.refs_1_), channel_id=1, source_target_pairs={{0,28},{1,29},{2,30},{3,31},{4,8},{5,9},{6,10},{7,11},{8,4},{9,5},... | collective-permute-start | bytes 258056 | tf_op jit(solution)/shard_map/ppermute | solution.py:55
  86.6 4.6 %collective-permute-start.21 = (f32[168,128]{1,0:T(8,128)S(1)}, f32[168,128]{1,0:T(8,128)S(1)}, u32[]{:S(2)}, u32[]{:S(2)}) collective-permute-start(f32[168,128]{1,0:T(8,128)S(1)} %get-tuple-element.83.refs_2_), channel_id=1, source_target_pairs={{0,4},{1,0},{2,1},{3,2},{4,5},{5,6},{6,7},{7,3},{8,12},{9,8},{10,9... | collective-permute-start | bytes 258056 | tf_op jit(solution)/shard_map/ppermute | solution.py:55
  86.6 4.6 %collective-permute-start.22 = (f32[168,128]{1,0:T(8,128)S(1)}, f32[168,128]{1,0:T(8,128)S(1)}, u32[]{:S(2)}, u32[]{:S(2)}) collective-permute-start(f32[168,128]{1,0:T(8,128)S(1)} %get-tuple-element.84.refs_3_), channel_id=1, source_target_pairs={{0,4},{1,5},{2,6},{3,7},{4,0},{5,1},{6,2},{7,3},{8,12},{9,13},{10,... | collective-permute-start | bytes 258056 | tf_op jit(solution)/shard_map/ppermute | solution.py:55
